TPU v7x, 256 devices: a whole 4x4x8 slice. The times are simulated.
256 devices in a mesh: ctx: 64 (over z, x, core), head: 4 (over y).
Axes of the slice: x: 4, y: 4, z: 8, core: 2. Of those that a mesh axis runs over, the one named last changes fastest.
Arguments:
- queries: bfloat16 [16384, 4096], P('ctx', 'head'), may hold values from -6 to 6
- keys: bfloat16 [16384, 4096], P('ctx', 'head'), may hold values from -6 to 6
- values: bfloat16 [16384, 4096], P('ctx', 'head'), may hold values from -8 to 8
- out_grad: bfloat16 [16384, 4096], P('ctx', 'head'), may hold values from -8 to 8
- feature_weights: bfloat16 [128, 2, 32, 128], P('ctx', None, None, 'head'), may hold values from -0.5 to 0.5
Outputs:
- attended: bfloat16 [16384, 4096], P('ctx', 'head')
- query_grad: bfloat16 [16384, 4096], P('ctx', 'head')
- key_grad: bfloat16 [16384, 4096], P('ctx', 'head')
- value_grad: bfloat16 [16384, 4096], P('ctx', 'head')
- map_grad: float32 [128, 2, 32, 128], P('ctx', None, None, 'head')
All inputs are finite; a program needn't handle non-finite values.
Results may differ from a plain program's by a relative error of at most 0.015.
Values may be sent and summed in bfloat16 or wider, within the bound.
No kernel may reach another device: no remote copies, remote signals or barrier semaphores. Data moves between devices by JAX's collectives and lax.ppermute only.
A program may use at most 192 MiB of HBM per device.

v0:
```python
import jax
import jax.numpy as jnp
from jax import lax
from jax.sharding import PartitionSpec as P

HEAD_DIM = 128


PRECISE = lax.Precision.HIGHEST


def prefix(value, axis, join, neutral, backward):
    count, mine = (lax.axis_size(axis), lax.axis_index(axis))
    pieces = jax.tree.map(lambda part: lax.all_gather(part, axis), value)
    if backward:
        pieces = jax.tree.map(lambda part: part[::-1], pieces)
        mine = count - 1 - mine
    subtotal = jax.tree.map(
        lambda part, zero: jnp.full_like(part, 0) + jnp.asarray(zero, part.dtype), value, neutral
    )

    def lap(position, subtotal):
        longer = join(subtotal, jax.tree.map(lambda part: part[position], pieces))
        return jax.tree.map(lambda new, old: jnp.where(position < mine, new, old), longer, subtotal)

    return lax.fori_loop(0, count - 1, lap, subtotal)


def elu_slope(pre_act):
    return jnp.where(pre_act > 0, 1.0, jnp.exp(jnp.minimum(pre_act, 0.0)))


def add_pairs(earlier, latter):
    return (earlier[0] + latter[0], earlier[1] + latter[1])


def body(queries, keys, values, out_grad, feature_weights):
    token_count = queries.shape[0]
    heads_dev = queries.shape[1] // HEAD_DIM
    head_shape = (token_count, heads_dev, HEAD_DIM)
    flat_width = heads_dev * HEAD_DIM
    query_rows = queries.reshape(head_shape)
    key_rows = keys.reshape(head_shape)
    value_rows = values.reshape(head_shape)
    cotangent = out_grad.reshape(head_shape)
    own_maps = lax.all_to_all(feature_weights, "head", split_axis=2, concat_axis=3, tiled=True)
    full_maps = lax.all_gather(own_maps, "ctx", axis=0, tiled=True)
    map_q = full_maps[:, 0]
    map_k = full_maps[:, 1]
    pre_q = jnp.einsum("tha,ahc->thc", query_rows, map_q, preferred_element_type=jnp.float32)
    pre_k = jnp.einsum("tha,ahc->thc", key_rows, map_k, preferred_element_type=jnp.float32)
    feat_q = (1.0 + jax.nn.elu(pre_q)).astype(jnp.bfloat16)
    feat_k = (1.0 + jax.nn.elu(pre_k)).astype(jnp.bfloat16)
    fq_wide = feat_q.astype(jnp.float32)
    fk_wide = feat_k.astype(jnp.float32)
    local_state = jnp.einsum("thc,the->hce", feat_k, value_rows, preferred_element_type=jnp.float32)
    local_norm = jnp.sum(fk_wide, axis=0)
    row_ids = lax.broadcasted_iota(jnp.int32, (token_count, token_count), 0)
    col_ids = lax.broadcasted_iota(jnp.int32, (token_count, token_count), 1)
    causal = row_ids >= col_ids
    scores = jnp.einsum("thc,jhc->htj", feat_q, feat_k, preferred_element_type=jnp.float32)
    scores = jnp.where(causal[None], scores, 0.0)
    weights = scores.astype(jnp.bfloat16)
    within = jnp.einsum("htj,jhe->the", weights, value_rows, preferred_element_type=jnp.float32)
    within_norm = jnp.sum(scores, axis=2).T
    empty = (jnp.zeros_like(local_state), jnp.zeros_like(local_norm))
    prior, prior_norm = prefix((local_state, local_norm), "ctx", add_pairs, empty, False)
    numer = jnp.einsum("thc,hce->the", fq_wide, prior, precision=PRECISE) + within
    denom = jnp.einsum("thc,hc->th", fq_wide, prior_norm, precision=PRECISE) + within_norm
    attended_wide = numer / denom[:, :, None]
    grad = cotangent.astype(jnp.float32) / denom[:, :, None]
    grad_half = grad.astype(jnp.bfloat16)
    slope_den = -jnp.sum(grad * attended_wide, axis=2)
    local_adjoint = jnp.einsum("thc,the->hce", fq_wide, grad, precision=PRECISE)
    local_adjoint_norm = jnp.einsum("th,thc->hc", slope_den, fq_wide, precision=PRECISE)
    empty_adjoint = (jnp.zeros_like(local_adjoint), jnp.zeros_like(local_adjoint_norm))
    after, after_norm = prefix(
        (local_adjoint, local_adjoint_norm), "ctx", add_pairs, empty_adjoint, True
    )
    dscore = (
        jnp.einsum("the,jhe->htj", grad_half, value_rows, preferred_element_type=jnp.float32)
        + slope_den.T[:, :, None]
    )
    dscore = jnp.where(causal[None], dscore, 0.0).astype(jnp.bfloat16)
    value_wide = value_rows.astype(jnp.float32)
    d_feat_q = jnp.einsum("hce,the->thc", prior, grad, precision=PRECISE)
    d_feat_q = d_feat_q + slope_den[:, :, None] * prior_norm[None]
    d_feat_q = d_feat_q + jnp.einsum(
        "htj,jhc->thc", dscore, feat_k, preferred_element_type=jnp.float32
    )
    d_feat_k = jnp.einsum("hce,jhe->jhc", after, value_wide, precision=PRECISE) + after_norm[None]
    d_feat_k = d_feat_k + jnp.einsum(
        "htj,thc->jhc", dscore, feat_q, preferred_element_type=jnp.float32
    )
    d_value = jnp.einsum("htj,the->jhe", weights, grad_half, preferred_element_type=jnp.float32)
    d_value = d_value + jnp.einsum("hce,jhc->jhe", after, fk_wide, precision=PRECISE)
    dpre_q = (d_feat_q * elu_slope(pre_q)).astype(jnp.bfloat16)
    dpre_k = (d_feat_k * elu_slope(pre_k)).astype(jnp.bfloat16)
    query_back = jnp.einsum(
        "thc,ahc->tha", dpre_q, map_q, preferred_element_type=jnp.float32
    ).astype(jnp.bfloat16)
    key_back = jnp.einsum("thc,ahc->tha", dpre_k, map_k, preferred_element_type=jnp.float32).astype(
        jnp.bfloat16
    )
    from_query = jnp.einsum("tha,thc->ahc", query_rows, dpre_q, preferred_element_type=jnp.float32)
    from_key = jnp.einsum("tha,thc->ahc", key_rows, dpre_k, preferred_element_type=jnp.float32)
    summed_grad = lax.psum_scatter(
        jnp.stack((from_query, from_key), axis=1), "ctx", scatter_dimension=0, tiled=True
    )
    summed_grad = summed_grad / (token_count * lax.axis_size("ctx"))
    map_grad = lax.all_to_all(summed_grad, "head", split_axis=3, concat_axis=2, tiled=True)
    flat_shape = (token_count, flat_width)
    return (
        attended_wide.astype(jnp.bfloat16).reshape(flat_shape),
        query_back.reshape(flat_shape),
        key_back.reshape(flat_shape),
        d_value.astype(jnp.bfloat16).reshape(flat_shape),
        map_grad,
    )


def solution(mesh):
    placed = (
        P("ctx", "head"),
        P("ctx", "head"),
        P("ctx", "head"),
        P("ctx", "head"),
        P("ctx", None, None, "head"),
    )
    return jax.shard_map(
        body,
        mesh=mesh,
        in_specs=placed,
        out_specs=(
            P("ctx", "head"),
            P("ctx", "head"),
            P("ctx", "head"),
            P("ctx", "head"),
            P("ctx", None, None, "head"),
        ),
        check_vma=False,
    )
```

profile of v0, /device:TPU:1, one launch (start us, length us, event | category | flops | bytes accessed | tf_op | source)
XLA Modules:
  0.0 736.8 jit_solution(5543810707687383963)
XLA Ops:
  8.2 9.0 %all_to_all.36 = bf16[4,2,512]{2,1,0:T(2,128)(2,1)S(1)} all-to-all(bf16[4,2,512]{2,1,0:T(2,128)(2,1)S(1)} %reshape.64), channel_id=1, replica_groups=mesh['ctx'=64,'head'=4] {'head'}, dimensions={0} | all-to-all | bytes 16384 | tf_op jit(solution)/shard_map/all_to_all | solution.py:46
  17.4 55.2 %all_gather.27 = bf16[128,2,8,128]{3,2,1,0:T(8,128)(2,1)S(1)} all-gather(bf16[2,2,8,128]{3,2,1,0:T(8,128)(2,1)S(1)} %all_to_all.29), channel_id=1, replica_groups=mesh['ctx'=64,'head'=4] {'ctx'}, dimensions={0}, use_global_device_ids=true | all-gather | bytes 532480 | tf_op jit(solution)/shard_map/all_gather | solution.py:47
  72.9 1.6 convert_reduce_fusion
  77.1 46.4 %all-gather.1 = f32[512,128]{1,0:T(8,128)} all-gather(f32[8,128]{1,0:T(8,128)S(1)} %get-tuple-element.305), channel_id=3, replica_groups=mesh['ctx'=64,'head'=4] {'ctx'}, dimensions={0}, use_global_device_ids=true | all-gather | bytes 266240 | tf_op jit(solution)/shard_map/all_gather | solution.py:14
  123.6 1.5 fusion.16
  125.1 1.5 select_reduce_fusion
  126.6 87.3 %all-gather.7.cloned.1.call-done = f32[512,128,128]{2,1,0:T(8,128)} async-done(((f32[8,128,128]{2,1,0:T(8,128)}), f32[512,128,128]{2,1,0:T(8,128)}) %all-gather.7.cloned.1.call-update) | async-done | bytes 33554448 | tf_op jit(solution)/shard_map/all_gather | solution.py:14
  213.9 121.9 %while.32 = (s32[]{:T(128)}, f32[8,128,128]{2,1,0:T(8,128)S(1)}, f32[8,128]{1,0:T(8,128)S(1)}, s32[]{:T(128)}, f32[64,8,128,128]{3,2,1,0:T(8,128)}, /*index=5*/f32[64,8,128]{2,1,0:T(8,128)}, s32[]{:T(128)}, s32[]{:T(128)}) while((s32[]{:T(128)}, f32[8,128,128]{2,1,0:T(8,128)S(1)}, f32[8,128]{1,0:T(8,128)S(1)}, s32[]{:T(128)}, ...), condition=%wide.region_2.3_spmd.clone, body=%wide.region_1.2_spmd.clone.sunk | while | flops 396292 | bytes 1585275 | solution.py:26
  336.1 1.5 fusion.45
  337.7 1.7 convolution_bitcast_fusion.4
  339.4 1.5 multiply_reduce_fusion
  341.4 42.6 %all-gather.3 = f32[512,128]{1,0:T(8,128)S(1)} all-gather(f32[8,128]{1,0:T(8,128)S(1)} %bitcast.207), channel_id=5, replica_groups=mesh['ctx'=64,'head'=4] {'ctx'}, dimensions={0}, use_global_device_ids=true | all-gather | bytes 266240 | tf_op jit(solution)/shard_map/all_gather | solution.py:14
  384.1 2.5 fusion.7
  390.1 87.0 %all-gather.9.cloned.1.call-done = f32[512,128,128]{2,1,0:T(8,128)} async-done(((f32[8,128,128]{2,1,0:T(8,128)}), f32[512,128,128]{2,1,0:T(8,128)}) %all-gather.9.cloned.1.call-update) | async-done | bytes 33554448 | tf_op jit(solution)/shard_map/all_gather | solution.py:14
  477.1 23.0 %rev.6 = f32[64,8,128,128]{3,2,1,0:T(8,128)} reverse(f32[64,8,128,128]{3,2,1,0:T(8,128)} %bitcast.189), dimensions={0} | reverse | bytes 67108864 | tf_op jit(solution)/shard_map/rev | solution.py:16
  500.1 80.2 %while.33 = (s32[]{:T(128)}, f32[8,128,128]{2,1,0:T(8,128)S(1)}, f32[8,128]{1,0:T(8,128)S(1)}, s32[]{:T(128)}, f32[64,8,128,128]{3,2,1,0:T(8,128)}, /*index=5*/f32[64,8,128]{2,1,0:T(8,128)S(1)}, s32[]{:T(128)}, s32[]{:T(128)}) while((s32[]{:T(128)}, f32[8,128,128]{2,1,0:T(8,128)S(1)}, f32[8,128]{1,0:T(8,128)S(1)}, s32[]{:T(128)}, ...), condition=%wide.region_6.7_spmd.clone, body=%wide.region_5.6_spmd.clone.sunk | while | flops 396292 | bytes 1585275 | solution.py:26
  501.4 1.2 add_select_fusion.10
  502.7 1.2 add_select_fusion.10
  503.9 1.2 add_select_fusion.10
  505.2 1.2 add_select_fusion.10
  506.5 1.2 add_select_fusion.10
  509.0 1.2 add_select_fusion.10
  511.6 1.2 add_select_fusion.10
  514.1 1.2 add_select_fusion.10
  516.7 1.2 add_select_fusion.10
  519.2 1.2 add_select_fusion.10
  521.8 1.2 add_select_fusion.10
  523.1 1.2 add_select_fusion.10
  524.3 1.2 add_select_fusion.10
  525.6 1.2 add_select_fusion.10
  526.9 1.2 add_select_fusion.10
  528.1 1.2 add_select_fusion.10
  529.4 1.2 add_select_fusion.10
  530.7 1.2 add_select_fusion.10
  533.2 1.2 add_select_fusion.10
  535.8 1.2 add_select_fusion.10
  538.3 1.2 add_select_fusion.10
  540.9 1.2 add_select_fusion.10
  543.4 1.2 add_select_fusion.10
  546.0 1.2 add_select_fusion.10
  547.3 1.2 add_select_fusion.10
  548.5 1.2 add_select_fusion.10
  584.3 2.7 copy.76
  588.1 1.3 convolution_convert_fusion.1
  590.4 2.0 convolution_bitcast_fusion.5
  593.0 124.7 %reduce-scatter.2.cloned.1.call-done = f32[2,2,8,128]{3,2,1,0:T(8,128)} async-done(((f32[128,2,8,128]{3,2,1,0:T(8,128)}), f32[2,2,8,128]{3,2,1,0:T(8,128)}) %reduce-scatter.2.cloned.1.call-update) | async-done | bytes 16400 | tf_op jit(solution)/shard_map/reduce_scatter | solution.py:107
  719.6 4.0 all-to-all-start.1
  726.0 1.9 all-to-all-done.1
  (304 shorter events, 188.3 us)
Async XLA Ops:
  7.2 67.3 %copy-start = (bf16[256,1024]{1,0:T(8,128)(2,1)S(1)}, bf16[256,1024]{1,0:T(8,128)(2,1)}, u32[]{:S(2)}) copy-start(bf16[256,1024]{1,0:T(8,128)(2,1)} %param.11) | copy-start | bytes 1572868
  7.2 65.7 %copy-start.13 = (bf16[256,1024]{1,0:T(8,128)(2,1)S(1)}, bf16[256,1024]{1,0:T(8,128)(2,1)}, u32[]{:S(2)}) copy-start(bf16[256,1024]{1,0:T(8,128)(2,1)} %param.10) | copy-start | bytes 1572868
  7.2 206.7 %all-gather.7.cloned.1.call-start = ((), (), s32[]{:S(2)}) async-start(), calls=%async_computation.4 | async-start | bytes 34078720 | tf_op jit(solution)/shard_map/all_gather | solution.py:14
  72.9 2.8 copy-start.10
  74.5 49.1 %copy-start.11 = (bf16[256,1024]{1,0:T(8,128)(2,1)S(1)}, bf16[256,1024]{1,0:T(8,128)(2,1)}, u32[]{:S(2)}) copy-start(bf16[256,1024]{1,0:T(8,128)(2,1)} %param.9) | copy-start | bytes 1572868
  75.6 401.5 %all-gather.9.cloned.1.call-start = ((), (), s32[]{:S(2)}) async-start(), calls=%async_computation.5 | async-start | bytes 34078720 | tf_op jit(solution)/shard_map/all_gather | solution.py:14
  77.1 49.5 %copy-start.4 = (bf16[128,1,8,128]{0,3,2,1:T(8,128)(2,1)}, bf16[128,1,8,128]{0,3,2,1:T(8,128)(2,1)S(1)}, u32[]{:S(2)}) copy-start(bf16[128,1,8,128]{0,3,2,1:T(8,128)(2,1)S(1)} %copy.107) | copy-start | bytes 786436
  213.9 122.2 %copy-start.5 = (f32[256,1024]{0,1:T(8,128)S(1)}, f32[256,1024]{0,1:T(8,128)}, u32[]{:S(2)}) copy-start(f32[256,1024]{0,1:T(8,128)} %copy.57) | copy-start | bytes 3145732
  337.6 380.1 %reduce-scatter.2.cloned.1.call-start = ((), (), s32[]{:S(2)}) async-start(), calls=%async_computation.3 | async-start | bytes 1064960 | tf_op jit(solution)/shard_map/reduce_scatter | solution.py:107
  337.7 1.7 copy-start.6
  384.1 2.5 copy-start.7
  386.6 1.2 copy-start.9
  387.1 1.2 copy-start.1
  387.8 1.2 copy-start.12
  580.4 1.2 copy-start.2
  580.4 1.5 copy-start.8
  581.9 1.0 copy-start.14
  581.9 1.3 copy-start.3
  584.3 2.7 copy-start.15
  719.6 8.2 %all-to-all-start.1 = ((f32[4,1,1024]{2,1,0:T(1,128)}), f32[4,1,1024]{2,1,0:T(1,128)S(1)}, u32[]{:S(2)}, u32[]{:S(2)}) async-start(f32[4,1,1024]{2,1,0:T(1,128)} %reshape.66), calls=%async_computation.2 | async-start | bytes 32768 | tf_op jit(solution)/shard_map/all_to_all | solution.py:111
Sparse Core Ops, SparseCore 0:
  75.7 138.1 all-gather.6
  337.8 139.3 all-gather.8
  587.2 130.4 reduce-scatter.1
where the time goes:
time: 751 us; the launch traced here: 737 us
  waiting for transfers between devices  301 us (40%)
  other arithmetic  201 us (27%)
  blocking collectives  153 us (20%)
  local copies, waits for them, and re-layouts  38.5 us (5%)
  matrix products  21.4 us (3%)
  between operations  14.1 us (2%)
    select_n x252, other arithmetic, lap(): jnp.where(position < mine, new, old)  198 us
    all_gather x2, waiting for transfers between devices, prefix(): pieces = jax.tree.map(lambda part: lax.all_gather(part, axis), value)  174 us
    reduce_scatter x1, waiting for transfers between devices, body(): lax.psum_scatter(jnp.stack((from_query, from_key), axis=1), 'ctx', scatte...  125 us
    all_gather x2, blocking collectives, prefix(): pieces = jax.tree.map(lambda part: lax.all_gather(part, axis), value)  89 us
    all_gather x1, blocking collectives, body(): full_maps = lax.all_gather(own_maps, 'ctx', axis=0, tiled=True)  55.2 us
    rev x2, local copies, waits for them, and re-layouts, prefix(): pieces = jax.tree.map(lambda part: part[::-1], pieces)  23 us
  transfers between devices with their start and end apart: 4, of which 4 were waited for; matrix products, arithmetic and copies ran while one was open for 3% of the time, Pallas kernels for 0%

commit v1 on v0

v1 whole, which is shorter than its diff:
```python
import functools

import jax
import jax.numpy as jnp
from jax import lax
from jax.experimental import pallas as pl
from jax.experimental.pallas import tpu as pltpu
from jax.sharding import Mesh
from jax.sharding import PartitionSpec as P

HEAD_DIM = 128
BLOCK = 256
F32 = jnp.float32
BF16 = jnp.bfloat16
ROW = ("x", "core")
CTX = ("z", "x", "core")
EVERY = ("z", "x", "core", "y")


def mm(a, b):
    return lax.dot_general(a, b, (((1,), (0,)), ((), ())), preferred_element_type=F32)


def mm_nt(a, b):
    return lax.dot_general(a, b, (((1,), (1,)), ((), ())), preferred_element_type=F32)


def mm_tn(a, b):
    return lax.dot_general(a, b, (((0,), (0,)), ((), ())), preferred_element_type=F32)


def feature(pre):
    return jnp.where(pre > 0, pre + 1.0, jnp.exp(jnp.minimum(pre, 0.0)))


def halves(value):
    high = value.astype(BF16)
    return high, (value - high.astype(F32)).astype(BF16)


def causal_mask():
    rows = lax.broadcasted_iota(jnp.int32, (BLOCK, BLOCK), 0)
    cols = lax.broadcasted_iota(jnp.int32, (BLOCK, BLOCK), 1)
    return rows >= cols


def lanes(shape):
    return lax.broadcasted_iota(jnp.int32, shape, 1)


def row_slope(grad, attended):
    return jnp.broadcast_to(-jnp.sum(grad * attended, axis=1, keepdims=True), grad.shape)


def packed(total, out_ref):
    norms = total[:, HEAD_DIM:].T[:8]
    for z in range(out_ref.shape[0]):
        out_ref[z, :HEAD_DIM] = total[:, :HEAD_DIM]
        out_ref[z, HEAD_DIM:] = norms


def key_state(kv_ref, map_ref, fk_ref, out_ref):
    blocks = kv_ref.shape[0]
    ones = jnp.ones((BLOCK, HEAD_DIM), BF16)
    total = jnp.zeros((HEAD_DIM, 2 * HEAD_DIM), F32)
    for b in range(blocks):
        feat = feature(mm(kv_ref[b, 0], map_ref[...])).astype(BF16)
        fk_ref[b] = feat
        total = total + mm_tn(feat, jnp.concatenate([kv_ref[b, 1], ones], axis=1))
    packed(total, out_ref)


def forward(place_ref, kv_ref, qd_ref, fk_ref, map_ref, sums_ref,
            fq_ref, att_ref, weight_ref, grad_ref, slope_ref, high_ref, low_ref, adjoint_ref, out_ref):
    blocks = kv_ref.shape[0]
    place = place_ref[0]
    ones = jnp.ones((BLOCK, HEAD_DIM), BF16)
    prior = jnp.zeros((HEAD_DIM + 8, HEAD_DIM), F32)
    for z in range(sums_ref.shape[0]):
        prior = prior + jnp.where(z < place, sums_ref[z], 0.0)
    column = jnp.broadcast_to(prior[HEAD_DIM:HEAD_DIM + 1], (HEAD_DIM, HEAD_DIM)).T
    prior = jnp.concatenate([prior[:HEAD_DIM], column], axis=1)
    causal = causal_mask()
    lane = lanes((BLOCK, HEAD_DIM))
    total = jnp.zeros((HEAD_DIM, 2 * HEAD_DIM), F32)
    for b in range(blocks):
        feat_q = feature(mm(qd_ref[b, 0], map_ref[...])).astype(BF16)
        fq_ref[b] = feat_q
        feat_k = fk_ref[b]
        wide = jnp.concatenate([kv_ref[b, 1], ones], axis=1)
        high, low = halves(prior)
        high_ref[b] = high
        low_ref[b] = low
        scores = jnp.where(causal, mm_nt(feat_q, feat_k), 0.0)
        weight = scores.astype(BF16)
        weight_ref[b] = weight
        both = mm(jnp.concatenate([feat_q, feat_q], axis=1), jnp.concatenate([high, low], axis=0))
        inverse = 1.0 / (both[:, HEAD_DIM:] + jnp.sum(scores, axis=1, keepdims=True))
        attended = (both[:, :HEAD_DIM] + mm(weight, kv_ref[b, 1])) * inverse
        att_ref[b] = attended.astype(BF16)
        exact = qd_ref[b, 1].astype(F32) * inverse
        grad = exact.astype(BF16)
        slope_ref[b] = row_slope(exact, attended)
        slope_high, slope_low = halves(row_slope(grad.astype(F32), attended))
        none = jnp.zeros_like(slope_high)
        pair = jnp.where(lane == 0, slope_high, jnp.where(lane == 1, slope_low, none))
        grad = jnp.concatenate([grad, pair], axis=1)
        grad_ref[b] = grad
        adjoint = mm_tn(feat_q, grad)
        adjoint_ref[b] = adjoint
        total = total + adjoint
        prior = prior + mm_tn(feat_k, wide)
    packed(total, out_ref)


def query_side(kv_ref, qd_ref, fk_ref, fq_ref, att_ref, weight_ref, grad_ref, slope_ref, high_ref, low_ref, map_ref,
               aq_ref, key_ref, value_ref, map_grad_ref):
    blocks = kv_ref.shape[0]
    causal = causal_mask()
    map_grad = jnp.zeros((HEAD_DIM, HEAD_DIM), F32)
    for b in range(blocks):
        grad = grad_ref[b]
        half = grad[:, :HEAD_DIM]
        slope = slope_ref[b]
        feat_q = fq_ref[b]
        feat_k = fk_ref[b]
        dscore = mm_nt(half, kv_ref[b, 1]) + jnp.concatenate([slope, slope], axis=1)
        dscore = jnp.where(causal, dscore, 0.0).astype(BF16)
        d_feat = mm_nt(grad, high_ref[b]) + mm_nt(grad, low_ref[b]) + mm(dscore, feat_k)
        dpre = (d_feat * jnp.minimum(feat_q.astype(F32), 1.0)).astype(BF16)
        aq_ref[b, 0] = att_ref[b]
        aq_ref[b, 1] = mm_nt(dpre, map_ref[...]).astype(BF16)
        map_grad = map_grad + mm_tn(qd_ref[b, 0], dpre)
        key_ref[b] = mm_tn(dscore, feat_q)
        value_ref[b] = mm_tn(weight_ref[b], half)
    map_grad_ref[...] = map_grad


def key_side(place_ref, kv_ref, fk_ref, key_ref, value_ref, adjoint_ref, map_ref, sums_ref, out_ref, map_grad_ref):
    blocks = kv_ref.shape[0]
    place = place_ref[0]
    after = jnp.zeros((HEAD_DIM + 8, HEAD_DIM), F32)
    for z in range(sums_ref.shape[0]):
        after = after + jnp.where(z > place, sums_ref[z], 0.0)
    column = jnp.concatenate([after[HEAD_DIM:], jnp.zeros((HEAD_DIM - 8, HEAD_DIM), F32)], axis=0).T
    after = jnp.concatenate([after[:HEAD_DIM], column], axis=1)
    lane = lanes((BLOCK, HEAD_DIM))
    pair = jnp.where(lane < 2, 1.0, 0.0).astype(BF16)
    map_grad = jnp.zeros((HEAD_DIM, HEAD_DIM), F32)
    for b in range(blocks - 1, -1, -1):
        high, low = halves(after)
        feat_k = fk_ref[b]
        wide = jnp.concatenate([kv_ref[b, 1], pair], axis=1)
        d_feat = mm_nt(wide, high) + mm_nt(wide, low) + key_ref[b]
        dpre = (d_feat * jnp.minimum(feat_k.astype(F32), 1.0)).astype(BF16)
        out_ref[b, 0] = mm_nt(dpre, map_ref[...]).astype(BF16)
        stacked = jnp.concatenate([high[:, :HEAD_DIM], low[:, :HEAD_DIM]], axis=0)
        d_value = mm(jnp.concatenate([feat_k, feat_k], axis=1), stacked) + value_ref[b]
        out_ref[b, 1] = d_value.astype(BF16)
        map_grad = map_grad + mm_tn(kv_ref[b, 0], dpre)
        after = after + adjoint_ref[b]
    map_grad_ref[...] = map_grad


def call(kernel, shapes, scalars, flops, *operands):
    held = sum(v.size * v.dtype.itemsize for v in operands) + sum(
        s.size * s.dtype.itemsize for s in shapes
    )
    return pl.pallas_call(
        kernel,
        out_shape=shapes,
        in_specs=[pl.BlockSpec(memory_space=pltpu.SMEM)] * scalars
        + [pl.BlockSpec(memory_space=pltpu.VMEM)] * (len(operands) - scalars),
        out_specs=[pl.BlockSpec(memory_space=pltpu.VMEM)] * len(shapes),
        compiler_params=pltpu.CompilerParams(vmem_limit_bytes=40 * 1024 * 1024),
        cost_estimate=pl.CostEstimate(flops=flops, bytes_accessed=held, transcendentals=0),
    )(*operands)


def shape(*dims, dtype=BF16):
    return jax.ShapeDtypeStruct(dims, dtype)


def join_pair(first_ref, second_ref, out_ref):
    out_ref[0, 0] = first_ref[...]
    out_ref[0, 1] = second_ref[...]


def split_pair(in_ref, first_ref, second_ref):
    first_ref[...] = in_ref[0, 0]
    second_ref[...] = in_ref[0, 1]


def to_heads(first, second):
    rows, width = first.shape
    column = pl.BlockSpec((rows, HEAD_DIM), lambda h: (0, h))
    pieces = pl.pallas_call(
        join_pair,
        out_shape=shape(width // HEAD_DIM, 2, rows, HEAD_DIM),
        grid=(width // HEAD_DIM,),
        in_specs=[column, column],
        out_specs=pl.BlockSpec((1, 2, rows, HEAD_DIM), lambda h: (h, 0, 0, 0)),
    )(first, second)
    return lax.all_to_all(pieces, ROW, 0, 0, tiled=True)


def to_tokens(pieces):
    back = lax.all_to_all(pieces, ROW, 0, 0, tiled=True)
    heads, _, rows, _ = back.shape
    column = pl.BlockSpec((rows, HEAD_DIM), lambda h: (0, h))
    return pl.pallas_call(
        split_pair,
        out_shape=[shape(rows, heads * HEAD_DIM)] * 2,
        grid=(heads,),
        in_specs=[pl.BlockSpec((1, 2, rows, HEAD_DIM), lambda h: (h, 0, 0, 0))],
        out_specs=[column, column],
    )(back)


def body(queries, keys, values, out_grad, feature_weights):
    z_size, y_size = lax.axis_size("z"), lax.axis_size("y")
    row = lax.axis_size("x") * lax.axis_size("core")
    own, _, heads, cut = feature_weights.shape
    tokens = queries.shape[0] * lax.axis_size(CTX)
    place = lax.axis_index("z").astype(jnp.int32).reshape(1)

    kv = to_heads(keys, values)
    maps = feature_weights.transpose(2, 0, 1, 3).reshape(y_size, row, own * 2 * cut)
    maps = maps.transpose(1, 0, 2).reshape(1, heads, own * 2 * cut)
    maps = jnp.broadcast_to(maps, (z_size, heads, own * 2 * cut)).reshape(z_size * heads, -1)
    maps = lax.all_to_all(maps, EVERY, 0, 0, tiled=True)
    maps = maps.reshape(z_size * row, y_size, own, 2, cut).transpose(3, 0, 2, 1, 4)
    maps = maps.reshape(2, HEAD_DIM, HEAD_DIM)
    map_q, map_k = maps[0], maps[1]
    qd = to_heads(queries, out_grad)

    sums = shape(z_size, HEAD_DIM + 8, HEAD_DIM, dtype=F32)
    blocked = shape(row, BLOCK, HEAD_DIM)
    wide = shape(row, BLOCK, HEAD_DIM, dtype=F32)
    doubled = shape(row, BLOCK, 2 * HEAD_DIM)
    paired = shape(row, 2, BLOCK, HEAD_DIM)
    square = shape(HEAD_DIM, HEAD_DIM, dtype=F32)
    aug = shape(row, HEAD_DIM, 2 * HEAD_DIM)
    aug_wide = shape(row, HEAD_DIM, 2 * HEAD_DIM, dtype=F32)
    unit = 2 * row * BLOCK * HEAD_DIM * HEAD_DIM

    fk, state = call(key_state, [blocked, sums], 0, 3 * unit, kv, map_k)
    state = lax.all_to_all(state, "z", 0, 0, tiled=True)
    fq, att, weight, grad, slope, high, low, adjoint, total = call(
        forward,
        [blocked, blocked, doubled, doubled, wide, aug, aug, aug_wide, sums],
        1, 12 * unit, place, kv, qd, fk, map_q, state)
    total = lax.all_to_all(total, "z", 0, 0, tiled=True)
    aq, key_part, value_part, map_grad_q = call(
        query_side, [paired, wide, wide, square], 0, 14 * unit,
        kv, qd, fk, fq, att, weight, grad, slope, high, low, map_q)
    attended, query_grad = to_tokens(aq)
    dkv, map_grad_k = call(
        key_side, [paired, square], 1, 7 * unit,
        place, kv, fk, key_part, value_part, adjoint, map_k, total)
    key_grad, value_grad = to_tokens(dkv)

    map_grad = jnp.stack((map_grad_q, map_grad_k)).reshape(2, z_size * row, own, y_size, cut)
    map_grad = map_grad.transpose(1, 3, 2, 0, 4).reshape(z_size * heads, own * 2 * cut)
    map_grad = lax.all_to_all(map_grad, EVERY, 0, 0, tiled=True)
    map_grad = jnp.sum(map_grad.reshape(z_size, heads, own * 2 * cut), axis=0) / tokens
    map_grad = map_grad.reshape(row, y_size, own, 2, cut).transpose(2, 3, 1, 0, 4)
    map_grad = map_grad.reshape(own, 2, heads, cut)
    return attended, query_grad, key_grad, value_grad, map_grad


def solution(mesh):
    fine = Mesh(mesh.devices.reshape(8, 4, 2, 4), EVERY)
    flat = P(CTX, "y")
    maps = P(CTX, None, None, "y")
    return jax.shard_map(
        body,
        mesh=fine,
        in_specs=(flat, flat, flat, flat, maps),
        out_specs=(flat, flat, flat, flat, maps),
        check_vma=False,
    )
```

time: 751 us -> 191 us (0.25); the launches traced: 737 us -> 190 us
  waiting for transfers between devices: 301 us -> 67.5 us
  other arithmetic: 201 us -> 0.52 us
  blocking collectives: 153 us -> 18.4 us
  starting transfers between devices: 4.12 us -> 40.1 us
  Pallas kernels: 0 us -> 31.7 us
  matrix products: 21.4 us -> 0 us
  between operations: 14.1 us -> 0.8 us
  local copies, waits for them, and re-layouts: 38.5 us -> 30.5 us
    select_n x252 -> x0, other arithmetic: 198 us -> none  [lap(): jnp.where(position < mine, new, old)]
    all_gather x2 -> x0, waiting for transfers between devices: 174 us -> none  [prefix(): pieces = jax.tree.map(lambda part: lax.all_gather(part, axis), value)]
    all_gather x3 -> x0, blocking collectives: 144 us -> none  [the longest x2 89 us: prefix(): pieces = jax.tree.map(lambda part: lax.all_gather(part, axis), value)]
    reduce_scatter x1 -> x0, waiting for transfers between devices: 125 us -> none  [body(): lax.psum_scatter(jnp.stack((from_query, from_key), axis=1), 'ctx', scatte...]
    all_to_all x1 -> x7, waiting for transfers between devices: 1.86 us -> 67.5 us  [the longest x2 22.5 us: to_heads(): return lax.all_to_all(pieces, ROW, 0, 0, tiled=True)]
    all_to_all x1 -> x7, starting transfers between devices: 4 us -> 40.1 us  [the longest x1 15.7 us: body(): maps = lax.all_to_all(maps, EVERY, 0, 0, tiled=True)]
    pallas_call x0 -> x8, Pallas kernels: none -> 31.7 us  [the longest x4 11.3 us: call(): pl.pallas_call(kernel, out_shape=shapes, in_specs=[pl.BlockSpec(memory_sp...]
    rev x2 -> x0, local copies, waits for them, and re-layouts: 23 us -> none  [prefix(): pieces = jax.tree.map(lambda part: part[::-1], pieces)]
  transfers between devices with their start and end apart: 4 -> 7, of which waited for: 4 -> 7; matrix products, arithmetic and copies ran while one was open for 3% -> 3% of each run, Pallas kernels for 0% -> 12%
where the time goes in v1:
time: 191 us; the launch traced here: 190 us
  waiting for transfers between devices  67.5 us (35%)
  starting transfers between devices  40.1 us (21%)
  Pallas kernels  31.7 us (17%)
  local copies, waits for them, and re-layouts  30.5 us (16%)
  blocking collectives  18.4 us (10%)
    unnamed x50, local copies, waits for them, and re-layouts  23.7 us
    all_to_all x2, waiting for transfers between devices, to_heads(): return lax.all_to_all(pieces, ROW, 0, 0, tiled=True)  22.5 us
    all_to_all x1, blocking collectives, body(): map_grad = lax.all_to_all(map_grad, EVERY, 0, 0, tiled=True)  18.4 us
    all_to_all x1, waiting for transfers between devices, body(): state = lax.all_to_all(state, 'z', 0, 0, tiled=True)  16.8 us
    all_to_all x2, waiting for transfers between devices, to_tokens(): back = lax.all_to_all(pieces, ROW, 0, 0, tiled=True)  16.1 us
    all_to_all x1, starting transfers between devices, body(): maps = lax.all_to_all(maps, EVERY, 0, 0, tiled=True)  15.7 us
    pallas_call x4, Pallas kernels, call(): pl.pallas_call(kernel, out_shape=shapes, in_specs=[pl.BlockSpec(memory_sp...  11.3 us
    pallas_call x2, Pallas kernels, to_tokens(): pl.pallas_call(split_pair, out_shape=[shape(rows, heads * HEAD_DIM)] * 2,...  10.3 us
  transfers between devices with their start and end apart: 7, of which 7 were waited for; matrix products, arithmetic and copies ran while one was open for 3% of the time, Pallas kernels for 12%

profile of v1, /device:TPU:1, one launch (start us, length us, event | category | flops | bytes accessed | tf_op | source)
XLA Modules:
  0.0 189.5 jit_solution(676697713641014694)
XLA Ops:
  2.3 15.7 %all-to-all-start.2 = ((bf16[256,1,128]{2,1,0:T(2,128)(2,1)}), bf16[256,1,128]{2,1,0:T(2,128)(2,1)S(1)}, u32[]{:S(2)}, u32[]{:S(2)}) async-start(bf16[256,1,128]{2,1,0:T(2,128)(2,1)} %copy.30), calls=%async_computation.2 | async-start | bytes 262144 | tf_op jit(solution)/shard_map/all_to_all | solution.py:231
  18.0 5.0 %shard_map.92 = bf16[8,2,256,128]{3,2,1,0:T(8,128)(2,1)} custom-call(bf16[256,1024]{1,0:T(8,128)(2,1)} %first_ref.2, bf16[256,1024]{1,0:T(8,128)(2,1)} %second_ref.2), custom_call_target="tpu_custom_call" | custom-call | tf_op jit(solution)/shard_map/pallas_call | solution.py:197
  23.0 7.6 %all-to-all-done.2 = bf16[256,1,128]{2,1,0:T(2,128)(2,1)S(1)} async-done(((bf16[256,1,128]{2,1,0:T(2,128)(2,1)}), bf16[256,1,128]{2,1,0:T(2,128)(2,1)S(1)}, u32[]{:S(2)}, u32[]{:S(2)}) %all-to-all-start.2) | async-done | bytes 65568 | tf_op jit(solution)/shard_map/all_to_all | solution.py:231
  30.6 4.2 %all-to-all-start = ((bf16[8,2,256,128]{3,2,1,0:T(8,128)(2,1)}), bf16[8,2,256,128]{3,2,1,0:T(8,128)(2,1)S(1)}, u32[]{:S(2)}, u32[]{:S(2)}) async-start(bf16[8,2,256,128]{3,2,1,0:T(8,128)(2,1)} %shard_map.92), calls=%async_computation | async-start | bytes 2097152 | tf_op jit(solution)/shard_map/all_to_all | solution.py:204
  34.8 5.0 %shard_map.93 = bf16[8,2,256,128]{3,2,1,0:T(8,128)(2,1)} custom-call(bf16[256,1024]{1,0:T(8,128)(2,1)} %first_ref.3, bf16[256,1024]{1,0:T(8,128)(2,1)} %second_ref.3), custom_call_target="tpu_custom_call" | custom-call | tf_op jit(solution)/shard_map/pallas_call | solution.py:197
  39.8 10.1 %all-to-all-done.kv_ref = bf16[8,2,256,128]{3,2,1,0:T(8,128)(2,1)S(1)} async-done(((bf16[8,2,256,128]{3,2,1,0:T(8,128)(2,1)}), bf16[8,2,256,128]{3,2,1,0:T(8,128)(2,1)S(1)}, u32[]{:S(2)}, u32[]{:S(2)}) %all-to-all-start) | async-done | bytes 1048608 | tf_op jit(solution)/shard_map/all_to_all | solution.py:204
  49.9 4.3 %all-to-all-start.1 = ((bf16[8,2,256,128]{3,2,1,0:T(8,128)(2,1)}), bf16[8,2,256,128]{3,2,1,0:T(8,128)(2,1)S(1)}, u32[]{:S(2)}, u32[]{:S(2)}) async-start(bf16[8,2,256,128]{3,2,1,0:T(8,128)(2,1)} %shard_map.93), calls=%async_computation.1 | async-start | bytes 2097152 | tf_op jit(solution)/shard_map/all_to_all | solution.py:204
  55.3 0.8 shard_map.94
  56.2 0.8 copy-done.13
  57.0 12.4 %all-to-all-done.1.qd_ref = bf16[8,2,256,128]{3,2,1,0:T(8,128)(2,1)S(1)} async-done(((bf16[8,2,256,128]{3,2,1,0:T(8,128)(2,1)}), bf16[8,2,256,128]{3,2,1,0:T(8,128)(2,1)S(1)}, u32[]{:S(2)}, u32[]{:S(2)}) %all-to-all-start.1) | async-done | bytes 1048608 | tf_op jit(solution)/shard_map/all_to_all | solution.py:204
  69.4 3.5 %all-to-all-start.3 = ((f32[8,136,128]{2,1,0:T(8,128)}), f32[8,136,128]{2,1,0:T(8,128)S(1)}, u32[]{:S(2)}, u32[]{:S(2)}) async-start(f32[8,136,128]{2,1,0:T(8,128)} %copy-done.13), calls=%async_computation.3 | async-start | bytes 1114112 | tf_op jit(solution)/shard_map/all_to_all | solution.py:248
  73.6 1.0 squeeze.7.map_ref
  74.7 16.8 %all-to-all-done.3.sums_ref = f32[8,136,128]{2,1,0:T(8,128)S(1)} async-done(((f32[8,136,128]{2,1,0:T(8,128)}), f32[8,136,128]{2,1,0:T(8,128)S(1)}, u32[]{:S(2)}, u32[]{:S(2)}) %all-to-all-start.3) | async-done | bytes 557088 | tf_op jit(solution)/shard_map/all_to_all | solution.py:248
  91.5 4.2 %shard_map.95 = (bf16[8,256,128]{2,1,0:T(8,128)(2,1)S(1)}, bf16[8,256,128]{2,1,0:T(8,128)(2,1)S(1)}, bf16[8,256,256]{2,1,0:T(8,128)(2,1)S(1)}, bf16[8,256,256]{2...) custom-call(s32[1]{0:T(128)} %bitcast.5.place_ref, ...), custom_call_target="tpu_custom_call" | custom-call | flops 805306368 | bytes 10059780 | tf_op jit(solution)/shard_map/pallas_call | solution.py:169
  95.7 1.0 copy-done
  96.6 1.0 copy-done.2
  97.6 1.0 copy-done.4
  98.6 1.0 copy-done.7
  99.6 0.8 copy-done.14
  100.4 0.8 copy-done.15
  101.2 0.8 copy-done.17
  102.0 0.8 copy-done.19
  102.8 0.8 copy-done.21
  103.5 3.5 %all-to-all-start.5 = ((f32[8,136,128]{2,1,0:T(8,128)}), f32[8,136,128]{2,1,0:T(8,128)S(1)}, u32[]{:S(2)}, u32[]{:S(2)}) async-start(f32[8,136,128]{2,1,0:T(8,128)} %copy-done.14), calls=%async_computation.5 | async-start | bytes 1114112 | tf_op jit(solution)/shard_map/all_to_all | solution.py:253
  107.1 1.2 copy-done.1
  108.3 1.2 copy-done.3
  109.5 1.2 copy-done.5
  110.8 1.0 copy-done.16
  111.8 1.0 copy-done.18
  112.8 1.0 copy-done.20
  113.9 1.0 copy-done.22
  114.9 3.3 %shard_map.96 = (bf16[8,2,256,128]{3,2,1,0:T(8,128)(2,1)S(1)}, f32[8,256,128]{2,1,0:T(8,128)S(1)}, f32[8,256,128]{2,1,0:T(8,128)S(1)}, f32[128,128]{1,0:T(8,128)S(1)}) custom-call(bf16[8,2,256,128]{3,2,1,0:T(8,128)(2,1)S(1)} %all-to-all-done.kv_ref, bf16[8,2,256,128]{3,2,1,0:T(8,128)(2,1)S(1)} %all-to-all-done.1.qd_ref, ...), custom_call_target="tpu_custom_call" | custom-call | flops 939524096 | bytes 11108352 | tf_op jit(solution)/shard_map/pallas_call | solution.py:169
  118.3 1.0 copy-done.6
  119.2 1.0 copy-done.9
  120.2 1.0 copy-done.11
  121.3 4.5 %all-to-all-done.5.sums_ref = f32[8,136,128]{2,1,0:T(8,128)S(1)} async-done(((f32[8,136,128]{2,1,0:T(8,128)}), f32[8,136,128]{2,1,0:T(8,128)S(1)}, u32[]{:S(2)}, u32[]{:S(2)}) %all-to-all-start.5) | async-done | bytes 557088 | tf_op jit(solution)/shard_map/all_to_all | solution.py:253
  125.7 4.7 %all-to-all-start.4 = ((bf16[8,2,256,128]{3,2,1,0:T(8,128)(2,1)}), bf16[8,2,256,128]{3,2,1,0:T(8,128)(2,1)}, u32[]{:S(2)}, u32[]{:S(2)}) async-start(bf16[8,2,256,128]{3,2,1,0:T(8,128)(2,1)} %copy-done.6), calls=%async_computation.4 | async-start | bytes 2097152 | tf_op jit(solution)/shard_map/all_to_all | solution.py:208
  130.4 0.9 stack.9
  131.3 1.2 copy-done.10
  132.6 1.2 copy-done.12
  133.8 3.0 %shard_map.98 = (bf16[8,2,256,128]{3,2,1,0:T(8,128)(2,1)}, f32[128,128]{1,0:T(8,128)S(1)}) custom-call(s32[1]{0:T(128)} %bitcast.5.place_ref, bf16[8,2,256,128]{3,2,1,0:T(8,128)(2,1)S(1)} %all-to-all-done.kv_ref, bf16[8,256,128]{2,1,0:T(8,128)(2,1)S(1)} %get-tuple-element.26.fk_ref, f32[8,256,128]{2,1,0:T(8,128)S(1)} %copy-done.10, ...), custom_call_target="tpu_custom_call" | custom-call | flops 469762048 | bytes 6422532 | tf_op jit(solution)/shard_map/pallas_call | solution.py:169
  138.7 7.0 %all-to-all-done.4.in_ref = bf16[8,2,256,128]{3,2,1,0:T(8,128)(2,1)} async-done(((bf16[8,2,256,128]{3,2,1,0:T(8,128)(2,1)}), bf16[8,2,256,128]{3,2,1,0:T(8,128)(2,1)}, u32[]{:S(2)}, u32[]{:S(2)}) %all-to-all-start.4) | async-done | bytes 1048608 | tf_op jit(solution)/shard_map/all_to_all | solution.py:208
  145.7 18.4 %all_to_all.48 = f32[256,1,128]{2,1,0:T(1,128)S(1)} all-to-all(f32[256,1,128]{2,1,0:T(1,128)S(1)} %bitcast.17), channel_id=1, replica_groups=mesh['z'=8,'x'=4,'core'=2,'y'=4] {'z','x','core','y'}, dimensions={0} | all-to-all | bytes 262144 | tf_op jit(solution)/shard_map/all_to_all | solution.py:265
  164.1 4.2 %all-to-all-start.6 = ((bf16[8,2,256,128]{3,2,1,0:T(8,128)(2,1)}), bf16[8,2,256,128]{3,2,1,0:T(8,128)(2,1)S(1)}, u32[]{:S(2)}, u32[]{:S(2)}) async-start(bf16[8,2,256,128]{3,2,1,0:T(8,128)(2,1)} %get-tuple-element.42), calls=%async_computation.6 | async-start | bytes 2097152 | tf_op jit(solution)/shard_map/all_to_all | solution.py:208
  168.3 5.2 %shard_map.97 = (bf16[256,1024]{1,0:T(8,128)(2,1)}, bf16[256,1024]{1,0:T(8,128)(2,1)}) custom-call(bf16[8,2,256,128]{3,2,1,0:T(8,128)(2,1)} %all-to-all-done.4.in_ref), custom_call_target="tpu_custom_call" | custom-call | tf_op jit(solution)/shard_map/pallas_call | solution.py:211
  174.2 9.2 %all-to-all-done.6.in_ref = bf16[8,2,256,128]{3,2,1,0:T(8,128)(2,1)S(1)} async-done(((bf16[8,2,256,128]{3,2,1,0:T(8,128)(2,1)}), bf16[8,2,256,128]{3,2,1,0:T(8,128)(2,1)S(1)}, u32[]{:S(2)}, u32[]{:S(2)}) %all-to-all-start.6) | async-done | bytes 1048608 | tf_op jit(solution)/shard_map/all_to_all | solution.py:208
  183.4 1.0 copy-done.23
  184.4 5.2 %shard_map.99 = (bf16[256,1024]{1,0:T(8,128)(2,1)}, bf16[256,1024]{1,0:T(8,128)(2,1)}) custom-call(bf16[8,2,256,128]{3,2,1,0:T(8,128)(2,1)} %copy-done.23), custom_call_target="tpu_custom_call" | custom-call | tf_op jit(solution)/shard_map/pallas_call | solution.py:211
  (46 shorter events, 6.2 us)
Async XLA Ops:
  2.3 28.3 %all-to-all-start.2 = ((bf16[256,1,128]{2,1,0:T(2,128)(2,1)}), bf16[256,1,128]{2,1,0:T(2,128)(2,1)S(1)}, u32[]{:S(2)}, u32[]{:S(2)}) async-start(bf16[256,1,128]{2,1,0:T(2,128)(2,1)} %copy.30), calls=%async_computation.2 | async-start | bytes 262144 | tf_op jit(solution)/shard_map/all_to_all | solution.py:231
  30.6 19.3 %all-to-all-start = ((bf16[8,2,256,128]{3,2,1,0:T(8,128)(2,1)}), bf16[8,2,256,128]{3,2,1,0:T(8,128)(2,1)S(1)}, u32[]{:S(2)}, u32[]{:S(2)}) async-start(bf16[8,2,256,128]{3,2,1,0:T(8,128)(2,1)} %shard_map.92), calls=%async_computation | async-start | bytes 2097152 | tf_op jit(solution)/shard_map/all_to_all | solution.py:204
  49.9 19.4 %all-to-all-start.1 = ((bf16[8,2,256,128]{3,2,1,0:T(8,128)(2,1)}), bf16[8,2,256,128]{3,2,1,0:T(8,128)(2,1)S(1)}, u32[]{:S(2)}, u32[]{:S(2)}) async-start(bf16[8,2,256,128]{3,2,1,0:T(8,128)(2,1)} %shard_map.93), calls=%async_computation.1 | async-start | bytes 2097152 | tf_op jit(solution)/shard_map/all_to_all | solution.py:204
  56.2 0.8 copy-start.13
  69.4 22.1 %all-to-all-start.3 = ((f32[8,136,128]{2,1,0:T(8,128)}), f32[8,136,128]{2,1,0:T(8,128)S(1)}, u32[]{:S(2)}, u32[]{:S(2)}) async-start(f32[8,136,128]{2,1,0:T(8,128)} %copy-done.13), calls=%async_computation.3 | async-start | bytes 1114112 | tf_op jit(solution)/shard_map/all_to_all | solution.py:248
  95.7 1.0 copy-start
  96.6 1.0 copy-start.2
  97.6 1.0 copy-start.4
  98.6 1.0 copy-start.7
  99.6 0.8 copy-start.14
  100.4 0.8 copy-start.15
  101.2 0.8 copy-start.17
  102.0 0.8 copy-start.19
  102.7 0.8 copy-start.21
  103.5 22.2 %all-to-all-start.5 = ((f32[8,136,128]{2,1,0:T(8,128)}), f32[8,136,128]{2,1,0:T(8,128)S(1)}, u32[]{:S(2)}, u32[]{:S(2)}) async-start(f32[8,136,128]{2,1,0:T(8,128)} %copy-done.14), calls=%async_computation.5 | async-start | bytes 1114112 | tf_op jit(solution)/shard_map/all_to_all | solution.py:253
  107.1 1.2 copy-start.1
  108.3 1.2 copy-start.3
  109.5 1.2 copy-start.5
  110.8 1.0 copy-start.16
  111.8 1.0 copy-start.18
  112.8 1.0 copy-start.20
  113.9 1.0 copy-start.22
  118.3 1.0 copy-start.6
  119.2 1.0 copy-start.9
  120.2 1.0 copy-start.11
  125.7 5.6 %copy-start.8 = (f32[8,128,256]{2,1,0:T(8,128)S(1)}, f32[8,128,256]{2,1,0:T(8,128)}, u32[]{:S(2)}) copy-start(f32[8,128,256]{2,1,0:T(8,128)} %copy-done.7) | copy-start | bytes 3145732
  125.7 20.0 %all-to-all-start.4 = ((bf16[8,2,256,128]{3,2,1,0:T(8,128)(2,1)}), bf16[8,2,256,128]{3,2,1,0:T(8,128)(2,1)}, u32[]{:S(2)}, u32[]{:S(2)}) async-start(bf16[8,2,256,128]{3,2,1,0:T(8,128)(2,1)} %copy-done.6), calls=%async_computation.4 | async-start | bytes 2097152 | tf_op jit(solution)/shard_map/all_to_all | solution.py:208
  131.3 1.2 copy-start.10
  132.5 1.2 copy-start.12
  136.8 0.9 copy-start.24
  164.1 19.3 %all-to-all-start.6 = ((bf16[8,2,256,128]{3,2,1,0:T(8,128)(2,1)}), bf16[8,2,256,128]{3,2,1,0:T(8,128)(2,1)S(1)}, u32[]{:S(2)}, u32[]{:S(2)}) async-start(bf16[8,2,256,128]{3,2,1,0:T(8,128)(2,1)} %get-tuple-element.42), calls=%async_computation.6 | async-start | bytes 2097152 | tf_op jit(solution)/shard_map/all_to_all | solution.py:208
  183.4 1.0 copy-start.23

commit v2 on v1

v2 whole, which is shorter than its diff:
```python
import jax
import jax.numpy as jnp
from jax import lax
from jax.experimental import pallas as pl
from jax.experimental.pallas import tpu as pltpu
from jax.sharding import Mesh
from jax.sharding import PartitionSpec as P

HEAD_DIM = 128
BLOCK = 256
F32 = jnp.float32
BF16 = jnp.bfloat16
ROW = ("x", "core")
PLANE = ("z", "y")
CTX = ("z", "x", "core")
EVERY = ("z", "x", "core", "y")
HBM = pl.BlockSpec(memory_space=pltpu.HBM)
VMEM = pl.BlockSpec(memory_space=pltpu.VMEM)
SMEM = pl.BlockSpec(memory_space=pltpu.SMEM)
DMA = pltpu.SemaphoreType.DMA
AUX = 32
STATE_ROWS = HEAD_DIM + AUX


def mm(a, b):
    return lax.dot_general(a, b, (((1,), (0,)), ((), ())), preferred_element_type=F32)


def mm_nt(a, b):
    return lax.dot_general(a, b, (((1,), (1,)), ((), ())), preferred_element_type=F32)


def mm_tn(a, b):
    return lax.dot_general(a, b, (((0,), (0,)), ((), ())), preferred_element_type=F32)


def feature(pre):
    return jnp.where(pre > 0, pre + 1.0, jnp.exp(jnp.minimum(pre, 0.0)))


def halves(value):
    high = value.astype(BF16)
    return high, (value - high.astype(F32)).astype(BF16)


def causal_mask():
    rows = lax.broadcasted_iota(jnp.int32, (BLOCK, BLOCK), 0)
    cols = lax.broadcasted_iota(jnp.int32, (BLOCK, BLOCK), 1)
    return rows >= cols


def lanes(rows):
    return lax.broadcasted_iota(jnp.int32, (rows, HEAD_DIM), 1)


def row_slope(grad, attended):
    return jnp.broadcast_to(-jnp.sum(grad * attended, axis=1, keepdims=True), grad.shape)


def start_all(copies):
    for copy in copies:
        copy.start()
    return copies


def wait_all(copies):
    for copy in copies:
        copy.wait()


def norm_rows(column):
    rows = column.T[:16]
    index = lax.broadcasted_iota(jnp.int32, (16, HEAD_DIM), 0)
    high = rows.astype(BF16).astype(F32)
    mid = (rows - high).astype(BF16).astype(F32)
    low = rows - high - mid
    return jnp.where(
        index == 0, high, jnp.where(index == 1, mid, jnp.where(index == 2, low, 0.0))
    ).astype(BF16)


def pack_keys(k_ref, v_ref, map_ref, out_ref, sem):
    copies = []
    for h in range(out_ref.shape[0]):
        column = pl.ds(h * HEAD_DIM, HEAD_DIM)
        copies.append(pltpu.make_async_copy(k_ref.at[:, column], out_ref.at[h, pl.ds(0, BLOCK)], sem.at[h, 0]))
        copies.append(pltpu.make_async_copy(v_ref.at[:, column], out_ref.at[h, pl.ds(BLOCK, BLOCK)], sem.at[h, 1]))
        rows = pl.ds(h * AUX, AUX)
        copies.append(pltpu.make_async_copy(map_ref.at[rows], out_ref.at[h, pl.ds(2 * BLOCK, AUX)], sem.at[h, 2]))
    wait_all(start_all(copies))


def pack_pair(place_ref, first_ref, second_ref, *rest):
    outs, sem = rest[:-1], rest[-1]
    copies = []
    for s, out_ref in enumerate(outs):
        column = pl.ds(pl.multiple_of((place_ref[1] ^ s) * HEAD_DIM, HEAD_DIM), HEAD_DIM)
        copies.append(pltpu.make_async_copy(first_ref.at[:, column], out_ref.at[0], sem.at[s, 0]))
        copies.append(pltpu.make_async_copy(second_ref.at[:, column], out_ref.at[1], sem.at[s, 1]))
    wait_all(start_all(copies))


def split_pair(place_ref, *rest):
    pieces, (first_ref, second_ref, sem) = rest[:-3], rest[-3:]
    copies = []
    for s, in_ref in enumerate(pieces):
        column = pl.ds(pl.multiple_of((place_ref[1] ^ s) * HEAD_DIM, HEAD_DIM), HEAD_DIM)
        copies.append(pltpu.make_async_copy(in_ref.at[0], first_ref.at[:, column], sem.at[s, 0]))
        copies.append(pltpu.make_async_copy(in_ref.at[1], second_ref.at[:, column], sem.at[s, 1]))
    wait_all(start_all(copies))


def split_keys(in_ref, k_ref, v_ref, sem):
    copies = []
    for h in range(in_ref.shape[0]):
        column = pl.ds(h * HEAD_DIM, HEAD_DIM)
        copies.append(pltpu.make_async_copy(in_ref.at[h, pl.ds(0, BLOCK)], k_ref.at[:, column], sem.at[h, 0]))
        copies.append(pltpu.make_async_copy(in_ref.at[h, pl.ds(BLOCK, BLOCK)], v_ref.at[:, column], sem.at[h, 1]))
    wait_all(start_all(copies))


def key_state(kw_ref, map_ref, fk_ref, out_ref, kv, fk, send, in_sem, fk_sem, out_sem):
    blocks = kw_ref.shape[0]
    loads = start_all([
        pltpu.make_async_copy(kw_ref.at[b, pl.ds(0, 2 * BLOCK)], kv.at[b], in_sem.at[b]) for b in range(blocks)
    ])
    ones = jnp.ones((BLOCK, HEAD_DIM), BF16)
    total = jnp.zeros((HEAD_DIM, 2 * HEAD_DIM), F32)
    mean = jnp.zeros((1, HEAD_DIM), F32)
    stores = []
    for b in range(blocks):
        loads[b].wait()
        feat = feature(mm(kv[b, :BLOCK], map_ref[...])).astype(BF16)
        fk[b] = feat
        stores += start_all([pltpu.make_async_copy(fk.at[b], fk_ref.at[b], fk_sem.at[b])])
        value = kv[b, BLOCK:]
        mean = mean + jnp.sum(value.astype(F32), axis=0, keepdims=True)
        total = total + mm_tn(feat, jnp.concatenate([value, ones], axis=1))
    centre = (mean * (1.0 / (blocks * BLOCK))).astype(BF16)
    column = total[:, HEAD_DIM:]
    send[:HEAD_DIM] = (total[:, :HEAD_DIM] - column * centre.astype(F32)).astype(BF16)
    send[HEAD_DIM:HEAD_DIM + 16] = norm_rows(column)
    send[HEAD_DIM + 16:] = jnp.broadcast_to(centre, (16, HEAD_DIM))
    stores += start_all([
        pltpu.make_async_copy(send, out_ref.at[z], out_sem.at[z]) for z in range(out_ref.shape[0])
    ])
    wait_all(stores)


def forward(place_ref, kw_ref, fk_ref, map_ref, sums_ref, *rest):
    blocks = kw_ref.shape[0]
    qd_refs = rest[:blocks]
    (fq_ref, att_ref, weight_ref, grad_ref, high_ref, low_ref, adjoint_ref, out_ref,
     v, fk, qd, fq, att, weights, grads, highs, lows, adjoints, send,
     v_sem, fk_sem, qd_sem, store_sem, out_sem) = rest[blocks:]
    place = place_ref[0]
    loads = []
    for s in range(blocks):
        slot = place_ref[1] ^ s
        loads.append(pltpu.make_async_copy(qd_refs[s], qd.at[slot], qd_sem.at[s]))
        loads.append(pltpu.make_async_copy(kw_ref.at[s, pl.ds(BLOCK, BLOCK)], v.at[s], v_sem.at[s]))
        loads.append(pltpu.make_async_copy(fk_ref.at[s], fk.at[s], fk_sem.at[s]))
    start_all(loads)
    prior = jnp.zeros((HEAD_DIM, HEAD_DIM), F32)
    norms, centres = [], []
    for z in range(sums_ref.shape[0]):
        part = sums_ref[z].astype(F32)
        part = jnp.where(z < place, part, 0.0)
        prior = prior + part[:HEAD_DIM]
        norms.append(part[HEAD_DIM:HEAD_DIM + 16].astype(BF16))
        centres.append(sums_ref[z, HEAD_DIM + 16:])
    norms = jnp.concatenate(norms, axis=0)
    centres = jnp.concatenate(centres, axis=0)
    centres = jnp.concatenate([centres, jnp.ones_like(centres)], axis=1)
    prior = jnp.concatenate([prior, jnp.zeros_like(prior)], axis=1) + mm_tn(norms, centres)
    causal = causal_mask()
    lane = lanes(BLOCK)
    few = lanes(HEAD_DIM) < 2
    ones = jnp.ones((BLOCK, HEAD_DIM), BF16)
    total = jnp.zeros((HEAD_DIM, 2 * HEAD_DIM), F32)
    centre = jnp.zeros((1, HEAD_DIM), F32)
    wait_all(loads)
    stores = []
    for b in range(blocks):
        feat_q = feature(mm(qd[b, 0], map_ref[...])).astype(BF16)
        fq[b] = feat_q
        feat_k = fk[b]
        value = v[b]
        centre = centre + jnp.sum(value.astype(F32), axis=0, keepdims=True)
        high, low = halves(prior)
        none = jnp.zeros((HEAD_DIM, HEAD_DIM), BF16)
        highs[b] = jnp.concatenate([high[:, :HEAD_DIM], jnp.where(few, high[:, HEAD_DIM:], none)], axis=1)
        lows[b] = jnp.concatenate([low[:, :HEAD_DIM], jnp.where(few, low[:, HEAD_DIM:], none)], axis=1)
        scores = jnp.where(causal, mm_nt(feat_q, feat_k), 0.0)
        weight = scores.astype(BF16)
        weights[b] = weight
        both = mm(jnp.concatenate([feat_q, feat_q], axis=1), jnp.concatenate([high, low], axis=0))
        inverse = 1.0 / (both[:, HEAD_DIM:] + jnp.sum(scores, axis=1, keepdims=True))
        attended = (both[:, :HEAD_DIM] + mm(weight, value)) * inverse
        att[b] = attended.astype(BF16)
        exact = qd[b, 1].astype(F32) * inverse
        grad = exact.astype(BF16)
        within_high, within_low = halves(row_slope(exact, attended))
        across_high, across_low = halves(row_slope(grad.astype(F32), attended))
        pair = jnp.where(lane == 0, across_high, jnp.where(lane == 1, across_low, 0.0))
        pair = jnp.where(lane == 2, within_high, jnp.where(lane == 3, within_low, pair)).astype(BF16)
        grad = jnp.concatenate([grad, pair], axis=1)
        grads[b] = grad
        adjoint = mm_tn(feat_q, grad)
        adjoints[b] = adjoint
        total = total + adjoint
        prior = prior + mm_tn(feat_k, jnp.concatenate([value, ones], axis=1))
        pairs = ((fq, fq_ref), (att, att_ref), (weights, weight_ref), (grads, grad_ref),
                 (highs, high_ref), (lows, low_ref), (adjoints, adjoint_ref))
        stores += start_all([
            pltpu.make_async_copy(held.at[b], out.at[b], store_sem.at[n, b]) for n, (held, out) in enumerate(pairs)
        ])
    sent = total[:, :HEAD_DIM].astype(BF16)
    centre = (centre * (1.0 / (blocks * BLOCK))).astype(BF16).astype(F32)
    rest_of = jnp.sum((total[:, :HEAD_DIM] - sent.astype(F32)) * centre, axis=1, keepdims=True)
    column = jnp.sum(jnp.where(few, total[:, HEAD_DIM:], 0.0), axis=1, keepdims=True) + rest_of
    send[:HEAD_DIM] = sent
    send[HEAD_DIM:HEAD_DIM + 16] = norm_rows(jnp.broadcast_to(column, (HEAD_DIM, HEAD_DIM)))
    send[HEAD_DIM + 16:] = jnp.zeros((16, HEAD_DIM), BF16)
    stores += start_all([
        pltpu.make_async_copy(send, out_ref.at[z], out_sem.at[z]) for z in range(out_ref.shape[0])
    ])
    wait_all(stores)


def query_side(place_ref, kw_ref, fk_ref, map_ref, fq_ref, att_ref, weight_ref, grad_ref, high_ref, low_ref, *rest):
    blocks = kw_ref.shape[0]
    qd_refs, rest = rest[:blocks], rest[blocks:]
    aq_refs, rest = rest[:blocks], rest[blocks:]
    (key_ref, value_ref, map_grad_ref, v, q, fk, fq, weights, grads, highs, lows, dq, keys, values,
     att_sem, load_sem, q_sem, dq_sem, store_sem) = rest
    loads = [[] for _ in range(blocks)]
    others, turned = [], []
    for s in range(blocks):
        slot = place_ref[1] ^ s
        turned.append(pltpu.make_async_copy(qd_refs[s].at[0], q.at[slot], q_sem.at[s]))
        others.append(pltpu.make_async_copy(att_ref.at[slot], aq_refs[s].at[0], att_sem.at[s]))
    start_all(turned)
    for b in range(blocks):
        loads[b].append(pltpu.make_async_copy(kw_ref.at[b, pl.ds(BLOCK, BLOCK)], v.at[b], load_sem.at[0, b]))
        pairs = ((fk_ref, fk), (fq_ref, fq), (weight_ref, weights), (grad_ref, grads), (high_ref, highs), (low_ref, lows))
        for n, (held, into) in enumerate(pairs):
            loads[b].append(pltpu.make_async_copy(held.at[b], into.at[b], load_sem.at[n + 1, b]))
        start_all(loads[b])
    start_all(others)
    causal = causal_mask()
    lane = lanes(BLOCK)
    unit = jnp.where((lane == 2) | (lane == 3), 1.0, 0.0).astype(BF16)
    map_grad = jnp.zeros((HEAD_DIM, HEAD_DIM), F32)
    wait_all(turned)
    stores = []
    for b in range(blocks):
        wait_all(loads[b])
        grad = grads[b]
        feat_q = fq[b]
        dscore = mm_nt(grad, jnp.concatenate([v[b], unit], axis=1))
        dscore = jnp.where(causal, dscore, 0.0).astype(BF16)
        d_feat = mm_nt(grad, highs[b]) + mm_nt(grad, lows[b]) + mm(dscore, fk[b])
        dpre = (d_feat * jnp.minimum(feat_q.astype(F32), 1.0)).astype(BF16)
        dq[b] = mm_nt(dpre, map_ref[...]).astype(BF16)
        map_grad = map_grad + mm_tn(q[b], dpre)
        keys[b] = mm_tn(dscore, feat_q)
        values[b] = mm_tn(weights[b], grad[:, :HEAD_DIM])
        stores += start_all([
            pltpu.make_async_copy(keys.at[b], key_ref.at[b], store_sem.at[0, b]),
            pltpu.make_async_copy(values.at[b], value_ref.at[b], store_sem.at[1, b]),
        ])
    stores += start_all([
        pltpu.make_async_copy(dq.at[place_ref[1] ^ s], aq_refs[s].at[1], dq_sem.at[s]) for s in range(blocks)
    ])
    map_grad_ref[...] = map_grad
    wait_all(others)
    wait_all(stores)


def key_side(place_ref, kw_ref, fk_ref, key_ref, value_ref, adjoint_ref, map_ref, sums_ref, map_grad_ref,
             out_ref, kv, fk, keys, values, adjoints, out, load_sem, out_sem):
    blocks = kw_ref.shape[0]
    place = place_ref[0]
    loads = []
    for b in range(blocks):
        copies = [pltpu.make_async_copy(kw_ref.at[b, pl.ds(0, 2 * BLOCK)], kv.at[b], load_sem.at[0, b])]
        pairs = ((fk_ref, fk), (key_ref, keys), (value_ref, values), (adjoint_ref, adjoints))
        for n, (held, into) in enumerate(pairs):
            copies.append(pltpu.make_async_copy(held.at[b], into.at[b], load_sem.at[n + 1, b]))
        loads.append(copies)
    for b in range(blocks - 1, -1, -1):
        start_all(loads[b])
    after = jnp.zeros((HEAD_DIM, HEAD_DIM), F32)
    norms = []
    for z in range(sums_ref.shape[0]):
        part = jnp.where(z > place, sums_ref[z].astype(F32), 0.0)
        after = after + part[:HEAD_DIM]
        norms.append(part[HEAD_DIM:HEAD_DIM + 16].astype(BF16))
    norms = jnp.concatenate(norms, axis=0)
    first = jnp.where(lanes(HEAD_DIM) == 0, 1.0, 0.0).astype(BF16)
    after = jnp.concatenate([after, mm_tn(norms, first)], axis=1)
    pair = jnp.where(lanes(BLOCK) < 2, 1.0, 0.0).astype(BF16)
    map_grad = jnp.zeros((HEAD_DIM, HEAD_DIM), F32)
    for b in range(blocks - 1, -1, -1):
        wait_all(loads[b])
        high, low = halves(after)
        feat_k = fk[b]
        wide = jnp.concatenate([kv[b, BLOCK:], pair], axis=1)
        d_feat = mm_nt(wide, high) + mm_nt(wide, low) + keys[b]
        dpre = (d_feat * jnp.minimum(feat_k.astype(F32), 1.0)).astype(BF16)
        out[b, :BLOCK] = mm_nt(dpre, map_ref[...]).astype(BF16)
        stacked = jnp.concatenate([high[:, :HEAD_DIM], low[:, :HEAD_DIM]], axis=0)
        d_value = mm(jnp.concatenate([feat_k, feat_k], axis=1), stacked) + values[b]
        out[b, BLOCK:2 * BLOCK] = d_value.astype(BF16)
        map_grad = map_grad + mm_tn(kv[b, :BLOCK], dpre)
        after = after + adjoints[b]
    width = HEAD_DIM // blocks
    to = lax.broadcasted_iota(jnp.int32, (HEAD_DIM, HEAD_DIM), 0)
    of = lax.broadcasted_iota(jnp.int32, (HEAD_DIM, HEAD_DIM), 1)
    source = (to % width) // 2 * width + to // width * 2 + to % 2
    order = jnp.where(source == of, 1.0, 0.0).astype(BF16)
    for n, grad in enumerate((map_grad_ref[...], map_grad)):
        for m, part in enumerate(halves(grad)):
            rows = mm(order, part).astype(BF16)
            for b in range(blocks):
                at = 2 * BLOCK + (2 * n + m) * width
                out[b, at:at + width] = rows[b * width:(b + 1) * width]
    wait_all(start_all([
        pltpu.make_async_copy(out.at[b], out_ref.at[b], out_sem.at[b]) for b in range(blocks)
    ]))


def shape(*dims, dtype=BF16):
    return jax.ShapeDtypeStruct(dims, dtype)


def call(kernel, outs, operands, scratch, cycles=1, vmem=30):
    return pl.pallas_call(
        kernel,
        out_shape=[s for _, s in outs],
        in_specs=[spec for spec, _ in operands],
        out_specs=[spec for spec, _ in outs],
        scratch_shapes=scratch,
        compiler_params=pltpu.CompilerParams(vmem_limit_bytes=vmem * 1024 * 1024),
        cost_estimate=pl.CostEstimate(flops=cycles * 500_000_000, bytes_accessed=cycles * 2_000_000, transcendentals=0),
    )(*[v for _, v in operands])


def trade(pieces):
    count = len(pieces)
    return [pieces[0]] + [
        lax.ppermute(pieces[s], ROW, [(i, i ^ s) for i in range(count)]) for s in range(1, count)
    ]


def body(queries, keys, values, out_grad, feature_weights):
    z_size, y_size = lax.axis_size("z"), lax.axis_size("y")
    row = lax.axis_size("x") * lax.axis_size("core")
    own, _, heads, cut = feature_weights.shape
    tokens = queries.shape[0] * lax.axis_size(CTX)
    place = jnp.stack([lax.axis_index("z"), lax.axis_index(ROW)]).astype(jnp.int32)
    scratch = pltpu.VMEM

    maps = feature_weights.transpose(2, 0, 1, 3).reshape(1, heads, own * 2 * cut)
    maps = jnp.broadcast_to(maps, (z_size, heads, own * 2 * cut)).reshape(z_size * heads, -1)
    maps = lax.all_to_all(maps, PLANE, 0, 0, tiled=True)
    maps = maps.reshape(z_size * y_size, row, -1).transpose(1, 0, 2).reshape(row * AUX, HEAD_DIM)

    long = shape(row, 2 * BLOCK + AUX, HEAD_DIM)
    piece = shape(2, BLOCK, HEAD_DIM)
    (kw,) = call(pack_keys, [(HBM, long)], [(HBM, keys), (HBM, values), (HBM, maps)], [DMA((row, 3))])
    qd = call(pack_pair, [(HBM, piece)] * row, [(SMEM, place), (HBM, queries), (HBM, out_grad)], [DMA((row, 2))])
    kw = lax.all_to_all(kw, ROW, 0, 0, tiled=True)
    qd = trade(qd)
    maps = kw[:, 2 * BLOCK:].reshape(row, z_size, y_size, own, 2, cut).transpose(4, 1, 0, 3, 2, 5)
    maps = maps.reshape(2, HEAD_DIM, HEAD_DIM)
    map_q, map_k = maps[0], maps[1]

    sums = shape(z_size, STATE_ROWS, HEAD_DIM)
    one = (row, BLOCK, HEAD_DIM)
    two = (row, BLOCK, 2 * HEAD_DIM)
    aug = (row, HEAD_DIM, 2 * HEAD_DIM)
    send = scratch((STATE_ROWS, HEAD_DIM), BF16)

    fk, state = call(
        key_state, [(HBM, shape(*one)), (HBM, sums)], [(HBM, kw), (VMEM, map_k)],
        [scratch((row, 2 * BLOCK, HEAD_DIM), BF16), scratch(one, BF16), send, DMA((row,)), DMA((row,)), DMA((z_size,))])
    state = lax.all_to_all(state, "z", 0, 0, tiled=True)
    fq, att, weight, grad, high, low, adjoint, total = call(
        forward,
        [(HBM, shape(*one)), (HBM, shape(*one)), (HBM, shape(*two)), (HBM, shape(*two)), (HBM, shape(*aug)),
         (HBM, shape(*aug)), (HBM, shape(*aug, dtype=F32)), (HBM, sums)],
        [(SMEM, place), (HBM, kw), (HBM, fk), (VMEM, map_q), (VMEM, state)] + [(HBM, v) for v in qd],
        [scratch(one, BF16), scratch(one, BF16), scratch((row, 2, BLOCK, HEAD_DIM), BF16),
         scratch(one, BF16), scratch(one, BF16), scratch(two, BF16), scratch(two, BF16), scratch(aug, BF16),
         scratch(aug, BF16), scratch(aug, F32), send,
         DMA((row,)), DMA((row,)), DMA((row,)), DMA((7, row)), DMA((z_size,))], cycles=4)
    total = lax.all_to_all(total, "z", 0, 0, tiled=True)
    *aq, key_part, value_part, map_grad_q = call(
        query_side,
        [(HBM, piece)] * row + [(HBM, shape(*one, dtype=F32))] * 2 + [(VMEM, shape(HEAD_DIM, HEAD_DIM, dtype=F32))],
        [(SMEM, place), (HBM, kw), (HBM, fk), (VMEM, map_q), (HBM, fq), (HBM, att), (HBM, weight), (HBM, grad),
         (HBM, high), (HBM, low)] + [(HBM, v) for v in qd],
        [scratch(one, BF16), scratch(one, BF16), scratch(one, BF16), scratch(one, BF16), scratch(two, BF16),
         scratch(two, BF16), scratch(aug, BF16), scratch(aug, BF16), scratch(one, BF16), scratch(one, F32),
         scratch(one, F32), DMA((row,)), DMA((7, row)), DMA((row,)), DMA((row,)), DMA((2, row))], cycles=3)
    aq = trade(aq)
    flat = (HBM, shape(*queries.shape))
    width = 4 * HEAD_DIM // row
    longer = (row, 2 * BLOCK + width, HEAD_DIM)
    (dkv,) = call(
        key_side, [(HBM, shape(*longer))],
        [(SMEM, place), (HBM, kw), (HBM, fk), (HBM, key_part), (HBM, value_part), (HBM, adjoint), (VMEM, map_k),
         (VMEM, total), (VMEM, map_grad_q)],
        [scratch((row, 2 * BLOCK, HEAD_DIM), BF16), scratch(one, BF16), scratch(one, F32), scratch(one, F32),
         scratch(aug, F32), scratch(longer, BF16), DMA((5, row)), DMA((row,))], cycles=3)
    dkv = lax.all_to_all(dkv, ROW, 0, 0, tiled=True)
    attended, query_grad = call(
        split_pair, [flat, flat], [(SMEM, place)] + [(HBM, v) for v in aq], [DMA((row, 2))])
    key_grad, value_grad = call(split_keys, [flat, flat], [(HBM, dkv)], [DMA((row, 2))])

    map_grad = dkv[:, 2 * BLOCK:].reshape(row, 2, 2, z_size, own, y_size, cut).astype(F32)
    map_grad = map_grad[:, :, 0] + map_grad[:, :, 1]
    map_grad = map_grad.transpose(2, 4, 0, 1, 3, 5).reshape(z_size * heads, 2 * own * cut)
    map_grad = lax.all_to_all(map_grad, PLANE, 0, 0, tiled=True)
    map_grad = jnp.sum(map_grad.reshape(z_size, heads, 2, own, cut), axis=0) / tokens
    map_grad = map_grad.transpose(2, 1, 0, 3)
    return attended, query_grad, key_grad, value_grad, map_grad


def solution(mesh):
    fine = Mesh(mesh.devices.reshape(8, 4, 2, 4), EVERY)
    flat = P(CTX, "y")
    maps = P(CTX, None, None, "y")
    return jax.shard_map(
        body,
        mesh=fine,
        in_specs=(flat, flat, flat, flat, maps),
        out_specs=(flat, flat, flat, flat, maps),
        check_vma=False,
    )
```

time: 191 us -> 230 us (1.20)
  waiting for transfers between devices: 67.5 us -> 31.3 us
  Pallas kernels: 31.7 us -> 59.2 us
  blocking collectives: 18.4 us -> 42.9 us
  local copies, waits for them, and re-layouts: 30.5 us -> 52.4 us
    all_to_all x5 -> x2, waiting for transfers between devices: 46.2 us -> 14.8 us  [the longest x1 14.8 us: body(): dkv = lax.all_to_all(dkv, ROW, 0, 0, tiled=True)]
    pallas_call x8, Pallas kernels: 31.7 us -> 59.2 us  [call(): pl.pallas_call(kernel, out_shape=[s for _, s in outs], in_specs=[spec for...]
    all_to_all x1 -> x2, blocking collectives: 18.4 us -> 42.9 us  [the longest x1 22.3 us: body(): kw = lax.all_to_all(kw, ROW, 0, 0, tiled=True)]
    unnamed x50 -> x131, local copies, waits for them, and re-layouts: 23.7 us -> 46.4 us
    all_to_all x5 -> x2, starting transfers between devices: 33.1 us -> 12.4 us  [the longest x1 8.17 us: body(): map_grad = lax.all_to_all(map_grad, PLANE, 0, 0, tiled=True)]
    ppermute x0 -> x14, starting transfers between devices: none -> 18.4 us  [trade(): lax.ppermute(pieces[s], ROW, [(i, i ^ s) for i in range(count)])]
    all_to_all x1, waiting for transfers between devices: 16.8 us -> 0.01 us  [body(): state = lax.all_to_all(state, 'z', 0, 0, tiled=True)]
    ppermute x0 -> x14, waiting for transfers between devices: none -> 16.5 us  [trade(): lax.ppermute(pieces[s], ROW, [(i, i ^ s) for i in range(count)])]
  transfers between devices with their start and end apart: 7 -> 18, of which waited for: 7 -> 8; matrix products, arithmetic and copies ran while one was open for 3% -> 1% of each run, Pallas kernels for 12% -> 10%
where the time goes in v2:
time: 230 us; the launch traced here: 229 us
  Pallas kernels  59.2 us (26%)
  local copies, waits for them, and re-layouts  52.4 us (23%)
  blocking collectives  42.9 us (19%)
  starting transfers between devices  41.1 us (18%)
  waiting for transfers between devices  31.3 us (14%)
    pallas_call x8, Pallas kernels, call(): pl.pallas_call(kernel, out_shape=[s for _, s in outs], in_specs=[spec for...  59.2 us
    unnamed x131, local copies, waits for them, and re-layouts  46.4 us
    all_to_all x1, blocking collectives, body(): kw = lax.all_to_all(kw, ROW, 0, 0, tiled=True)  22.3 us
    all_to_all x1, blocking collectives, body(): maps = lax.all_to_all(maps, PLANE, 0, 0, tiled=True)  20.7 us
    ppermute x14, starting transfers between devices, trade(): lax.ppermute(pieces[s], ROW, [(i, i ^ s) for i in range(count)])  18.4 us
    ppermute x14, waiting for transfers between devices, trade(): lax.ppermute(pieces[s], ROW, [(i, i ^ s) for i in range(count)])  16.5 us
    all_to_all x1, waiting for transfers between devices, body(): dkv = lax.all_to_all(dkv, ROW, 0, 0, tiled=True)  14.8 us
    all_to_all x1, starting transfers between devices, body(): map_grad = lax.all_to_all(map_grad, PLANE, 0, 0, tiled=True)  8.17 us
  transfers between devices with their start and end apart: 18, of which 8 were waited for; matrix products, arithmetic and copies ran while one was open for 1% of the time, Pallas kernels for 10%

profile of v2, /device:TPU:1, one launch (start us, length us, event | category | flops | bytes accessed | tf_op | source)
XLA Modules:
  0.0 228.8 jit_solution(775647255869963452)
XLA Ops:
  1.5 20.7 %all_to_all.38 = bf16[32,8,128]{2,1,0:T(8,128)(2,1)S(1)} all-to-all(bf16[32,8,128]{2,1,0:T(8,128)(2,1)S(1)} %bitcast.17), channel_id=1, replica_groups=mesh['z'=8,'x'=4,'core'=2,'y'=4] {'z','y'}, dimensions={0} | all-to-all | bytes 131072 | tf_op jit(solution)/shard_map/all_to_all | solution.py:367
  22.2 1.0 copy-done.8
  23.2 1.0 copy-done.9
  24.9 22.3 %all_to_all.39.kw_ref = bf16[8,544,128]{2,1,0:T(8,128)(2,1)S(1)} all-to-all(bf16[8,544,128]{2,1,0:T(8,128)(2,1)S(1)} %shard_map.92), channel_id=1, replica_groups=mesh['z'=8,'x'=4,'core'=2,'y'=4] {'x','core'}, dimensions={0} | all-to-all | bytes 2228224 | tf_op jit(solution)/shard_map/all_to_all | solution.py:374
  48.4 5.3 %shard_map.93 = (bf16[8,256,128]{2,1,0:T(8,128)(2,1)S(1)}, bf16[8,160,128]{2,1,0:T(8,128)(2,1)}) custom-call(bf16[8,544,128]{2,1,0:T(8,128)(2,1)S(1)} %all_to_all.39.kw_ref, bf16[128,128]{1,0:T(8,128)(2,1)S(1)} %squeeze.8.map_ref), custom_call_target="tpu_custom_call" | custom-call | flops 500000000 | bytes 2000000 | tf_op jit(solution)/shard_map/pallas_call | solution.py:339
  53.7 3.4 %all-to-all-start.2 = ((bf16[8,160,128]{2,1,0:T(8,128)(2,1)}), bf16[8,160,128]{2,1,0:T(8,128)(2,1)S(1)}, u32[]{:S(2)}, u32[]{:S(2)}) async-start(bf16[8,160,128]{2,1,0:T(8,128)(2,1)} %get-tuple-element.39), calls=%async_computation.2 | async-start | bytes 655360 | tf_op jit(solution)/shard_map/all_to_all | solution.py:389
  57.2 1.5 shard_map.94
  60.4 1.4 collective-permute-start.2
  62.4 2.6 %collective-permute-start.4 = (bf16[2,256,128]{2,1,0:T(8,128)(2,1)S(1)}, bf16[2,256,128]{2,1,0:T(8,128)(2,1)S(1)}, u32[]{:S(2)}, u32[]{:S(2)}) collective-permute-start(bf16[2,256,128]{2,1,0:T(8,128)(2,1)S(1)} %get-tuple-element.45), channel_id=1, source_target_pairs={{0,20},{4,16},{8,28},{12,24},{16,4},{20,0},{24,12},{28,8},{1,21},{... | collective-permute-start | bytes 393224 | tf_op jit(solution)/shard_map/ppermute | solution.py:353
  67.3 2.0 collective-permute-start.6
  69.3 1.7 squeeze.9.map_ref
  72.2 2.2 collective-permute-done.4.rest_5_
  75.1 2.3 %collective-permute-done.5.rest_6_ = bf16[2,256,128]{2,1,0:T(8,128)(2,1)S(1)} collective-permute-done((bf16[2,256,128]{2,1,0:T(8,128)(2,1)S(1)}, bf16[2,256,128]{2,1,0:T(8,128)(2,1)S(1)}, u32[]{:S(2)}, u32[]{:S(2)}) %collective-permute-start.5) | collective-permute-done | bytes 131104 | tf_op jit(solution)/shard_map/ppermute | solution.py:353
  78.1 2.2 collective-permute-done.6.rest_7_
  85.3 0.9 copy-done.34
  88.9 18.4 %shard_map.95 = (bf16[8,256,128]{2,1,0:T(8,128)(2,1)S(1)}, bf16[8,256,128]{2,1,0:T(8,128)(2,1)S(1)}, bf16[8,256,256]{2,1,0:T(8,128)(2,1)S(1)}, bf16[8,256,256]{2...) custom-call(s32[2]{0:T(128)S(1)} %pad_add_fusion.place_ref, ...), custom_call_target="tpu_custom_call" | custom-call | flops 2000000000 | bytes 8000000 | tf_op jit(solution)/shard_map/pallas_call | solution.py:339
  107.3 0.9 copy-done.4
  108.2 1.0 copy-done.6
  112.3 6.8 %all-to-all-start.3 = ((bf16[8,160,128]{2,1,0:T(8,128)(2,1)}), bf16[8,160,128]{2,1,0:T(8,128)(2,1)S(1)}, u32[]{:S(2)}, u32[]{:S(2)}) async-start(bf16[8,160,128]{2,1,0:T(8,128)(2,1)} %copy-done.16), calls=%async_computation.3 | async-start | bytes 655360 | tf_op jit(solution)/shard_map/all_to_all | solution.py:399
  119.1 1.2 copy-done.5
  120.4 1.2 copy-done.7
  121.6 1.0 copy-done.11
  122.6 1.0 copy-done.13
  123.7 1.0 copy-done.15
  126.4 0.9 copy-done.26
  127.3 0.9 copy-done.29
  132.7 19.2 %shard_map.96 = (bf16[2,256,128]{2,1,0:T(8,128)(2,1)S(1)}, bf16[2,256,128]{2,1,0:T(8,128)(2,1)S(1)}, bf16[2,256,128]{2,1,0:T(8,128)(2,1)S(1)}, bf16[2,256,128]{2...) custom-call(s32[2]{0:T(128)S(1)} %pad_add_fusion.place_ref, ...), custom_call_target="tpu_custom_call" | custom-call | flops 1500000000 | bytes 6000000 | tf_op jit(solution)/shard_map/pallas_call | solution.py:339
  151.9 0.9 copy-done
  152.9 1.0 copy-done.2
  159.7 1.2 copy-done.1
  160.9 1.2 copy-done.3
  163.8 11.6 %shard_map.98 = bf16[8,576,128]{2,1,0:T(8,128)(2,1)} custom-call(s32[2]{0:T(128)S(1)} %pad_add_fusion.place_ref, bf16[8,544,128]{2,1,0:T(8,128)(2,1)S(1)} %all_to_all.39.kw_ref, bf16[8,256,128]{2,1,0:T(8,128)(2,1)S(1)} %get-tuple-element.38.fk_ref, f32[8,256,128]{2,1,0:T(8,128)S(1)} %copy-done.1, f32[8,256,128]{2,1,0:T(8,128)S(1)} %copy-done.3, ...), custom_call_target="tpu_custom_call" | custom-call | flops 1500000000 | bytes 6000000 | tf_op jit(solution)/shard_map/pallas_call | solution.py:339
  175.4 4.3 %all-to-all-start.4 = ((bf16[8,576,128]{2,1,0:T(8,128)(2,1)}), bf16[8,576,128]{2,1,0:T(8,128)(2,1)S(1)}, u32[]{:S(2)}, u32[]{:S(2)}) async-start(bf16[8,576,128]{2,1,0:T(8,128)(2,1)} %shard_map.98), calls=%async_computation.4 | async-start | bytes 2359296 | tf_op jit(solution)/shard_map/all_to_all | solution.py:418
  179.9 1.6 collective-permute-start.8
  181.4 14.8 %all-to-all-done.4.in_ref = bf16[8,576,128]{2,1,0:T(8,128)(2,1)S(1)} async-done(((bf16[8,576,128]{2,1,0:T(8,128)(2,1)}), bf16[8,576,128]{2,1,0:T(8,128)(2,1)S(1)}, u32[]{:S(2)}, u32[]{:S(2)}) %all-to-all-start.4) | async-done | bytes 1179680 | tf_op jit(solution)/shard_map/all_to_all | solution.py:418
  197.4 1.1 all_to_all.30
  198.5 8.2 %all-to-all-start.5 = ((f32[32,8,128]{2,1,0:T(8,128)}), f32[32,8,128]{2,1,0:T(8,128)S(1)}, u32[]{:S(2)}, u32[]{:S(2)}) async-start(f32[32,8,128]{2,1,0:T(8,128)} %all_to_all.30), calls=%async_computation.5 | async-start | bytes 262144 | tf_op jit(solution)/shard_map/all_to_all | solution.py:426
  206.7 1.9 collective-permute-start.9
  208.6 1.8 collective-permute-start.10
  210.4 1.3 collective-permute-start.11
  211.7 0.9 collective-permute-start.12
  212.6 2.2 collective-permute-start.13
  214.8 1.7 collective-permute-done.10.rest_4_
  216.5 2.4 %collective-permute-done.11.rest_5_ = bf16[2,256,128]{2,1,0:T(8,128)(2,1)S(1)} collective-permute-done((bf16[2,256,128]{2,1,0:T(8,128)(2,1)S(1)}, bf16[2,256,128]{2,1,0:T(8,128)(2,1)S(1)}, u32[]{:S(2)}, u32[]{:S(2)}) %collective-permute-start.11) | collective-permute-done | bytes 131104 | tf_op jit(solution)/shard_map/ppermute | solution.py:353
  218.9 2.9 %collective-permute-done.12.rest_6_ = bf16[2,256,128]{2,1,0:T(8,128)(2,1)S(1)} collective-permute-done((bf16[2,256,128]{2,1,0:T(8,128)(2,1)S(1)}, bf16[2,256,128]{2,1,0:T(8,128)(2,1)S(1)}, u32[]{:S(2)}, u32[]{:S(2)}) %collective-permute-start.12) | collective-permute-done | bytes 131104 | tf_op jit(solution)/shard_map/ppermute | solution.py:353
  221.8 2.8 %collective-permute-done.13.rest_7_ = bf16[2,256,128]{2,1,0:T(8,128)(2,1)S(1)} collective-permute-done((bf16[2,256,128]{2,1,0:T(8,128)(2,1)S(1)}, bf16[2,256,128]{2,1,0:T(8,128)(2,1)S(1)}, u32[]{:S(2)}, u32[]{:S(2)}) %collective-permute-start.13) | collective-permute-done | bytes 131104 | tf_op jit(solution)/shard_map/ppermute | solution.py:353
  224.7 1.6 shard_map.97
  226.3 1.1 shard_map.99
  (148 shorter events, 37.2 us)
Async XLA Ops:
  22.2 1.0 copy-start.8
  23.2 1.0 copy-start.9
  48.4 5.3 %copy-start.17 = (bf16[128,128]{1,0:T(8,128)(2,1)}, bf16[128,128]{1,0:T(8,128)(2,1)S(1)}, u32[]{:S(2)}) copy-start(bf16[128,128]{1,0:T(8,128)(2,1)S(1)} %squeeze.8.map_ref) | copy-start | bytes 98308
  48.4 8.9 %copy-start.47 = (bf16[256,1024]{1,0:T(8,128)(2,1)S(1)}, bf16[256,1024]{1,0:T(8,128)(2,1)}, u32[]{:S(2)}) copy-start(bf16[256,1024]{1,0:T(8,128)(2,1)} %first_ref.1) | copy-start | bytes 1572868
  48.4 8.8 %copy-start.48 = (bf16[256,1024]{1,0:T(8,128)(2,1)S(1)}, bf16[256,1024]{1,0:T(8,128)(2,1)}, u32[]{:S(2)}) copy-start(bf16[256,1024]{1,0:T(8,128)(2,1)} %second_ref.1) | copy-start | bytes 1572868
  53.7 27.2 %all-to-all-start.2 = ((bf16[8,160,128]{2,1,0:T(8,128)(2,1)}), bf16[8,160,128]{2,1,0:T(8,128)(2,1)S(1)}, u32[]{:S(2)}, u32[]{:S(2)}) async-start(bf16[8,160,128]{2,1,0:T(8,128)(2,1)} %get-tuple-element.39), calls=%async_computation.2 | async-start | bytes 655360 | tf_op jit(solution)/shard_map/all_to_all | solution.py:389
  59.4 5.7 %collective-permute-start = (bf16[2,256,128]{2,1,0:T(8,128)(2,1)S(1)}, bf16[2,256,128]{2,1,0:T(8,128)(2,1)S(1)}, u32[]{:S(2)}, u32[]{:S(2)}) collective-permute-start(bf16[2,256,128]{2,1,0:T(8,128)(2,1)S(1)} %get-tuple-element.41), channel_id=1, source_target_pairs={{0,4},{4,0},{8,12},{12,8},{16,20},{20,16},{24,28},{28,24},{1,5},{5... | collective-permute-start | bytes 393224 | tf_op jit(solution)/shard_map/ppermute | solution.py:353
  60.1 6.5 %collective-permute-start.1 = (bf16[2,256,128]{2,1,0:T(8,128)(2,1)S(1)}, bf16[2,256,128]{2,1,0:T(8,128)(2,1)S(1)}, u32[]{:S(2)}, u32[]{:S(2)}) collective-permute-start(bf16[2,256,128]{2,1,0:T(8,128)(2,1)S(1)} %get-tuple-element.42), channel_id=1, source_target_pairs={{0,8},{4,12},{8,0},{12,4},{16,24},{20,28},{24,16},{28,20},{1,9},{5... | collective-permute-start | bytes 393224 | tf_op jit(solution)/shard_map/ppermute | solution.py:353
  60.4 10.5 %collective-permute-start.2 = (bf16[2,256,128]{2,1,0:T(8,128)(2,1)}, bf16[2,256,128]{2,1,0:T(8,128)(2,1)S(1)}, u32[]{:S(2)}, u32[]{:S(2)}) collective-permute-start(bf16[2,256,128]{2,1,0:T(8,128)(2,1)} %get-tuple-element.43), channel_id=1, source_target_pairs={{0,12},{4,8},{8,4},{12,0},{16,28},{20,24},{24,20},{28,16},{1,13},{... | collective-permute-start | bytes 393224 | tf_op jit(solution)/shard_map/ppermute | solution.py:353
  61.7 9.9 %collective-permute-start.3 = (bf16[2,256,128]{2,1,0:T(8,128)(2,1)S(1)}, bf16[2,256,128]{2,1,0:T(8,128)(2,1)S(1)}, u32[]{:S(2)}, u32[]{:S(2)}) collective-permute-start(bf16[2,256,128]{2,1,0:T(8,128)(2,1)S(1)} %get-tuple-element.44), channel_id=1, source_target_pairs={{0,16},{4,20},{8,24},{12,28},{16,0},{20,4},{24,8},{28,12},{1,17},{... | collective-permute-start | bytes 393224 | tf_op jit(solution)/shard_map/ppermute | solution.py:353
  62.4 12.0 %collective-permute-start.4 = (bf16[2,256,128]{2,1,0:T(8,128)(2,1)S(1)}, bf16[2,256,128]{2,1,0:T(8,128)(2,1)S(1)}, u32[]{:S(2)}, u32[]{:S(2)}) collective-permute-start(bf16[2,256,128]{2,1,0:T(8,128)(2,1)S(1)} %get-tuple-element.45), channel_id=1, source_target_pairs={{0,20},{4,16},{8,28},{12,24},{16,4},{20,0},{24,12},{28,8},{1,21},{... | collective-permute-start | bytes 393224 | tf_op jit(solution)/shard_map/ppermute | solution.py:353
  65.8 11.7 %collective-permute-start.5 = (bf16[2,256,128]{2,1,0:T(8,128)(2,1)S(1)}, bf16[2,256,128]{2,1,0:T(8,128)(2,1)S(1)}, u32[]{:S(2)}, u32[]{:S(2)}) collective-permute-start(bf16[2,256,128]{2,1,0:T(8,128)(2,1)S(1)} %get-tuple-element.46), channel_id=1, source_target_pairs={{0,24},{4,28},{8,16},{12,20},{16,8},{20,12},{24,0},{28,4},{1,25},{... | collective-permute-start | bytes 393224 | tf_op jit(solution)/shard_map/ppermute | solution.py:353
  67.3 12.9 %collective-permute-start.6 = (bf16[2,256,128]{2,1,0:T(8,128)(2,1)S(1)}, bf16[2,256,128]{2,1,0:T(8,128)(2,1)S(1)}, u32[]{:S(2)}, u32[]{:S(2)}) collective-permute-start(bf16[2,256,128]{2,1,0:T(8,128)(2,1)S(1)} %get-tuple-element.47), channel_id=1, source_target_pairs={{0,28},{4,24},{8,20},{12,16},{16,12},{20,8},{24,4},{28,0},{1,29},{... | collective-permute-start | bytes 393224 | tf_op jit(solution)/shard_map/ppermute | solution.py:353
  83.5 0.9 copy-start.28
  84.4 0.9 copy-start.31
  85.3 0.9 copy-start.34
  107.2 1.0 copy-start.4
  108.2 1.0 copy-start.6
  112.3 47.4 %all-to-all-start.3 = ((bf16[8,160,128]{2,1,0:T(8,128)(2,1)}), bf16[8,160,128]{2,1,0:T(8,128)(2,1)S(1)}, u32[]{:S(2)}, u32[]{:S(2)}) async-start(bf16[8,160,128]{2,1,0:T(8,128)(2,1)} %copy-done.16), calls=%async_computation.3 | async-start | bytes 655360 | tf_op jit(solution)/shard_map/all_to_all | solution.py:399
  119.1 1.2 copy-start.5
  120.4 1.2 copy-start.7
  121.6 1.0 copy-start.11
  122.6 1.0 copy-start.13
  123.7 1.0 copy-start.15
  125.5 0.9 copy-start.23
  126.4 0.9 copy-start.26
  127.3 0.9 copy-start.29
  151.9 1.0 copy-start
  152.9 1.0 copy-start.2
  159.7 1.2 copy-start.1
  160.9 1.2 copy-start.3
  175.4 4.3 %copy-start.64 = (bf16[2,256,128]{2,1,0:T(8,128)(2,1)S(1)}, bf16[2,256,128]{2,1,0:T(8,128)(2,1)}, u32[]{:S(2)}) copy-start(bf16[2,256,128]{2,1,0:T(8,128)(2,1)} %copy-done.63) | copy-start | bytes 393220
  175.4 4.5 %copy-start.62 = (bf16[2,256,128]{2,1,0:T(8,128)(2,1)S(1)}, bf16[2,256,128]{2,1,0:T(8,128)(2,1)}, u32[]{:S(2)}) copy-start(bf16[2,256,128]{2,1,0:T(8,128)(2,1)} %copy-done.61) | copy-start | bytes 393220
  175.4 20.8 %all-to-all-start.4 = ((bf16[8,576,128]{2,1,0:T(8,128)(2,1)}), bf16[8,576,128]{2,1,0:T(8,128)(2,1)S(1)}, u32[]{:S(2)}, u32[]{:S(2)}) async-start(bf16[8,576,128]{2,1,0:T(8,128)(2,1)} %shard_map.98), calls=%async_computation.4 | async-start | bytes 2359296 | tf_op jit(solution)/shard_map/all_to_all | solution.py:418
  179.7 32.0 %collective-permute-start.7 = (bf16[2,256,128]{2,1,0:T(8,128)(2,1)S(1)}, bf16[2,256,128]{2,1,0:T(8,128)(2,1)S(1)}, u32[]{:S(2)}, u32[]{:S(2)}) collective-permute-start(bf16[2,256,128]{2,1,0:T(8,128)(2,1)S(1)} %copy-done.64), channel_id=1, source_target_pairs={{0,4},{4,0},{8,12},{12,8},{16,20},{20,16},{24,28},{28,24},{1,5},{5... | collective-permute-start | bytes 393224 | tf_op jit(solution)/shard_map/ppermute | solution.py:353
  179.9 32.7 %collective-permute-start.8 = (bf16[2,256,128]{2,1,0:T(8,128)(2,1)S(1)}, bf16[2,256,128]{2,1,0:T(8,128)(2,1)S(1)}, u32[]{:S(2)}, u32[]{:S(2)}) collective-permute-start(bf16[2,256,128]{2,1,0:T(8,128)(2,1)S(1)} %copy-done.62), channel_id=1, source_target_pairs={{0,8},{4,12},{8,0},{12,4},{16,24},{20,28},{24,16},{28,20},{1,9},{5... | collective-permute-start | bytes 393224 | tf_op jit(solution)/shard_map/ppermute | solution.py:353
  197.0 9.8 %copy-start.60 = (bf16[2,256,128]{2,1,0:T(8,128)(2,1)S(1)}, bf16[2,256,128]{2,1,0:T(8,128)(2,1)}, u32[]{:S(2)}) copy-start(bf16[2,256,128]{2,1,0:T(8,128)(2,1)} %copy-done.59) | copy-start | bytes 393220
  197.0 11.6 %copy-start.58 = (bf16[2,256,128]{2,1,0:T(8,128)(2,1)S(1)}, bf16[2,256,128]{2,1,0:T(8,128)(2,1)}, u32[]{:S(2)}) copy-start(bf16[2,256,128]{2,1,0:T(8,128)(2,1)} %copy-done.57) | copy-start | bytes 393220
  197.0 13.4 %copy-start.56 = (bf16[2,256,128]{2,1,0:T(8,128)(2,1)S(1)}, bf16[2,256,128]{2,1,0:T(8,128)(2,1)}, u32[]{:S(2)}) copy-start(bf16[2,256,128]{2,1,0:T(8,128)(2,1)} %copy-done.55) | copy-start | bytes 393220
  197.0 14.7 %copy-start.54 = (bf16[2,256,128]{2,1,0:T(8,128)(2,1)S(1)}, bf16[2,256,128]{2,1,0:T(8,128)(2,1)}, u32[]{:S(2)}) copy-start(bf16[2,256,128]{2,1,0:T(8,128)(2,1)} %copy-done.53) | copy-start | bytes 393220
  197.0 15.6 %copy-start.52 = (bf16[2,256,128]{2,1,0:T(8,128)(2,1)S(1)}, bf16[2,256,128]{2,1,0:T(8,128)(2,1)}, u32[]{:S(2)}) copy-start(bf16[2,256,128]{2,1,0:T(8,128)(2,1)} %copy-done.51) | copy-start | bytes 393220
  197.0 27.6 %copy-start.50 = (bf16[2,256,128]{2,1,0:T(8,128)(2,1)S(1)}, bf16[2,256,128]{2,1,0:T(8,128)(2,1)}, u32[]{:S(2)}) copy-start(bf16[2,256,128]{2,1,0:T(8,128)(2,1)} %copy-done.49) | copy-start | bytes 393220
  198.5 28.9 %all-to-all-start.5 = ((f32[32,8,128]{2,1,0:T(8,128)}), f32[32,8,128]{2,1,0:T(8,128)S(1)}, u32[]{:S(2)}, u32[]{:S(2)}) async-start(f32[32,8,128]{2,1,0:T(8,128)} %all_to_all.30), calls=%async_computation.5 | async-start | bytes 262144 | tf_op jit(solution)/shard_map/all_to_all | solution.py:426
  206.7 8.1 %collective-permute-start.9 = (bf16[2,256,128]{2,1,0:T(8,128)(2,1)S(1)}, bf16[2,256,128]{2,1,0:T(8,128)(2,1)S(1)}, u32[]{:S(2)}, u32[]{:S(2)}) collective-permute-start(bf16[2,256,128]{2,1,0:T(8,128)(2,1)S(1)} %copy-done.60), channel_id=1, source_target_pairs={{0,12},{4,8},{8,4},{12,0},{16,28},{20,24},{24,20},{28,16},{1,13},{... | collective-permute-start | bytes 393224 | tf_op jit(solution)/shard_map/ppermute | solution.py:353
  208.6 7.9 %collective-permute-start.10 = (bf16[2,256,128]{2,1,0:T(8,128)(2,1)S(1)}, bf16[2,256,128]{2,1,0:T(8,128)(2,1)S(1)}, u32[]{:S(2)}, u32[]{:S(2)}) collective-permute-start(bf16[2,256,128]{2,1,0:T(8,128)(2,1)S(1)} %copy-done.58), channel_id=1, source_target_pairs={{0,16},{4,20},{8,24},{12,28},{16,0},{20,4},{24,8},{28,12},{1,17},{... | collective-permute-start | bytes 393224 | tf_op jit(solution)/shard_map/ppermute | solution.py:353
  210.4 8.6 %collective-permute-start.11 = (bf16[2,256,128]{2,1,0:T(8,128)(2,1)S(1)}, bf16[2,256,128]{2,1,0:T(8,128)(2,1)S(1)}, u32[]{:S(2)}, u32[]{:S(2)}) collective-permute-start(bf16[2,256,128]{2,1,0:T(8,128)(2,1)S(1)} %copy-done.56), channel_id=1, source_target_pairs={{0,20},{4,16},{8,28},{12,24},{16,4},{20,0},{24,12},{28,8},{1,21},{... | collective-permute-start | bytes 393224 | tf_op jit(solution)/shard_map/ppermute | solution.py:353
  211.7 10.2 %collective-permute-start.12 = (bf16[2,256,128]{2,1,0:T(8,128)(2,1)S(1)}, bf16[2,256,128]{2,1,0:T(8,128)(2,1)S(1)}, u32[]{:S(2)}, u32[]{:S(2)}) collective-permute-start(bf16[2,256,128]{2,1,0:T(8,128)(2,1)S(1)} %copy-done.54), channel_id=1, source_target_pairs={{0,24},{4,28},{8,16},{12,20},{16,8},{20,12},{24,0},{28,4},{1,25},{... | collective-permute-start | bytes 393224 | tf_op jit(solution)/shard_map/ppermute | solution.py:353
  212.6 12.1 %collective-permute-start.13 = (bf16[2,256,128]{2,1,0:T(8,128)(2,1)S(1)}, bf16[2,256,128]{2,1,0:T(8,128)(2,1)S(1)}, u32[]{:S(2)}, u32[]{:S(2)}) collective-permute-start(bf16[2,256,128]{2,1,0:T(8,128)(2,1)S(1)} %copy-done.52), channel_id=1, source_target_pairs={{0,28},{4,24},{8,20},{12,16},{16,12},{20,8},{24,4},{28,0},{1,29},{... | collective-permute-start | bytes 393224 | tf_op jit(solution)/shard_map/ppermute | solution.py:353
  (35 other events, 26.3 us)

commit v3 on v1

v3 whole, which is shorter than its diff:
```python
import jax
import jax.numpy as jnp
from jax import lax
from jax.experimental import pallas as pl
from jax.experimental.pallas import tpu as pltpu
from jax.sharding import Mesh
from jax.sharding import PartitionSpec as P

HEAD_DIM = 128
BLOCK = 256
F32 = jnp.float32
BF16 = jnp.bfloat16
ROW = ("x", "core")
CTX = ("z", "x", "core")
FINE = ("z", "x", "core", "y")
ANY = pl.BlockSpec(memory_space=pl.ANY)
VMEM = pl.BlockSpec(memory_space=pltpu.VMEM)
SMEM = pl.BlockSpec(memory_space=pltpu.SMEM)
DMA = pltpu.SemaphoreType.DMA
PART = BF16
STATE_ROWS = HEAD_DIM + 32


def mm(a, b):
    return lax.dot_general(a, b, (((1,), (0,)), ((), ())), preferred_element_type=F32)


def mm_nt(a, b):
    return lax.dot_general(a, b, (((1,), (1,)), ((), ())), preferred_element_type=F32)


def mm_tn(a, b):
    return lax.dot_general(a, b, (((0,), (0,)), ((), ())), preferred_element_type=F32)


def feature(pre):
    return jnp.where(pre > 0, pre + 1.0, jnp.exp(jnp.minimum(pre, 0.0)))


def halves(value):
    high = value.astype(BF16)
    return high, (value - high.astype(F32)).astype(BF16)


def causal_mask():
    rows = lax.broadcasted_iota(jnp.int32, (BLOCK, BLOCK), 0)
    cols = lax.broadcasted_iota(jnp.int32, (BLOCK, BLOCK), 1)
    return rows >= cols


def lanes(rows):
    return lax.broadcasted_iota(jnp.int32, (rows, HEAD_DIM), 1)


def row_slope(grad, attended):
    return jnp.broadcast_to(-jnp.sum(grad * attended, axis=1, keepdims=True), grad.shape)


def norm_rows(column):
    rows = column.T[:16]
    index = lax.broadcasted_iota(jnp.int32, (16, HEAD_DIM), 0)
    high = rows.astype(BF16).astype(F32)
    mid = (rows - high).astype(BF16).astype(F32)
    low = rows - high - mid
    return jnp.where(
        index == 0, high, jnp.where(index == 1, mid, jnp.where(index == 2, low, 0.0))
    ).astype(BF16)


def pack(place_ref, *refs):
    ins, outs, (held, in_sem, out_sem) = refs[:4], refs[4:-3], refs[-3:]
    loads, stores = [], []
    for s in range(len(outs)):
        column = pl.ds(pl.multiple_of((place_ref[1] ^ s) * HEAD_DIM, HEAD_DIM), HEAD_DIM)
        for n, ref in enumerate(ins):
            loads.append(pltpu.make_async_copy(ref.at[:, column], held.at[s, n], in_sem.at[s, n]))
        stores.append(pltpu.make_async_copy(held.at[s], outs[s], out_sem.at[s]))
    for load in loads:
        load.start()
    for s, store in enumerate(stores):
        for load in loads[4 * s:4 * s + 4]:
            load.wait()
        store.start()
    for store in stores:
        store.wait()


def unpack(place_ref, *refs):
    pieces, outs, sem = refs[:-3], refs[-3:-1], refs[-1]
    copies = []
    for s, piece in enumerate(pieces):
        column = pl.ds(pl.multiple_of((place_ref[1] ^ s) * HEAD_DIM, HEAD_DIM), HEAD_DIM)
        for n, ref in enumerate(outs):
            copies.append(pltpu.make_async_copy(piece.at[n], ref.at[:, column], sem.at[s, n]))
    for copy in copies:
        copy.start()
    for copy in copies:
        copy.wait()


def key_state(place_ref, map_ref, *refs):
    pieces, (kv_ref, qd_ref, out_ref) = refs[:-3], refs[-3:]
    blocks = len(pieces)
    for s, piece in enumerate(pieces):
        kv_ref[place_ref[1] ^ s] = piece[:2]
        qd_ref[place_ref[1] ^ s] = piece[2:]
    ones = jnp.ones((BLOCK, HEAD_DIM), BF16)
    total = jnp.zeros((HEAD_DIM, 2 * HEAD_DIM), F32)
    mean = jnp.zeros((1, HEAD_DIM), F32)
    for b in range(blocks):
        feat = feature(mm(kv_ref[b, 0], map_ref[1])).astype(BF16)
        value = kv_ref[b, 1]
        mean = mean + jnp.sum(value.astype(F32), axis=0, keepdims=True)
        total = total + mm_tn(feat, jnp.concatenate([value, ones], axis=1))
    centre = (mean * (1.0 / (blocks * BLOCK))).astype(BF16)
    column = total[:, HEAD_DIM:]
    state = (total[:, :HEAD_DIM] - column * centre.astype(F32)).astype(BF16)
    norms = norm_rows(column)
    for z in range(out_ref.shape[0]):
        out_ref[z, :HEAD_DIM] = state
        out_ref[z, HEAD_DIM:HEAD_DIM + 16] = norms
        out_ref[z, HEAD_DIM + 16:] = jnp.broadcast_to(centre, (16, HEAD_DIM))


def prior_of(place, sums_ref):
    prior = jnp.zeros((HEAD_DIM, HEAD_DIM), F32)
    norms, centres = [], []
    for z in range(sums_ref.shape[0]):
        part = jnp.where(z < place, sums_ref[z].astype(F32), 0.0)
        prior = prior + part[:HEAD_DIM]
        norms.append(part[HEAD_DIM:HEAD_DIM + 16].astype(BF16))
        centres.append(sums_ref[z, HEAD_DIM + 16:])
    centres = jnp.concatenate(centres, axis=0)
    centres = jnp.concatenate([centres, jnp.ones_like(centres)], axis=1)
    prior = jnp.concatenate([prior, jnp.zeros_like(prior)], axis=1)
    return prior + mm_tn(jnp.concatenate(norms, axis=0), centres)


def forward_block(kv_ref, qd_ref, b, map_ref, prior, causal):
    feat_k = feature(mm(kv_ref[b, 0], map_ref[1])).astype(BF16)
    feat_q = feature(mm(qd_ref[b, 0], map_ref[0])).astype(BF16)
    high, low = halves(prior)
    scores = jnp.where(causal, mm_nt(feat_q, feat_k), 0.0)
    weight = scores.astype(BF16)
    both = mm(jnp.concatenate([feat_q, feat_q], axis=1), jnp.concatenate([high, low], axis=0))
    inverse = 1.0 / (both[:, HEAD_DIM:] + jnp.sum(scores, axis=1, keepdims=True))
    attended = (both[:, :HEAD_DIM] + mm(weight, kv_ref[b, 1])) * inverse
    exact = qd_ref[b, 1].astype(F32) * inverse
    grad = exact.astype(BF16)
    across = halves(row_slope(grad.astype(F32), attended))
    return feat_k, feat_q, high, low, weight, attended, exact, grad, across


def with_ones(value):
    return jnp.concatenate([value, jnp.ones((BLOCK, HEAD_DIM), BF16)], axis=1)


def forward(place_ref, kv_ref, qd_ref, map_ref, sums_ref, out_ref):
    blocks = kv_ref.shape[0]
    prior = prior_of(place_ref[0], sums_ref)
    causal = causal_mask()
    lane = lanes(BLOCK)
    total = jnp.zeros((HEAD_DIM, 2 * HEAD_DIM), F32)
    centre = jnp.zeros((1, HEAD_DIM), F32)
    for b in range(blocks):
        feat_k, feat_q, _, _, _, _, _, grad, (across, rest) = forward_block(kv_ref, qd_ref, b, map_ref, prior, causal)
        pair = jnp.where(lane == 0, across, jnp.where(lane == 1, rest, jnp.zeros_like(rest)))
        total = total + mm_tn(feat_q, jnp.concatenate([grad, pair], axis=1))
        prior = prior + mm_tn(feat_k, with_ones(kv_ref[b, 1]))
        centre = centre + jnp.sum(kv_ref[b, 1].astype(F32), axis=0, keepdims=True)
    sent = total[:, :HEAD_DIM].astype(BF16)
    centre = (centre * (1.0 / (blocks * BLOCK))).astype(BF16).astype(F32)
    rest = jnp.sum((total[:, :HEAD_DIM] - sent.astype(F32)) * centre, axis=1, keepdims=True)
    column = jnp.sum(total[:, HEAD_DIM:], axis=1, keepdims=True) + rest
    norms = norm_rows(jnp.broadcast_to(column, (HEAD_DIM, HEAD_DIM)))
    for z in range(out_ref.shape[0]):
        out_ref[z, :HEAD_DIM] = sent
        out_ref[z, HEAD_DIM:HEAD_DIM + 16] = norms
        out_ref[z, HEAD_DIM + 16:] = jnp.zeros((16, HEAD_DIM), BF16)


def inner(place_ref, kv_ref, qd_ref, map_ref, sums_ref, *refs):
    pieces, (part_ref, map_grad_ref, aq, fqs, fks, grads, weights, dscores, adjoints) = refs[:-9], refs[-9:]
    blocks = kv_ref.shape[0]
    prior = prior_of(place_ref[0], sums_ref)
    causal = causal_mask()
    lane = lanes(BLOCK)
    few = lanes(HEAD_DIM) < 2
    unit = jnp.where((lane == 2) | (lane == 3), 1.0, 0.0).astype(BF16)
    none = jnp.zeros((HEAD_DIM, HEAD_DIM), BF16)
    map_grad = jnp.zeros((HEAD_DIM, HEAD_DIM), F32)
    for b in range(blocks):
        feat_k, feat_q, high, low, weight, attended, exact, half, (across, rest) = forward_block(
            kv_ref, qd_ref, b, map_ref, prior, causal)
        value = kv_ref[b, 1]
        within, within_rest = halves(row_slope(exact, attended))
        pair = jnp.where(lane == 0, across, jnp.where(lane == 1, rest, jnp.zeros_like(rest)))
        pair = jnp.where(lane == 2, within, jnp.where(lane == 3, within_rest, pair))
        grad = jnp.concatenate([half, pair], axis=1)
        fks[b] = feat_k
        fqs[b] = feat_q
        grads[b] = grad
        weights[b] = weight
        high = jnp.concatenate([high[:, :HEAD_DIM], jnp.where(few, high[:, HEAD_DIM:], none)], axis=1)
        low = jnp.concatenate([low[:, :HEAD_DIM], jnp.where(few, low[:, HEAD_DIM:], none)], axis=1)
        dscore = mm_nt(grad, jnp.concatenate([value, unit], axis=1))
        dscore = jnp.where(causal, dscore, 0.0).astype(BF16)
        dscores[b] = dscore
        d_feat = mm_nt(grad, high) + mm_nt(grad, low) + mm(dscore, feat_k)
        dpre = (d_feat * jnp.minimum(feat_q.astype(F32), 1.0)).astype(BF16)
        aq[b, 0] = attended.astype(BF16)
        aq[b, 1] = mm_nt(dpre, map_ref[0]).astype(BF16)
        map_grad = map_grad + mm_tn(qd_ref[b, 0], dpre)
        adjoints[b] = mm_tn(feat_q, grad)
        prior = prior + mm_tn(feat_k, with_ones(value))
    map_grad_ref[...] = map_grad
    for s, piece in enumerate(pieces):
        piece[...] = aq[place_ref[1] ^ s]
    pair = jnp.where(lane < 2, 1.0, 0.0).astype(BF16)
    after = jnp.zeros((HEAD_DIM, 2 * HEAD_DIM), F32)
    for b in range(blocks - 1, -1, -1):
        high, low = halves(after)
        wide = jnp.concatenate([kv_ref[b, 1], pair], axis=1)
        feat_k = fks[b]
        part_ref[b, 0] = (mm_nt(wide, high) + mm_nt(wide, low) + mm_tn(dscores[b], fqs[b])).astype(PART)
        stacked = jnp.concatenate([high[:, :HEAD_DIM], low[:, :HEAD_DIM]], axis=0)
        inside = mm_tn(weights[b], grads[b, :, :HEAD_DIM])
        part_ref[b, 1] = (mm(jnp.concatenate([feat_k, feat_k], axis=1), stacked) + inside).astype(PART)
        after = after + adjoints[b]


def outer(place_ref, kv_ref, map_ref, sums_ref, part_ref, out_ref, *pieces):
    place = place_ref[0]
    after = jnp.zeros((HEAD_DIM, HEAD_DIM), F32)
    norms = []
    for z in range(sums_ref.shape[0]):
        part = jnp.where(z > place, sums_ref[z].astype(F32), 0.0)
        after = after + part[:HEAD_DIM]
        norms.append(part[HEAD_DIM:HEAD_DIM + 16].astype(BF16))
    first = jnp.where(lanes(HEAD_DIM) == 0, 1.0, 0.0).astype(BF16)
    after = jnp.concatenate([after, mm_tn(jnp.concatenate(norms, axis=0), first)], axis=1)
    high, low = halves(after)
    stacked = jnp.concatenate([high[:, :HEAD_DIM], low[:, :HEAD_DIM]], axis=0)
    pair = jnp.where(lanes(BLOCK) == 0, 1.0, 0.0).astype(BF16)
    map_grad = jnp.zeros((HEAD_DIM, HEAD_DIM), F32)
    for s, piece in enumerate(pieces):
        b = place_ref[1] ^ s
        feat_k = feature(mm(kv_ref[b, 0], map_ref[1])).astype(BF16)
        wide = jnp.concatenate([kv_ref[b, 1], pair], axis=1)
        d_feat = mm_nt(wide, high) + mm_nt(wide, low) + part_ref[b, 0].astype(F32)
        dpre = (d_feat * jnp.minimum(feat_k.astype(F32), 1.0)).astype(BF16)
        d_value = mm(jnp.concatenate([feat_k, feat_k], axis=1), stacked) + part_ref[b, 1].astype(F32)
        piece[0] = mm_nt(dpre, map_ref[1]).astype(BF16)
        piece[1] = d_value.astype(BF16)
        map_grad = map_grad + mm_tn(kv_ref[b, 0], dpre)
    out_ref[...] = map_grad


def shape(*dims, dtype=BF16):
    return jax.ShapeDtypeStruct(dims, dtype)


def call(kernel, outs, operands, scratch=(), cycles=1, limit=32):
    return pl.pallas_call(
        kernel,
        out_shape=[s for _, s in outs],
        in_specs=[spec for spec, _ in operands],
        out_specs=[spec for spec, _ in outs],
        scratch_shapes=list(scratch),
        compiler_params=pltpu.CompilerParams(vmem_limit_bytes=limit * 1024 * 1024),
        cost_estimate=pl.CostEstimate(flops=cycles * 500_000_000, bytes_accessed=cycles * 2_000_000, transcendentals=0),
    )(*[v for _, v in operands])


def trade(pieces):
    count = len(pieces)
    return [pieces[0]] + [
        lax.ppermute(pieces[s], ROW, [(i, i ^ s) for i in range(count)]) for s in range(1, count)
    ]


def gather_maps(maps):
    z_size, y_size = lax.axis_size("z"), lax.axis_size("y")
    row = lax.axis_size(ROW)
    own, _, heads, cut = maps.shape
    maps = maps.transpose(2, 0, 1, 3).reshape(y_size, row, own * 2 * cut)
    maps = maps.transpose(1, 0, 2).reshape(1, heads, own * 2 * cut)
    return jnp.broadcast_to(maps, (z_size, heads, own * 2 * cut)).reshape(z_size * heads, -1)


def body(queries, keys, values, out_grad, feature_weights):
    z_size = lax.axis_size("z")
    row = lax.axis_size("x") * lax.axis_size("core")
    own, _, heads, cut = feature_weights.shape
    tokens = queries.shape[0] * lax.axis_size(CTX)
    place = jnp.stack([lax.axis_index("z"), lax.axis_index(ROW)]).astype(jnp.int32)
    scratch = pltpu.VMEM
    one = (row, BLOCK, HEAD_DIM)
    two = (row, BLOCK, 2 * HEAD_DIM)
    four = (4, BLOCK, HEAD_DIM)
    paired = (VMEM, shape(row, 2, BLOCK, HEAD_DIM))
    piece = (VMEM, shape(2, BLOCK, HEAD_DIM))
    sums = (VMEM, shape(z_size, STATE_ROWS, HEAD_DIM))
    square = (VMEM, shape(HEAD_DIM, HEAD_DIM, dtype=F32))

    pieces = call(
        pack, [(ANY, shape(*four))] * row, [(SMEM, place)] + [(ANY, v) for v in (keys, values, queries, out_grad)],
        [scratch((row, *four), BF16), DMA((row, 4)), DMA((row,))], limit=60)
    pieces = trade(pieces)
    maps = gather_maps(feature_weights)
    maps, pieces[1] = lax.optimization_barrier((maps, pieces[1]))
    maps = lax.all_to_all(maps, FINE, 0, 0, tiled=True)
    maps = maps.reshape(z_size * row, heads // row, own, 2, cut).transpose(3, 0, 2, 1, 4)
    maps = maps.reshape(2, HEAD_DIM, HEAD_DIM)
    kv, qd, state = call(
        key_state, [paired, paired, sums], [(SMEM, place), (VMEM, maps)] + [(VMEM, v) for v in pieces])
    state = lax.all_to_all(state, "z", 0, 0, tiled=True)
    held = [(SMEM, place), (VMEM, kv), (VMEM, qd), (VMEM, maps), (VMEM, state)]
    (total,) = call(forward, [sums], held, cycles=4)
    total = lax.all_to_all(total, "z", 0, 0, tiled=True)
    *aq, part, map_grad_q = call(
        inner,
        [piece] * row + [(VMEM, shape(row, 2, BLOCK, HEAD_DIM, dtype=PART)), square],
        held,
        [scratch((row, 2, BLOCK, HEAD_DIM), BF16), scratch(one, BF16), scratch(one, BF16), scratch(two, BF16),
         scratch(two, BF16), scratch(two, BF16), scratch((row, HEAD_DIM, 2 * HEAD_DIM), F32)], cycles=6)
    aq = trade(aq)
    map_grad_k, *dkv = call(
        outer, [square] + [piece] * row,
        [(SMEM, place), (VMEM, kv), (VMEM, maps), (VMEM, total), (VMEM, part)], cycles=3)
    dkv = trade(dkv)

    map_grad = jnp.stack((map_grad_q, map_grad_k)).reshape(2, z_size * row, own, heads // row, cut)
    map_grad = map_grad.transpose(1, 3, 2, 0, 4).reshape(z_size * heads, own * 2 * cut)
    map_grad, dkv[1] = lax.optimization_barrier((map_grad, dkv[1]))
    map_grad = lax.all_to_all(map_grad, FINE, 0, 0, tiled=True)
    map_grad = jnp.sum(map_grad.reshape(z_size, heads, own * 2 * cut), axis=0) / tokens
    map_grad = map_grad.reshape(row, heads // row, own, 2, cut).transpose(2, 3, 1, 0, 4)
    map_grad = map_grad.reshape(own, 2, heads, cut)
    outs = [(ANY, shape(*queries.shape))] * 2
    attended, query_grad = call(unpack, outs, [(SMEM, place)] + [(VMEM, v) for v in aq], [DMA((row, 2))])
    key_grad, value_grad = call(unpack, outs, [(SMEM, place)] + [(VMEM, v) for v in dkv], [DMA((row, 2))])
    return attended, query_grad, key_grad, value_grad, map_grad


def solution(mesh):
    fine = Mesh(mesh.devices.reshape(8, 4, 2, 4), FINE)
    flat = P(CTX, "y")
    maps = P(CTX, None, None, "y")
    return jax.shard_map(
        body,
        mesh=fine,
        in_specs=(flat, flat, flat, flat, maps),
        out_specs=(flat, flat, flat, flat, maps),
        check_vma=False,
    )
```

time: 191 us -> 140 us (0.73)
  waiting for transfers between devices: 67.5 us -> 13.2 us
  blocking collectives: 18.4 us -> 42.9 us
  local copies, waits for them, and re-layouts: 30.5 us -> 9.68 us
  Pallas kernels: 31.7 us -> 26.3 us
  starting transfers between devices: 40.1 us -> 45.5 us
    all_to_all x6 -> x1, waiting for transfers between devices: 63 us -> 0.01 us  [body(): map_grad = lax.all_to_all(map_grad, FINE, 0, 0, tiled=True)]
    ppermute x0 -> x21, starting transfers between devices: none -> 29.7 us  [trade(): lax.ppermute(pieces[s], ROW, [(i, i ^ s) for i in range(count)])]
    all_to_all x1 -> x2, blocking collectives: 18.4 us -> 42.9 us  [the longest x1 24.6 us: body(): maps = lax.all_to_all(maps, FINE, 0, 0, tiled=True)]
    all_to_all x6 -> x1, starting transfers between devices: 36.6 us -> 12.2 us  [body(): map_grad = lax.all_to_all(map_grad, FINE, 0, 0, tiled=True)]
    unnamed x50 -> x22, local copies, waits for them, and re-layouts: 23.7 us -> 6.42 us
    ppermute x0 -> x21, waiting for transfers between devices: none -> 13.2 us  [trade(): lax.ppermute(pieces[s], ROW, [(i, i ^ s) for i in range(count)])]
    pallas_call x8 -> x7, Pallas kernels: 31.7 us -> 26.3 us  [call(): pl.pallas_call(kernel, out_shape=[s for _, s in outs], in_specs=[spec for...]
    all_to_all x1, waiting for transfers between devices: 4.46 us -> 0.01 us  [body(): total = lax.all_to_all(total, 'z', 0, 0, tiled=True)]
  transfers between devices with their start and end apart: 7 -> 23, of which waited for: 7 -> 5; matrix products, arithmetic and copies ran while one was open for 3% -> 2% of each run, Pallas kernels for 12% -> 11%
where the time goes in v3:
time: 140 us
  starting transfers between devices  45.5 us (32%)
  blocking collectives  42.9 us (31%)
  Pallas kernels  26.3 us (19%)
  waiting for transfers between devices  13.2 us (9%)
  local copies, waits for them, and re-layouts  9.68 us (7%)
    ppermute x21, starting transfers between devices, trade(): lax.ppermute(pieces[s], ROW, [(i, i ^ s) for i in range(count)])  29.7 us
    pallas_call x7, Pallas kernels, call(): pl.pallas_call(kernel, out_shape=[s for _, s in outs], in_specs=[spec for...  26.3 us
    all_to_all x1, blocking collectives, body(): maps = lax.all_to_all(maps, FINE, 0, 0, tiled=True)  24.6 us
    all_to_all x1, blocking collectives, body(): state = lax.all_to_all(state, 'z', 0, 0, tiled=True)  18.3 us
    ppermute x21, waiting for transfers between devices, trade(): lax.ppermute(pieces[s], ROW, [(i, i ^ s) for i in range(count)])  13.2 us
    all_to_all x1, starting transfers between devices, body(): map_grad = lax.all_to_all(map_grad, FINE, 0, 0, tiled=True)  12.2 us
    unnamed x22, local copies, waits for them, and re-layouts  6.42 us
    all_to_all x1, starting transfers between devices, body(): total = lax.all_to_all(total, 'z', 0, 0, tiled=True)  3.61 us
  transfers between devices with their start and end apart: 23, of which 5 were waited for; matrix products, arithmetic and copies ran while one was open for 2% of the time, Pallas kernels for 11%

profile of v3, /device:TPU:1, one launch (start us, length us, event | category | flops | bytes accessed | tf_op | source)
XLA Modules:
  0.0 139.7 jit_solution(14918456301309233733)
XLA Ops:
  0.6 0.7 pad_add_fusion.place_ref
  1.3 3.5 %shard_map.92 = (bf16[4,256,128]{2,1,0:T(8,128)(2,1)}, bf16[4,256,128]{2,1,0:T(8,128)(2,1)}, bf16[4,256,128]{2,1,0:T(8,128)(2,1)}, bf16[4,256,128]{2,1,0:T(8,128...) custom-call(s32[2]{0:T(128)} %pad_add_fusion.place_ref, ...), custom_call_target="tpu_custom_call" | custom-call | flops 500000000 | bytes 2000000 | tf_op jit(solution)/shard_map/pallas_call | solution.py:264
  4.8 3.3 %collective-permute-start = (bf16[4,256,128]{2,1,0:T(8,128)(2,1)}, bf16[4,256,128]{2,1,0:T(8,128)(2,1)S(1)}, u32[]{:S(2)}, u32[]{:S(2)}) collective-permute-start(bf16[4,256,128]{2,1,0:T(8,128)(2,1)} %get-tuple-element.43), channel_id=1, source_target_pairs={{0,4},{4,0},{8,12},{12,8},{16,20},{20,16},{24,28},{28,24},{1,5},{5... | collective-permute-start | bytes 786440 | tf_op jit(solution)/shard_map/ppermute | solution.py:278
  8.1 1.7 %collective-permute-start.2 = (bf16[4,256,128]{2,1,0:T(8,128)(2,1)}, bf16[4,256,128]{2,1,0:T(8,128)(2,1)S(1)}, u32[]{:S(2)}, u32[]{:S(2)}) collective-permute-start(bf16[4,256,128]{2,1,0:T(8,128)(2,1)} %get-tuple-element.48), channel_id=1, source_target_pairs={{0,12},{4,8},{8,4},{12,0},{16,28},{20,24},{24,20},{28,16},{1,13},{... | collective-permute-start | bytes 786440 | tf_op jit(solution)/shard_map/ppermute | solution.py:278
  9.9 1.0 collective-permute-start.3
  10.9 2.3 %collective-permute-start.4 = (bf16[4,256,128]{2,1,0:T(8,128)(2,1)}, bf16[4,256,128]{2,1,0:T(8,128)(2,1)S(1)}, u32[]{:S(2)}, u32[]{:S(2)}) collective-permute-start(bf16[4,256,128]{2,1,0:T(8,128)(2,1)} %get-tuple-element.50), channel_id=1, source_target_pairs={{0,20},{4,16},{8,28},{12,24},{16,4},{20,0},{24,12},{28,8},{1,21},{... | collective-permute-start | bytes 786440 | tf_op jit(solution)/shard_map/ppermute | solution.py:278
  13.2 0.7 collective-permute-start.5
  13.9 2.3 %collective-permute-done.1.refs_2_ = bf16[4,256,128]{2,1,0:T(8,128)(2,1)S(1)} collective-permute-done((bf16[4,256,128]{2,1,0:T(8,128)(2,1)}, bf16[4,256,128]{2,1,0:T(8,128)(2,1)S(1)}, u32[]{:S(2)}, u32[]{:S(2)}) %collective-permute-start.1) | collective-permute-done | bytes 262176 | tf_op jit(solution)/shard_map/ppermute | solution.py:278
  16.2 2.0 %collective-permute-start.6 = (bf16[4,256,128]{2,1,0:T(8,128)(2,1)}, bf16[4,256,128]{2,1,0:T(8,128)(2,1)S(1)}, u32[]{:S(2)}, u32[]{:S(2)}) collective-permute-start(bf16[4,256,128]{2,1,0:T(8,128)(2,1)} %get-tuple-element.52), channel_id=1, source_target_pairs={{0,28},{4,24},{8,20},{12,16},{16,12},{20,8},{24,4},{28,0},{1,29},{... | collective-permute-start | bytes 786440 | tf_op jit(solution)/shard_map/ppermute | solution.py:278
  18.4 24.6 %all_to_all.28 = bf16[256,1,128]{2,1,0:T(2,128)(2,1)S(1)} all-to-all(bf16[256,1,128]{2,1,0:T(2,128)(2,1)S(1)} %copy.27), channel_id=1, replica_groups=mesh['z'=8,'x'=4,'core'=2,'y'=4] {'z','x','core','y'}, dimensions={0} | all-to-all | bytes 131072 | tf_op jit(solution)/shard_map/all_to_all | solution.py:312
  43.0 0.4 reduce
  43.7 0.2 reshape.51.map_ref
  43.9 0.7 copy-done
  44.6 1.4 %shard_map.93 = (bf16[8,2,256,128]{3,2,1,0:T(8,128)(2,1)S(1)}, bf16[8,2,256,128]{3,2,1,0:T(8,128)(2,1)S(1)}, bf16[8,160,128]{2,1,0:T(8,128)(2,1)S(1)}) custom-call(s32[2]{0:T(128)S(1)} %copy-done.1, bf16[2,128,128]{2,1,0:T(8,128)(2,1)S(1)} %reshape.51.map_ref, bf16[4,256,128]{2,1,0:T(8,128)(2,1)S(1)} %copy-done, ...), custom_call_target="tpu_custom_call" | custom-call | flops 500000000 | bytes 2000000 | tf_op jit(solution)/shard_map/pallas_call | solution.py:264
  46.0 18.3 %all_to_all.29.sums_ref = bf16[8,160,128]{2,1,0:T(8,128)(2,1)S(1)} all-to-all(bf16[8,160,128]{2,1,0:T(8,128)(2,1)S(1)} %get-tuple-element.55), channel_id=1, replica_groups=mesh['z'=8,'x'=4,'core'=2,'y'=4] {'z'}, dimensions={0} | all-to-all | bytes 655360 | tf_op jit(solution)/shard_map/all_to_all | solution.py:317
  64.4 5.4 %shard_map.96 = bf16[8,160,128]{2,1,0:T(8,128)(2,1)} custom-call(s32[2]{0:T(128)S(1)} %copy-done.1, bf16[8,2,256,128]{3,2,1,0:T(8,128)(2,1)S(1)} %get-tuple-element.53.kv_ref, bf16[8,2,256,128]{3,2,1,0:T(8,128)(2,1)S(1)} %get-tuple-element.54.qd_ref, bf16[2,128,128]{2,1,0:T(8,128)(2,1)S(1)} %reshape.51.map_ref, bf16[8,160,128]{2,1,0:T(8,128)(2,1)S(1)} %all_to_all.29.sums_ref), custom_call_target="tpu_custom_call" | custom-call | flops 2000000000 | bytes 8000000 | tf_op jit(solution)/shard_map/pallas_call | solution.py:264
  69.8 1.0 copy-done.2
  70.8 3.6 %all-to-all-start.2 = ((bf16[8,160,128]{2,1,0:T(8,128)(2,1)}), bf16[8,160,128]{2,1,0:T(8,128)(2,1)S(1)}, u32[]{:S(2)}, u32[]{:S(2)}) async-start(bf16[8,160,128]{2,1,0:T(8,128)(2,1)} %shard_map.96), calls=%async_computation.2 | async-start | bytes 655360 | tf_op jit(solution)/shard_map/all_to_all | solution.py:320
  74.4 1.2 copy-done.3
  75.6 9.6 %shard_map.94 = (bf16[2,256,128]{2,1,0:T(8,128)(2,1)S(1)}, bf16[2,256,128]{2,1,0:T(8,128)(2,1)}, bf16[2,256,128]{2,1,0:T(8,128)(2,1)}, bf16[2,256,128]{2,1,0:T(8...) custom-call(s32[2]{0:T(128)S(1)} %copy-done.1, ...), custom_call_target="tpu_custom_call" | custom-call | flops 3000000000 | bytes 12000000 | tf_op jit(solution)/shard_map/pallas_call | solution.py:264
  85.3 0.7 copy-done.6
  85.9 1.0 copy-done.8
  86.9 2.6 %collective-permute-start.7 = (bf16[2,256,128]{2,1,0:T(8,128)(2,1)}, bf16[2,256,128]{2,1,0:T(8,128)(2,1)S(1)}, u32[]{:S(2)}, u32[]{:S(2)}) collective-permute-start(bf16[2,256,128]{2,1,0:T(8,128)(2,1)} %get-tuple-element.57), channel_id=1, source_target_pairs={{0,4},{4,0},{8,12},{12,8},{16,20},{20,16},{24,28},{28,24},{1,5},{5... | collective-permute-start | bytes 393224 | tf_op jit(solution)/shard_map/ppermute | solution.py:278
  89.5 1.6 %collective-permute-start.9 = (bf16[2,256,128]{2,1,0:T(8,128)(2,1)}, bf16[2,256,128]{2,1,0:T(8,128)(2,1)S(1)}, u32[]{:S(2)}, u32[]{:S(2)}) collective-permute-start(bf16[2,256,128]{2,1,0:T(8,128)(2,1)} %get-tuple-element.59), channel_id=1, source_target_pairs={{0,12},{4,8},{8,4},{12,0},{16,28},{20,24},{24,20},{28,16},{1,13},{... | collective-permute-start | bytes 393224 | tf_op jit(solution)/shard_map/ppermute | solution.py:278
  91.1 1.2 copy-done.9
  92.3 3.1 %shard_map.97 = (f32[128,128]{1,0:T(8,128)S(1)}, bf16[2,256,128]{2,1,0:T(8,128)(2,1)S(1)}, bf16[2,256,128]{2,1,0:T(8,128)(2,1)}, bf16[2,256,128]{2,1,0:T(8,128)(...) custom-call(s32[2]{0:T(128)S(1)} %copy-done.1, ...), custom_call_target="tpu_custom_call" | custom-call | flops 1500000000 | bytes 6000000 | tf_op jit(solution)/shard_map/pallas_call | solution.py:264
  95.4 0.6 copy-done.4
  96.0 0.2 collective-permute-start.14
  96.3 2.3 %collective-permute-start.10 = (bf16[2,256,128]{2,1,0:T(8,128)(2,1)S(1)}, bf16[2,256,128]{2,1,0:T(8,128)(2,1)S(1)}, u32[]{:S(2)}, u32[]{:S(2)}) collective-permute-start(bf16[2,256,128]{2,1,0:T(8,128)(2,1)S(1)} %get-tuple-element.60), channel_id=1, source_target_pairs={{0,16},{4,20},{8,24},{12,28},{16,0},{20,4},{24,8},{28,12},{1,17},{... | collective-permute-start | bytes 393224 | tf_op jit(solution)/shard_map/ppermute | solution.py:278
  98.7 0.2 stack.22
  98.9 1.2 collective-permute-start.11
  100.1 2.5 %collective-permute-start.12 = (bf16[2,256,128]{2,1,0:T(8,128)(2,1)S(1)}, bf16[2,256,128]{2,1,0:T(8,128)(2,1)S(1)}, u32[]{:S(2)}, u32[]{:S(2)}) collective-permute-start(bf16[2,256,128]{2,1,0:T(8,128)(2,1)S(1)} %get-tuple-element.62), channel_id=1, source_target_pairs={{0,24},{4,28},{8,16},{12,20},{16,8},{20,12},{24,0},{28,4},{1,25},{... | collective-permute-start | bytes 393224 | tf_op jit(solution)/shard_map/ppermute | solution.py:278
  102.6 0.3 collective-permute-start.13
  103.1 0.4 copy.29
  103.5 1.1 reshape.52
  104.6 12.2 %all-to-all-start.3 = ((f32[256,1,128]{2,1,0:T(1,128)}), f32[256,1,128]{2,1,0:T(1,128)S(1)}, u32[]{:S(2)}, u32[]{:S(2)}) async-start(f32[256,1,128]{2,1,0:T(1,128)} %bitcast.10), calls=%async_computation.3 | async-start | bytes 262144 | tf_op jit(solution)/shard_map/all_to_all | solution.py:336
  116.8 1.7 %collective-permute-start.16 = (bf16[2,256,128]{2,1,0:T(8,128)(2,1)S(1)}, bf16[2,256,128]{2,1,0:T(8,128)(2,1)S(1)}, u32[]{:S(2)}, u32[]{:S(2)}) collective-permute-start(bf16[2,256,128]{2,1,0:T(8,128)(2,1)S(1)} %get-tuple-element.73), channel_id=1, source_target_pairs={{0,12},{4,8},{8,4},{12,0},{16,28},{20,24},{24,20},{28,16},{1,13},{... | collective-permute-start | bytes 393224 | tf_op jit(solution)/shard_map/ppermute | solution.py:278
  118.5 2.4 %collective-permute-start.17 = (bf16[2,256,128]{2,1,0:T(8,128)(2,1)S(1)}, bf16[2,256,128]{2,1,0:T(8,128)(2,1)S(1)}, u32[]{:S(2)}, u32[]{:S(2)}) collective-permute-start(bf16[2,256,128]{2,1,0:T(8,128)(2,1)S(1)} %get-tuple-element.74), channel_id=1, source_target_pairs={{0,16},{4,20},{8,24},{12,28},{16,0},{20,4},{24,8},{28,12},{1,17},{... | collective-permute-start | bytes 393224 | tf_op jit(solution)/shard_map/ppermute | solution.py:278
  120.9 1.4 collective-permute-start.18
  122.3 1.3 collective-permute-start.19
  123.6 1.1 collective-permute-start.20
  124.7 1.6 %shard_map.95 = (bf16[256,1024]{1,0:T(8,128)(2,1)}, bf16[256,1024]{1,0:T(8,128)(2,1)}) custom-call(s32[2]{0:T(128)S(1)} %copy-done.1, bf16[2,256,128]{2,1,0:T(8,128)(2,1)S(1)} %copy-done.7, bf16[2,256,128]{2,1,0:T(8,128)(2,1)S(1)} %collective-permute-done.7.refs_1_, bf16[2,256,128]{2,1,0:T(8,128)(2,1)S(1)} %collective-permute-done.8.refs_2_, ...), custom_call_target="tpu_custom_call" | custom-call | flops 500000000 | bytes 2000000 | tf_op jit(solution)/shard_map/pallas_call | solution.py:264
  126.4 2.2 %collective-permute-done.17.refs_4_ = bf16[2,256,128]{2,1,0:T(8,128)(2,1)S(1)} collective-permute-done((bf16[2,256,128]{2,1,0:T(8,128)(2,1)S(1)}, bf16[2,256,128]{2,1,0:T(8,128)(2,1)S(1)}, u32[]{:S(2)}, u32[]{:S(2)}) %collective-permute-start.17) | collective-permute-done | bytes 131104 | tf_op jit(solution)/shard_map/ppermute | solution.py:278
  128.6 2.8 %collective-permute-done.18.refs_5_ = bf16[2,256,128]{2,1,0:T(8,128)(2,1)S(1)} collective-permute-done((bf16[2,256,128]{2,1,0:T(8,128)(2,1)S(1)}, bf16[2,256,128]{2,1,0:T(8,128)(2,1)S(1)}, u32[]{:S(2)}, u32[]{:S(2)}) %collective-permute-start.18) | collective-permute-done | bytes 131104 | tf_op jit(solution)/shard_map/ppermute | solution.py:278
  131.4 3.0 %collective-permute-done.19.refs_6_ = bf16[2,256,128]{2,1,0:T(8,128)(2,1)S(1)} collective-permute-done((bf16[2,256,128]{2,1,0:T(8,128)(2,1)S(1)}, bf16[2,256,128]{2,1,0:T(8,128)(2,1)S(1)}, u32[]{:S(2)}, u32[]{:S(2)}) %collective-permute-start.19) | collective-permute-done | bytes 131104 | tf_op jit(solution)/shard_map/ppermute | solution.py:278
  134.4 2.8 %collective-permute-done.20.refs_7_ = bf16[2,256,128]{2,1,0:T(8,128)(2,1)S(1)} collective-permute-done((bf16[2,256,128]{2,1,0:T(8,128)(2,1)S(1)}, bf16[2,256,128]{2,1,0:T(8,128)(2,1)S(1)}, u32[]{:S(2)}, u32[]{:S(2)}) %collective-permute-start.20) | collective-permute-done | bytes 131104 | tf_op jit(solution)/shard_map/ppermute | solution.py:278
  137.2 1.6 %shard_map.98 = (bf16[256,1024]{1,0:T(8,128)(2,1)}, bf16[256,1024]{1,0:T(8,128)(2,1)}) custom-call(s32[2]{0:T(128)S(1)} %copy-done.1, bf16[2,256,128]{2,1,0:T(8,128)(2,1)S(1)} %copy-done.5, bf16[2,256,128]{2,1,0:T(8,128)(2,1)S(1)} %collective-permute-done.14.refs_1_, bf16[2,256,128]{2,1,0:T(8,128)(2,1)S(1)} %collective-permute-done.15.refs_2_, ...), custom_call_target="tpu_custom_call" | custom-call | flops 500000000 | bytes 2000000 | tf_op jit(solution)/shard_map/pallas_call | solution.py:264
  139.0 0.7 copy.33
  (48 shorter events, 1.0 us)
Async XLA Ops:
  1.3 16.9 %copy-start.10 = (bf16[2,2,32,32]{3,2,1,0:T(8,128)(2,1)S(1)}, bf16[2,2,32,32]{3,2,1,0:T(8,128)(2,1)}, u32[]{:S(2)}) copy-start(bf16[2,2,32,32]{3,2,1,0:T(8,128)(2,1)} %param.9) | copy-start | bytes 24580
  4.8 8.4 %collective-permute-start = (bf16[4,256,128]{2,1,0:T(8,128)(2,1)}, bf16[4,256,128]{2,1,0:T(8,128)(2,1)S(1)}, u32[]{:S(2)}, u32[]{:S(2)}) collective-permute-start(bf16[4,256,128]{2,1,0:T(8,128)(2,1)} %get-tuple-element.43), channel_id=1, source_target_pairs={{0,4},{4,0},{8,12},{12,8},{16,20},{20,16},{24,28},{28,24},{1,5},{5... | collective-permute-start | bytes 786440 | tf_op jit(solution)/shard_map/ppermute | solution.py:278
  8.1 8.1 %collective-permute-start.1 = (bf16[4,256,128]{2,1,0:T(8,128)(2,1)}, bf16[4,256,128]{2,1,0:T(8,128)(2,1)S(1)}, u32[]{:S(2)}, u32[]{:S(2)}) collective-permute-start(bf16[4,256,128]{2,1,0:T(8,128)(2,1)} %get-tuple-element.47), channel_id=1, source_target_pairs={{0,8},{4,12},{8,0},{12,4},{16,24},{20,28},{24,16},{28,20},{1,9},{5... | collective-permute-start | bytes 786440 | tf_op jit(solution)/shard_map/ppermute | solution.py:278
  8.1 35.7 %collective-permute-start.2 = (bf16[4,256,128]{2,1,0:T(8,128)(2,1)}, bf16[4,256,128]{2,1,0:T(8,128)(2,1)S(1)}, u32[]{:S(2)}, u32[]{:S(2)}) collective-permute-start(bf16[4,256,128]{2,1,0:T(8,128)(2,1)} %get-tuple-element.48), channel_id=1, source_target_pairs={{0,12},{4,8},{8,4},{12,0},{16,28},{20,24},{24,20},{28,16},{1,13},{... | collective-permute-start | bytes 786440 | tf_op jit(solution)/shard_map/ppermute | solution.py:278
  9.9 34.0 %collective-permute-start.3 = (bf16[4,256,128]{2,1,0:T(8,128)(2,1)}, bf16[4,256,128]{2,1,0:T(8,128)(2,1)S(1)}, u32[]{:S(2)}, u32[]{:S(2)}) collective-permute-start(bf16[4,256,128]{2,1,0:T(8,128)(2,1)} %get-tuple-element.49), channel_id=1, source_target_pairs={{0,16},{4,20},{8,24},{12,28},{16,0},{20,4},{24,8},{28,12},{1,17},{... | collective-permute-start | bytes 786440 | tf_op jit(solution)/shard_map/ppermute | solution.py:278
  10.9 33.0 %collective-permute-start.4 = (bf16[4,256,128]{2,1,0:T(8,128)(2,1)}, bf16[4,256,128]{2,1,0:T(8,128)(2,1)S(1)}, u32[]{:S(2)}, u32[]{:S(2)}) collective-permute-start(bf16[4,256,128]{2,1,0:T(8,128)(2,1)} %get-tuple-element.50), channel_id=1, source_target_pairs={{0,20},{4,16},{8,28},{12,24},{16,4},{20,0},{24,12},{28,8},{1,21},{... | collective-permute-start | bytes 786440 | tf_op jit(solution)/shard_map/ppermute | solution.py:278
  13.2 30.7 %collective-permute-start.5 = (bf16[4,256,128]{2,1,0:T(8,128)(2,1)}, bf16[4,256,128]{2,1,0:T(8,128)(2,1)S(1)}, u32[]{:S(2)}, u32[]{:S(2)}) collective-permute-start(bf16[4,256,128]{2,1,0:T(8,128)(2,1)} %get-tuple-element.51), channel_id=1, source_target_pairs={{0,24},{4,28},{8,16},{12,20},{16,8},{20,12},{24,0},{28,4},{1,25},{... | collective-permute-start | bytes 786440 | tf_op jit(solution)/shard_map/ppermute | solution.py:278
  16.2 27.7 %collective-permute-start.6 = (bf16[4,256,128]{2,1,0:T(8,128)(2,1)}, bf16[4,256,128]{2,1,0:T(8,128)(2,1)S(1)}, u32[]{:S(2)}, u32[]{:S(2)}) collective-permute-start(bf16[4,256,128]{2,1,0:T(8,128)(2,1)} %get-tuple-element.52), channel_id=1, source_target_pairs={{0,28},{4,24},{8,20},{12,16},{16,12},{20,8},{24,4},{28,0},{1,29},{... | collective-permute-start | bytes 786440 | tf_op jit(solution)/shard_map/ppermute | solution.py:278
  43.7 1.0 copy-start
  43.9 0.8 copy-start.1
  69.8 1.0 copy-start.2
  70.8 20.3 %all-to-all-start.2 = ((bf16[8,160,128]{2,1,0:T(8,128)(2,1)}), bf16[8,160,128]{2,1,0:T(8,128)(2,1)S(1)}, u32[]{:S(2)}, u32[]{:S(2)}) async-start(bf16[8,160,128]{2,1,0:T(8,128)(2,1)} %shard_map.96), calls=%async_computation.2 | async-start | bytes 655360 | tf_op jit(solution)/shard_map/all_to_all | solution.py:320
  74.4 1.2 copy-start.3
  85.3 0.7 copy-start.6
  85.9 1.0 copy-start.8
  86.9 12.0 %collective-permute-start.7 = (bf16[2,256,128]{2,1,0:T(8,128)(2,1)}, bf16[2,256,128]{2,1,0:T(8,128)(2,1)S(1)}, u32[]{:S(2)}, u32[]{:S(2)}) collective-permute-start(bf16[2,256,128]{2,1,0:T(8,128)(2,1)} %get-tuple-element.57), channel_id=1, source_target_pairs={{0,4},{4,0},{8,12},{12,8},{16,20},{20,16},{24,28},{28,24},{1,5},{5... | collective-permute-start | bytes 393224 | tf_op jit(solution)/shard_map/ppermute | solution.py:278
  89.5 10.7 %collective-permute-start.8 = (bf16[2,256,128]{2,1,0:T(8,128)(2,1)}, bf16[2,256,128]{2,1,0:T(8,128)(2,1)S(1)}, u32[]{:S(2)}, u32[]{:S(2)}) collective-permute-start(bf16[2,256,128]{2,1,0:T(8,128)(2,1)} %get-tuple-element.58), channel_id=1, source_target_pairs={{0,8},{4,12},{8,0},{12,4},{16,24},{20,28},{24,16},{28,20},{1,9},{5... | collective-permute-start | bytes 393224 | tf_op jit(solution)/shard_map/ppermute | solution.py:278
  89.5 13.2 %collective-permute-start.9 = (bf16[2,256,128]{2,1,0:T(8,128)(2,1)}, bf16[2,256,128]{2,1,0:T(8,128)(2,1)S(1)}, u32[]{:S(2)}, u32[]{:S(2)}) collective-permute-start(bf16[2,256,128]{2,1,0:T(8,128)(2,1)} %get-tuple-element.59), channel_id=1, source_target_pairs={{0,12},{4,8},{8,4},{12,0},{16,28},{20,24},{24,20},{28,16},{1,13},{... | collective-permute-start | bytes 393224 | tf_op jit(solution)/shard_map/ppermute | solution.py:278
  91.1 1.2 copy-start.9
  95.4 0.6 copy-start.4
  96.0 6.9 %collective-permute-start.14 = (bf16[2,256,128]{2,1,0:T(8,128)(2,1)}, bf16[2,256,128]{2,1,0:T(8,128)(2,1)S(1)}, u32[]{:S(2)}, u32[]{:S(2)}) collective-permute-start(bf16[2,256,128]{2,1,0:T(8,128)(2,1)} %get-tuple-element.70), channel_id=1, source_target_pairs={{0,4},{4,0},{8,12},{12,8},{16,20},{20,16},{24,28},{28,24},{1,5},{5... | collective-permute-start | bytes 393224 | tf_op jit(solution)/shard_map/ppermute | solution.py:278
  96.3 20.5 %collective-permute-start.10 = (bf16[2,256,128]{2,1,0:T(8,128)(2,1)S(1)}, bf16[2,256,128]{2,1,0:T(8,128)(2,1)S(1)}, u32[]{:S(2)}, u32[]{:S(2)}) collective-permute-start(bf16[2,256,128]{2,1,0:T(8,128)(2,1)S(1)} %get-tuple-element.60), channel_id=1, source_target_pairs={{0,16},{4,20},{8,24},{12,28},{16,0},{20,4},{24,8},{28,12},{1,17},{... | collective-permute-start | bytes 393224 | tf_op jit(solution)/shard_map/ppermute | solution.py:278
  98.9 19.6 %collective-permute-start.11 = (bf16[2,256,128]{2,1,0:T(8,128)(2,1)S(1)}, bf16[2,256,128]{2,1,0:T(8,128)(2,1)S(1)}, u32[]{:S(2)}, u32[]{:S(2)}) collective-permute-start(bf16[2,256,128]{2,1,0:T(8,128)(2,1)S(1)} %get-tuple-element.61), channel_id=1, source_target_pairs={{0,20},{4,16},{8,28},{12,24},{16,4},{20,0},{24,12},{28,8},{1,21},{... | collective-permute-start | bytes 393224 | tf_op jit(solution)/shard_map/ppermute | solution.py:278
  100.1 20.8 %collective-permute-start.12 = (bf16[2,256,128]{2,1,0:T(8,128)(2,1)S(1)}, bf16[2,256,128]{2,1,0:T(8,128)(2,1)S(1)}, u32[]{:S(2)}, u32[]{:S(2)}) collective-permute-start(bf16[2,256,128]{2,1,0:T(8,128)(2,1)S(1)} %get-tuple-element.62), channel_id=1, source_target_pairs={{0,24},{4,28},{8,16},{12,20},{16,8},{20,12},{24,0},{28,4},{1,25},{... | collective-permute-start | bytes 393224 | tf_op jit(solution)/shard_map/ppermute | solution.py:278
  102.6 19.7 %collective-permute-start.13 = (bf16[2,256,128]{2,1,0:T(8,128)(2,1)S(1)}, bf16[2,256,128]{2,1,0:T(8,128)(2,1)S(1)}, u32[]{:S(2)}, u32[]{:S(2)}) collective-permute-start(bf16[2,256,128]{2,1,0:T(8,128)(2,1)S(1)} %get-tuple-element.63), channel_id=1, source_target_pairs={{0,28},{4,24},{8,20},{12,16},{16,12},{20,8},{24,4},{28,0},{1,29},{... | collective-permute-start | bytes 393224 | tf_op jit(solution)/shard_map/ppermute | solution.py:278
  102.9 20.7 %collective-permute-start.15 = (bf16[2,256,128]{2,1,0:T(8,128)(2,1)S(1)}, bf16[2,256,128]{2,1,0:T(8,128)(2,1)S(1)}, u32[]{:S(2)}, u32[]{:S(2)}) collective-permute-start(bf16[2,256,128]{2,1,0:T(8,128)(2,1)S(1)} %get-tuple-element.72), channel_id=1, source_target_pairs={{0,8},{4,12},{8,0},{12,4},{16,24},{20,28},{24,16},{28,20},{1,9},{5... | collective-permute-start | bytes 393224 | tf_op jit(solution)/shard_map/ppermute | solution.py:278
  104.6 20.1 %copy-start.7 = (bf16[2,256,128]{2,1,0:T(8,128)(2,1)S(1)}, bf16[2,256,128]{2,1,0:T(8,128)(2,1)}, u32[]{:S(2)}) copy-start(bf16[2,256,128]{2,1,0:T(8,128)(2,1)} %copy-done.6) | copy-start | bytes 393220
  104.6 34.3 %all-to-all-start.3 = ((f32[256,1,128]{2,1,0:T(1,128)}), f32[256,1,128]{2,1,0:T(1,128)S(1)}, u32[]{:S(2)}, u32[]{:S(2)}) async-start(f32[256,1,128]{2,1,0:T(1,128)} %bitcast.10), calls=%async_computation.3 | async-start | bytes 262144 | tf_op jit(solution)/shard_map/all_to_all | solution.py:336
  116.8 9.6 %collective-permute-start.16 = (bf16[2,256,128]{2,1,0:T(8,128)(2,1)S(1)}, bf16[2,256,128]{2,1,0:T(8,128)(2,1)S(1)}, u32[]{:S(2)}, u32[]{:S(2)}) collective-permute-start(bf16[2,256,128]{2,1,0:T(8,128)(2,1)S(1)} %get-tuple-element.73), channel_id=1, source_target_pairs={{0,12},{4,8},{8,4},{12,0},{16,28},{20,24},{24,20},{28,16},{1,13},{... | collective-permute-start | bytes 393224 | tf_op jit(solution)/shard_map/ppermute | solution.py:278
  118.5 10.1 %collective-permute-start.17 = (bf16[2,256,128]{2,1,0:T(8,128)(2,1)S(1)}, bf16[2,256,128]{2,1,0:T(8,128)(2,1)S(1)}, u32[]{:S(2)}, u32[]{:S(2)}) collective-permute-start(bf16[2,256,128]{2,1,0:T(8,128)(2,1)S(1)} %get-tuple-element.74), channel_id=1, source_target_pairs={{0,16},{4,20},{8,24},{12,28},{16,0},{20,4},{24,8},{28,12},{1,17},{... | collective-permute-start | bytes 393224 | tf_op jit(solution)/shard_map/ppermute | solution.py:278
  120.9 10.5 %collective-permute-start.18 = (bf16[2,256,128]{2,1,0:T(8,128)(2,1)S(1)}, bf16[2,256,128]{2,1,0:T(8,128)(2,1)S(1)}, u32[]{:S(2)}, u32[]{:S(2)}) collective-permute-start(bf16[2,256,128]{2,1,0:T(8,128)(2,1)S(1)} %get-tuple-element.75), channel_id=1, source_target_pairs={{0,20},{4,16},{8,28},{12,24},{16,4},{20,0},{24,12},{28,8},{1,21},{... | collective-permute-start | bytes 393224 | tf_op jit(solution)/shard_map/ppermute | solution.py:278
  122.3 12.1 %collective-permute-start.19 = (bf16[2,256,128]{2,1,0:T(8,128)(2,1)S(1)}, bf16[2,256,128]{2,1,0:T(8,128)(2,1)S(1)}, u32[]{:S(2)}, u32[]{:S(2)}) collective-permute-start(bf16[2,256,128]{2,1,0:T(8,128)(2,1)S(1)} %get-tuple-element.76), channel_id=1, source_target_pairs={{0,24},{4,28},{8,16},{12,20},{16,8},{20,12},{24,0},{28,4},{1,25},{... | collective-permute-start | bytes 393224 | tf_op jit(solution)/shard_map/ppermute | solution.py:278
  123.6 13.6 %collective-permute-start.20 = (bf16[2,256,128]{2,1,0:T(8,128)(2,1)S(1)}, bf16[2,256,128]{2,1,0:T(8,128)(2,1)S(1)}, u32[]{:S(2)}, u32[]{:S(2)}) collective-permute-start(bf16[2,256,128]{2,1,0:T(8,128)(2,1)S(1)} %get-tuple-element.77), channel_id=1, source_target_pairs={{0,28},{4,24},{8,20},{12,16},{16,12},{20,8},{24,4},{28,0},{1,29},{... | collective-permute-start | bytes 393224 | tf_op jit(solution)/shard_map/ppermute | solution.py:278
  124.7 12.5 %copy-start.5 = (bf16[2,256,128]{2,1,0:T(8,128)(2,1)S(1)}, bf16[2,256,128]{2,1,0:T(8,128)(2,1)}, u32[]{:S(2)}) copy-start(bf16[2,256,128]{2,1,0:T(8,128)(2,1)} %copy-done.4) | copy-start | bytes 393220

commit v4 on v3

v4 whole, which is shorter than its diff:
```python
import jax
import jax.numpy as jnp
from jax import lax
from jax.experimental import pallas as pl
from jax.experimental.pallas import tpu as pltpu
from jax.sharding import Mesh
from jax.sharding import PartitionSpec as P

HEAD_DIM = 128
BLOCK = 256
F32 = jnp.float32
BF16 = jnp.bfloat16
ROW = ("x", "core")
CTX = ("z", "x", "core")
FINE = ("z", "x", "core", "y")
ANY = pl.BlockSpec(memory_space=pl.ANY)
VMEM = pl.BlockSpec(memory_space=pltpu.VMEM)
SMEM = pl.BlockSpec(memory_space=pltpu.SMEM)
DMA = pltpu.SemaphoreType.DMA
PART = BF16
STATE_ROWS = HEAD_DIM + 16
GROUP = 4


def mm(a, b):
    return lax.dot_general(a, b, (((1,), (0,)), ((), ())), preferred_element_type=F32)


def mm_nt(a, b):
    return lax.dot_general(a, b, (((1,), (1,)), ((), ())), preferred_element_type=F32)


def mm_tn(a, b):
    return lax.dot_general(a, b, (((0,), (0,)), ((), ())), preferred_element_type=F32)


def feature(pre):
    return jnp.where(pre > 0, pre + 1.0, jnp.exp(jnp.minimum(pre, 0.0)))


def halves(value):
    high = value.astype(BF16)
    return high, (value - high.astype(F32)).astype(BF16)


def causal_mask():
    rows = lax.broadcasted_iota(jnp.int32, (BLOCK, BLOCK), 0)
    cols = lax.broadcasted_iota(jnp.int32, (BLOCK, BLOCK), 1)
    return rows >= cols


def lanes(rows):
    return lax.broadcasted_iota(jnp.int32, (rows, HEAD_DIM), 1)


def row_slope(grad, attended):
    return jnp.broadcast_to(-jnp.sum(grad * attended, axis=1, keepdims=True), grad.shape)


def norm_rows(column, centre):
    rows = column.T[:16]
    index = lax.broadcasted_iota(jnp.int32, (16, HEAD_DIM), 0)
    high = rows.astype(BF16).astype(F32)
    mid = (rows - high).astype(BF16).astype(F32)
    low = rows - high - mid
    parts = jnp.where(index == 0, high, jnp.where(index == 1, mid, jnp.where(index == 2, low, 0.0)))
    return jnp.where(index < 8, parts, jnp.broadcast_to(centre, (16, HEAD_DIM))).astype(BF16)


def turned(matrix):
    return matrix.astype(F32).T.astype(BF16)


def halves_into(value, high_ref, low_ref, b):
    high, low = halves(value)
    high_ref[b] = high
    low_ref[b] = low


def pack(place_ref, *refs):
    ins, outs, (held, in_sem, out_sem) = refs[:4], refs[4:-3], refs[-3:]
    loads, stores = [], []
    for s in range(len(outs)):
        column = pl.ds(pl.multiple_of((place_ref[1] ^ s) * HEAD_DIM, HEAD_DIM), HEAD_DIM)
        for n, ref in enumerate(ins):
            loads.append(pltpu.make_async_copy(ref.at[:, column], held.at[s, n], in_sem.at[s, n]))
        stores.append(pltpu.make_async_copy(held.at[s], outs[s], out_sem.at[s]))
    for load in loads:
        load.start()
    for s, store in enumerate(stores):
        for load in loads[4 * s:4 * s + 4]:
            load.wait()
        store.start()
    for store in stores:
        store.wait()


def unpack(place_ref, *refs):
    pieces, outs, sem = refs[:-5], refs[-5:-1], refs[-1]
    copies = []
    for s, piece in enumerate(pieces):
        column = pl.ds(pl.multiple_of((place_ref[1] ^ s) * HEAD_DIM, HEAD_DIM), HEAD_DIM)
        for n, ref in enumerate(outs):
            copies.append(pltpu.make_async_copy(piece.at[n], ref.at[:, column], sem.at[s, n]))
    for copy in copies:
        copy.start()
    for copy in copies:
        copy.wait()


def key_state(place_ref, map_ref, *refs):
    pieces, (kv_ref, qd_ref, out_ref) = refs[:-3], refs[-3:]
    blocks = len(pieces)
    for s, piece in enumerate(pieces):
        kv_ref[place_ref[1] ^ s] = piece[:2]
        qd_ref[place_ref[1] ^ s] = piece[2:]
    key_map = turned(map_ref[1])
    total = jnp.zeros((HEAD_DIM, 2 * HEAD_DIM), F32)
    mean = jnp.zeros((1, HEAD_DIM), F32)
    feats = [feature(mm_nt(key_map, kv_ref[b, 0])).astype(BF16) for b in range(blocks)]
    for b in range(blocks):
        value = kv_ref[b, 1]
        mean = mean + jnp.sum(value.astype(F32), axis=0, keepdims=True)
        total = total + mm(feats[b], with_ones(value))
    centre = (mean * (1.0 / (blocks * BLOCK))).astype(BF16).astype(F32)
    column = total[:, HEAD_DIM:]
    state = (total[:, :HEAD_DIM] - column * centre).astype(BF16)
    norms = norm_rows(column, centre)
    for z in range(out_ref.shape[0]):
        out_ref[z, :HEAD_DIM] = state
        out_ref[z, HEAD_DIM:] = norms


def with_ones(value):
    return jnp.concatenate([value, jnp.ones((BLOCK, HEAD_DIM), BF16)], axis=1)


def prior_of(place, sums_ref):
    prior = jnp.zeros((HEAD_DIM, HEAD_DIM), F32)
    norms, centres = [], []
    for z in range(sums_ref.shape[0]):
        part = jnp.where(z < place, sums_ref[z].astype(F32), 0.0)
        prior = prior + part[:HEAD_DIM]
        norms.append(part[HEAD_DIM:HEAD_DIM + 8])
        centres.append(part[HEAD_DIM + 8:])
    centres = jnp.concatenate(centres, axis=0).astype(BF16)
    centres = jnp.concatenate([centres, jnp.ones_like(centres)], axis=1)
    prior = jnp.concatenate([prior, jnp.zeros_like(prior)], axis=1)
    return prior + mm_tn(jnp.concatenate(norms, axis=0).astype(BF16), centres)


def key_stage(place, kv_ref, map_ref, sums_ref, highs, lows):
    blocks = kv_ref.shape[0]
    key_map = turned(map_ref[1])
    prior = prior_of(place, sums_ref)
    feats = [feature(mm_nt(key_map, kv_ref[b, 0])).astype(BF16) for b in range(blocks)]
    states = [mm(feats[b], with_ones(kv_ref[b, 1])) for b in range(blocks)]
    for b in range(blocks):
        halves_into(prior, highs, lows, b)
        prior = prior + states[b]
    return feats


def attend(group, kv_ref, qd_ref, feat_q, scores, highs, lows):
    weight = [s.astype(BF16) for s in scores]
    both = [mm(jnp.concatenate([f, f], axis=1), jnp.concatenate([highs[b], lows[b]], axis=0))
            for b, f in zip(group, feat_q)]
    inside = [mm(w, kv_ref[b, 1]) for b, w in zip(group, weight)]
    inverse = [1.0 / (p[:, HEAD_DIM:] + jnp.sum(s, axis=1, keepdims=True)) for p, s in zip(both, scores)]
    attended = [(p[:, :HEAD_DIM] + w) * i for p, w, i in zip(both, inside, inverse)]
    exact = [qd_ref[b, 1].astype(F32) * i for b, i in zip(group, inverse)]
    grad = [e.astype(BF16) for e in exact]
    across = [halves(row_slope(g.astype(F32), a)) for g, a in zip(grad, attended)]
    return attended, exact, grad, across


def groups_of(blocks):
    return [range(b, min(b + GROUP, blocks)) for b in range(0, blocks, GROUP)]


def forward(place_ref, kv_ref, qd_ref, map_ref, sums_ref, out_ref, highs, lows):
    blocks = kv_ref.shape[0]
    feats = key_stage(place_ref[0], kv_ref, map_ref, sums_ref, highs, lows)
    query_map = turned(map_ref[0])
    causal = causal_mask()
    lane = lanes(BLOCK)
    total = jnp.zeros((HEAD_DIM, 2 * HEAD_DIM), F32)
    centre = jnp.zeros((1, HEAD_DIM), F32)
    for group in groups_of(blocks):
        feat_q = [feature(mm(qd_ref[b, 0], map_ref[0])).astype(BF16) for b in group]
        feat_qt = [feature(mm_nt(query_map, qd_ref[b, 0])).astype(BF16) for b in group]
        scores = [jnp.where(causal, mm(f, feats[b]), 0.0) for b, f in zip(group, feat_q)]
        _, _, grads, across = attend(group, kv_ref, qd_ref, feat_q, scores, highs, lows)
        pairs = [jnp.where(lane == 0, a, jnp.where(lane == 1, r, jnp.zeros_like(r))) for a, r in across]
        for f, g, p in zip(feat_qt, grads, pairs):
            total = total + mm(f, jnp.concatenate([g, p], axis=1))
        for b in group:
            centre = centre + jnp.sum(kv_ref[b, 1].astype(F32), axis=0, keepdims=True)
    sent = total[:, :HEAD_DIM].astype(BF16)
    centre = (centre * (1.0 / (blocks * BLOCK))).astype(BF16).astype(F32)
    rest = jnp.sum((total[:, :HEAD_DIM] - sent.astype(F32)) * centre, axis=1, keepdims=True)
    column = jnp.sum(total[:, HEAD_DIM:], axis=1, keepdims=True) + rest
    norms = norm_rows(jnp.broadcast_to(column, (HEAD_DIM, HEAD_DIM)), jnp.zeros_like(centre))
    for z in range(out_ref.shape[0]):
        out_ref[z, :HEAD_DIM] = sent
        out_ref[z, HEAD_DIM:] = norms


def inner(place_ref, kv_ref, qd_ref, map_ref, sums_ref, aq_ref, part_ref, map_grad_ref,
          highs, lows, insides, adjoints, fks):
    blocks = kv_ref.shape[0]
    feats = key_stage(place_ref[0], kv_ref, map_ref, sums_ref, highs, lows)
    query_map = turned(map_ref[0])
    causal = causal_mask()
    rows = lax.broadcasted_iota(jnp.int32, (BLOCK, BLOCK), 0)
    cols = lax.broadcasted_iota(jnp.int32, (BLOCK, BLOCK), 1)
    anti = rows <= cols
    lane = lanes(BLOCK)
    few = lanes(HEAD_DIM) < 2
    unit = jnp.where((lane == 2) | (lane == 3), 1.0, 0.0).astype(BF16)
    none = jnp.zeros((HEAD_DIM, HEAD_DIM), BF16)
    map_grad = jnp.zeros((HEAD_DIM, HEAD_DIM), F32)

    def narrow(part):
        return jnp.concatenate([part[:, :HEAD_DIM], jnp.where(few, part[:, HEAD_DIM:], none)], axis=1)

    for group in groups_of(blocks):
        feat_q = [feature(mm(qd_ref[b, 0], map_ref[0])).astype(BF16) for b in group]
        feat_qt = [feature(mm_nt(query_map, qd_ref[b, 0])).astype(BF16) for b in group]
        feat_k = [feature(mm(kv_ref[b, 0], map_ref[1])).astype(BF16) for b in group]
        scores = [jnp.where(causal, mm(f, feats[b]), 0.0) for b, f in zip(group, feat_q)]
        weight_t = [jnp.where(anti, mm(k, q), 0.0).astype(BF16) for k, q in zip(feat_k, feat_qt)]
        attended, exact, halfs, across = attend(group, kv_ref, qd_ref, feat_q, scores, highs, lows)
        within = [halves(row_slope(e, a)) for e, a in zip(exact, attended)]
        pairs = [jnp.where(lane == 0, a, jnp.where(lane == 1, r, jnp.zeros_like(r))) for a, r in across]
        pairs = [jnp.where(lane == 2, a, jnp.where(lane == 3, r, p)) for p, (a, r) in zip(pairs, within)]
        grads = [jnp.concatenate([g, p], axis=1) for g, p in zip(halfs, pairs)]
        values = [jnp.concatenate([kv_ref[b, 1], unit], axis=1) for b in group]
        dscore = [jnp.where(causal, mm_nt(g, v), 0.0).astype(BF16) for g, v in zip(grads, values)]
        dscore_t = [jnp.where(anti, mm_nt(v, g), 0.0).astype(BF16) for g, v in zip(grads, values)]
        d_feat = [mm_nt(g, narrow(highs[b])) + mm_nt(g, narrow(lows[b])) + mm(d, k)
                  for b, g, d, k in zip(group, grads, dscore, feat_k)]
        dpre = [(d * jnp.minimum(f.astype(F32), 1.0)).astype(BF16) for d, f in zip(d_feat, feat_q)]
        for n, b in enumerate(group):
            aq_ref[b, 0] = attended[n].astype(BF16)
            aq_ref[b, 1] = mm_nt(dpre[n], map_ref[0]).astype(BF16)
            map_grad = map_grad + mm_tn(qd_ref[b, 0], dpre[n])
            insides[b, 0] = mm(dscore_t[n], feat_q[n])
            insides[b, 1] = mm(weight_t[n], halfs[n])
            adjoints[b] = mm(feat_qt[n], grads[n])
            fks[b] = feat_k[n]
    map_grad_ref[...] = map_grad
    pair = jnp.where(lane < 2, 1.0, 0.0).astype(BF16)
    after = jnp.zeros((HEAD_DIM, 2 * HEAD_DIM), F32)
    for b in range(blocks - 1, -1, -1):
        halves_into(after, highs, lows, b)
        after = after + adjoints[b]
    for b in range(blocks):
        wide = jnp.concatenate([kv_ref[b, 1], pair], axis=1)
        feat_k = fks[b]
        part_ref[b, 0] = (mm_nt(wide, highs[b]) + mm_nt(wide, lows[b]) + insides[b, 0]).astype(PART)
        stacked = jnp.concatenate([highs[b, :, :HEAD_DIM], lows[b, :, :HEAD_DIM]], axis=0)
        part_ref[b, 1] = (mm(jnp.concatenate([feat_k, feat_k], axis=1), stacked) + insides[b, 1]).astype(PART)


def outer(place_ref, kv_ref, map_ref, sums_ref, aq_ref, part_ref, out_ref, *pieces):
    place = place_ref[0]
    after = jnp.zeros((HEAD_DIM, HEAD_DIM), F32)
    norms = []
    for z in range(sums_ref.shape[0]):
        part = jnp.where(z > place, sums_ref[z].astype(F32), 0.0)
        after = after + part[:HEAD_DIM]
        norms.append(part[HEAD_DIM:HEAD_DIM + 8])
    norms = jnp.concatenate(norms, axis=0).astype(BF16)
    first = jnp.where(lax.broadcasted_iota(jnp.int32, norms.shape, 1) == 0, 1.0, 0.0).astype(BF16)
    after = jnp.concatenate([after, mm_tn(norms, first)], axis=1)
    high, low = halves(after)
    stacked = jnp.concatenate([high[:, :HEAD_DIM], low[:, :HEAD_DIM]], axis=0)
    pair = jnp.where(lanes(BLOCK) == 0, 1.0, 0.0).astype(BF16)
    map_grad = jnp.zeros((HEAD_DIM, HEAD_DIM), F32)
    for group in groups_of(len(pieces)):
        at = [place_ref[1] ^ s for s in group]
        feat_k = [feature(mm(kv_ref[b, 0], map_ref[1])).astype(BF16) for b in at]
        wide = [jnp.concatenate([kv_ref[b, 1], pair], axis=1) for b in at]
        d_feat = [mm_nt(w, high) + mm_nt(w, low) + part_ref[b, 0].astype(F32) for b, w in zip(at, wide)]
        dpre = [(d * jnp.minimum(f.astype(F32), 1.0)).astype(BF16) for d, f in zip(d_feat, feat_k)]
        d_value = [mm(jnp.concatenate([f, f], axis=1), stacked) + part_ref[b, 1].astype(F32)
                   for b, f in zip(at, feat_k)]
        for n, s in enumerate(group):
            pieces[s][:2] = aq_ref[at[n]]
            pieces[s][2] = mm_nt(dpre[n], map_ref[1]).astype(BF16)
            pieces[s][3] = d_value[n].astype(BF16)
            map_grad = map_grad + mm_tn(kv_ref[at[n], 0], dpre[n])
    out_ref[...] = map_grad


def shape(*dims, dtype=BF16):
    return jax.ShapeDtypeStruct(dims, dtype)


def call(kernel, outs, operands, scratch=(), cycles=1, limit=32):
    return pl.pallas_call(
        kernel,
        out_shape=[s for _, s in outs],
        in_specs=[spec for spec, _ in operands],
        out_specs=[spec for spec, _ in outs],
        scratch_shapes=list(scratch),
        compiler_params=pltpu.CompilerParams(vmem_limit_bytes=limit * 1024 * 1024),
        cost_estimate=pl.CostEstimate(flops=cycles * 500_000_000, bytes_accessed=cycles * 2_000_000, transcendentals=0),
    )(*[v for _, v in operands])


def trade(pieces):
    count = len(pieces)
    return [pieces[0]] + [
        lax.ppermute(pieces[s], ROW, [(i, i ^ s) for i in range(count)]) for s in range(1, count)
    ]


def gather_maps(maps):
    z_size, y_size = lax.axis_size("z"), lax.axis_size("y")
    row = lax.axis_size(ROW)
    own, _, heads, cut = maps.shape
    maps = maps.transpose(2, 0, 1, 3).reshape(y_size, row, own * 2 * cut)
    maps = maps.transpose(1, 0, 2).reshape(1, heads, own * 2 * cut)
    return jnp.broadcast_to(maps, (z_size, heads, own * 2 * cut)).reshape(z_size * heads, -1)


def body(queries, keys, values, out_grad, feature_weights):
    z_size = lax.axis_size("z")
    row = lax.axis_size("x") * lax.axis_size("core")
    own, _, heads, cut = feature_weights.shape
    tokens = queries.shape[0] * lax.axis_size(CTX)
    place = jnp.stack([lax.axis_index("z"), lax.axis_index(ROW)]).astype(jnp.int32)
    scratch = pltpu.VMEM
    four = (4, BLOCK, HEAD_DIM)
    paired = (VMEM, shape(row, 2, BLOCK, HEAD_DIM))
    sums = (VMEM, shape(z_size, STATE_ROWS, HEAD_DIM))
    square = (VMEM, shape(HEAD_DIM, HEAD_DIM, dtype=F32))

    pieces = call(
        pack, [(ANY, shape(*four))] * row, [(SMEM, place)] + [(ANY, v) for v in (keys, values, queries, out_grad)],
        [scratch((row, *four), BF16), DMA((row, 4)), DMA((row,))], limit=60)
    pieces = trade(pieces)
    maps = gather_maps(feature_weights)
    maps, pieces[1] = lax.optimization_barrier((maps, pieces[1]))
    maps = lax.all_to_all(maps, FINE, 0, 0, tiled=True)
    maps = maps.reshape(z_size * row, heads // row, own, 2, cut).transpose(3, 0, 2, 1, 4)
    maps = maps.reshape(2, HEAD_DIM, HEAD_DIM)
    kv, qd, state = call(
        key_state, [paired, paired, sums], [(SMEM, place), (VMEM, maps)] + [(VMEM, v) for v in pieces])
    state = lax.all_to_all(state, "z", 0, 0, tiled=True)
    held = [(SMEM, place), (VMEM, kv), (VMEM, qd), (VMEM, maps), (VMEM, state)]
    halved = [scratch((row, HEAD_DIM, 2 * HEAD_DIM), BF16)] * 2
    (total,) = call(forward, [sums], held, halved, cycles=4)
    total = lax.all_to_all(total, "z", 0, 0, tiled=True)
    aq, part, map_grad_q = call(
        inner, [paired, (VMEM, shape(row, 2, BLOCK, HEAD_DIM, dtype=PART)), square], held,
        halved + [scratch((row, 2, BLOCK, HEAD_DIM), F32), scratch((row, HEAD_DIM, 2 * HEAD_DIM), F32),
                  scratch((row, BLOCK, HEAD_DIM), BF16)], cycles=6)
    map_grad_k, *pieces = call(
        outer, [square] + [(VMEM, shape(*four))] * row,
        [(SMEM, place), (VMEM, kv), (VMEM, maps), (VMEM, total), (VMEM, aq), (VMEM, part)], cycles=3)
    pieces = trade(pieces)

    map_grad = jnp.stack((map_grad_q, map_grad_k)).reshape(2, z_size * row, own, heads // row, cut)
    map_grad = map_grad.transpose(1, 3, 2, 0, 4).reshape(z_size * heads, own * 2 * cut)
    map_grad, pieces[1] = lax.optimization_barrier((map_grad, pieces[1]))
    map_grad = lax.all_to_all(map_grad, FINE, 0, 0, tiled=True)
    map_grad = jnp.sum(map_grad.reshape(z_size, heads, own * 2 * cut), axis=0) / tokens
    map_grad = map_grad.reshape(row, heads // row, own, 2, cut).transpose(2, 3, 1, 0, 4)
    map_grad = map_grad.reshape(own, 2, heads, cut)
    attended, query_grad, key_grad, value_grad = call(
        unpack, [(ANY, shape(*queries.shape))] * 4, [(SMEM, place)] + [(VMEM, v) for v in pieces], [DMA((row, 4))])
    return attended, query_grad, key_grad, value_grad, map_grad


def solution(mesh):
    fine = Mesh(mesh.devices.reshape(8, 4, 2, 4), FINE)
    flat = P(CTX, "y")
    maps = P(CTX, None, None, "y")
    return jax.shard_map(
        body,
        mesh=fine,
        in_specs=(flat, flat, flat, flat, maps),
        out_specs=(flat, flat, flat, flat, maps),
        check_vma=False,
    )
```

time: 140 us -> 128 us (0.914)
  starting transfers between devices: 45.5 us -> 36.8 us
  Pallas kernels: 26.3 us -> 20.4 us
  local copies, waits for them, and re-layouts: 9.68 us -> 11.3 us
  waiting for transfers between devices: 13.2 us -> 14.8 us
    pallas_call x7 -> x6, Pallas kernels: 26.3 us -> 20.4 us  [call(): pl.pallas_call(kernel, out_shape=[s for _, s in outs], in_specs=[spec for...]
    all_to_all x1, starting transfers between devices: 12.2 us -> 7.57 us  [body(): map_grad = lax.all_to_all(map_grad, FINE, 0, 0, tiled=True)]
    ppermute x21 -> x14, starting transfers between devices: 29.7 us -> 25.7 us  [trade(): lax.ppermute(pieces[s], ROW, [(i, i ^ s) for i in range(count)])]
    unnamed x22, local copies, waits for them, and re-layouts: 6.42 us -> 8.07 us
    ppermute x21 -> x14, waiting for transfers between devices: 13.2 us -> 14.8 us  [trade(): lax.ppermute(pieces[s], ROW, [(i, i ^ s) for i in range(count)])]
  transfers between devices with their start and end apart: 23 -> 16, of which waited for: 5 -> 5; matrix products, arithmetic and copies ran while one was open for 2% -> 2% of each run, Pallas kernels for 11% -> 7%
where the time goes in v4:
time: 128 us; the launch traced here: 127 us
  blocking collectives  42.1 us (33%)
  starting transfers between devices  36.8 us (29%)
  Pallas kernels  20.4 us (16%)
  waiting for transfers between devices  14.8 us (12%)
  local copies, waits for them, and re-layouts  11.3 us (9%)
    ppermute x14, starting transfers between devices, trade(): lax.ppermute(pieces[s], ROW, [(i, i ^ s) for i in range(count)])  25.7 us
    all_to_all x1, blocking collectives, body(): maps = lax.all_to_all(maps, FINE, 0, 0, tiled=True)  24.6 us
    pallas_call x6, Pallas kernels, call(): pl.pallas_call(kernel, out_shape=[s for _, s in outs], in_specs=[spec for...  20.4 us
    all_to_all x1, blocking collectives, body(): state = lax.all_to_all(state, 'z', 0, 0, tiled=True)  17.5 us
    ppermute x14, waiting for transfers between devices, trade(): lax.ppermute(pieces[s], ROW, [(i, i ^ s) for i in range(count)])  14.8 us
    unnamed x22, local copies, waits for them, and re-layouts  8.07 us
    all_to_all x1, starting transfers between devices, body(): map_grad = lax.all_to_all(map_grad, FINE, 0, 0, tiled=True)  7.57 us
    all_to_all x1, starting transfers between devices, body(): total = lax.all_to_all(total, 'z', 0, 0, tiled=True)  3.6 us
  transfers between devices with their start and end apart: 16, of which 5 were waited for; matrix products, arithmetic and copies ran while one was open for 2% of the time, Pallas kernels for 7%

profile of v4, /device:TPU:1, one launch (start us, length us, event | category | flops | bytes accessed | tf_op | source)
XLA Modules:
  0.0 127.5 jit_solution(6432264831504961792)
XLA Ops:
  0.6 0.6 pad_add_fusion.place_ref
  1.3 3.5 %shard_map.92 = (bf16[4,256,128]{2,1,0:T(8,128)(2,1)}, bf16[4,256,128]{2,1,0:T(8,128)(2,1)}, bf16[4,256,128]{2,1,0:T(8,128)(2,1)}, bf16[4,256,128]{2,1,0:T(8,128...) custom-call(s32[2]{0:T(128)} %pad_add_fusion.place_ref, ...), custom_call_target="tpu_custom_call" | custom-call | flops 500000000 | bytes 2000000 | tf_op jit(solution)/shard_map/pallas_call | solution.py:302
  4.7 3.3 %collective-permute-start = (bf16[4,256,128]{2,1,0:T(8,128)(2,1)}, bf16[4,256,128]{2,1,0:T(8,128)(2,1)S(1)}, u32[]{:S(2)}, u32[]{:S(2)}) collective-permute-start(bf16[4,256,128]{2,1,0:T(8,128)(2,1)} %get-tuple-element.36), channel_id=1, source_target_pairs={{0,4},{4,0},{8,12},{12,8},{16,20},{20,16},{24,28},{28,24},{1,5},{5... | collective-permute-start | bytes 786440 | tf_op jit(solution)/shard_map/ppermute | solution.py:316
  8.1 1.7 %collective-permute-start.2 = (bf16[4,256,128]{2,1,0:T(8,128)(2,1)}, bf16[4,256,128]{2,1,0:T(8,128)(2,1)S(1)}, u32[]{:S(2)}, u32[]{:S(2)}) collective-permute-start(bf16[4,256,128]{2,1,0:T(8,128)(2,1)} %get-tuple-element.41), channel_id=1, source_target_pairs={{0,12},{4,8},{8,4},{12,0},{16,28},{20,24},{24,20},{28,16},{1,13},{... | collective-permute-start | bytes 786440 | tf_op jit(solution)/shard_map/ppermute | solution.py:316
  9.8 1.0 collective-permute-start.3
  10.8 2.3 %collective-permute-start.4 = (bf16[4,256,128]{2,1,0:T(8,128)(2,1)}, bf16[4,256,128]{2,1,0:T(8,128)(2,1)S(1)}, u32[]{:S(2)}, u32[]{:S(2)}) collective-permute-start(bf16[4,256,128]{2,1,0:T(8,128)(2,1)} %get-tuple-element.43), channel_id=1, source_target_pairs={{0,20},{4,16},{8,28},{12,24},{16,4},{20,0},{24,12},{28,8},{1,21},{... | collective-permute-start | bytes 786440 | tf_op jit(solution)/shard_map/ppermute | solution.py:316
  13.1 0.7 collective-permute-start.5
  13.9 2.3 %collective-permute-done.1.refs_2_ = bf16[4,256,128]{2,1,0:T(8,128)(2,1)S(1)} collective-permute-done((bf16[4,256,128]{2,1,0:T(8,128)(2,1)}, bf16[4,256,128]{2,1,0:T(8,128)(2,1)S(1)}, u32[]{:S(2)}, u32[]{:S(2)}) %collective-permute-start.1) | collective-permute-done | bytes 262176 | tf_op jit(solution)/shard_map/ppermute | solution.py:316
  16.2 2.0 %collective-permute-start.6 = (bf16[4,256,128]{2,1,0:T(8,128)(2,1)}, bf16[4,256,128]{2,1,0:T(8,128)(2,1)S(1)}, u32[]{:S(2)}, u32[]{:S(2)}) collective-permute-start(bf16[4,256,128]{2,1,0:T(8,128)(2,1)} %get-tuple-element.45), channel_id=1, source_target_pairs={{0,28},{4,24},{8,20},{12,16},{16,12},{20,8},{24,4},{28,0},{1,29},{... | collective-permute-start | bytes 786440 | tf_op jit(solution)/shard_map/ppermute | solution.py:316
  18.3 0.1 copy.27
  18.4 24.6 %all_to_all.28 = bf16[256,1,128]{2,1,0:T(2,128)(2,1)S(1)} all-to-all(bf16[256,1,128]{2,1,0:T(2,128)(2,1)S(1)} %copy.27), channel_id=1, replica_groups=mesh['z'=8,'x'=4,'core'=2,'y'=4] {'z','x','core','y'}, dimensions={0} | all-to-all | bytes 131072 | tf_op jit(solution)/shard_map/all_to_all | solution.py:347
  43.0 0.4 reduce
  43.3 0.2 reshape.50
  43.5 0.1 copy.28
  43.6 0.2 reshape.51.map_ref
  43.9 0.7 copy-done
  44.6 1.3 %shard_map.93 = (bf16[8,2,256,128]{3,2,1,0:T(8,128)(2,1)S(1)}, bf16[8,2,256,128]{3,2,1,0:T(8,128)(2,1)S(1)}, bf16[8,144,128]{2,1,0:T(8,128)(2,1)S(1)}) custom-call(s32[2]{0:T(128)S(1)} %copy-done.1, bf16[2,128,128]{2,1,0:T(8,128)(2,1)S(1)} %reshape.51.map_ref, bf16[4,256,128]{2,1,0:T(8,128)(2,1)S(1)} %copy-done, ...), custom_call_target="tpu_custom_call" | custom-call | flops 500000000 | bytes 2000000 | tf_op jit(solution)/shard_map/pallas_call | solution.py:302
  45.9 17.5 %all_to_all.29.sums_ref = bf16[8,144,128]{2,1,0:T(8,128)(2,1)S(1)} all-to-all(bf16[8,144,128]{2,1,0:T(8,128)(2,1)S(1)} %get-tuple-element.48), channel_id=1, replica_groups=mesh['z'=8,'x'=4,'core'=2,'y'=4] {'z'}, dimensions={0} | all-to-all | bytes 589824 | tf_op jit(solution)/shard_map/all_to_all | solution.py:352
  63.4 3.8 %shard_map.94 = bf16[8,144,128]{2,1,0:T(8,128)(2,1)} custom-call(s32[2]{0:T(128)S(1)} %copy-done.1, bf16[8,2,256,128]{3,2,1,0:T(8,128)(2,1)S(1)} %get-tuple-element.46.kv_ref, bf16[8,2,256,128]{3,2,1,0:T(8,128)(2,1)S(1)} %get-tuple-element.47.qd_ref, bf16[2,128,128]{2,1,0:T(8,128)(2,1)S(1)} %reshape.51.map_ref, bf16[8,144,128]{2,1,0:T(8,128)(2,1)S(1)} %all_to_all.29.sums_ref), custom_call_target="tpu_custom_call" | custom-call | flops 2000000000 | bytes 8000000 | tf_op jit(solution)/shard_map/pallas_call | solution.py:302
  67.2 1.0 copy-done.2
  68.2 3.6 %all-to-all-start.2 = ((bf16[8,144,128]{2,1,0:T(8,128)(2,1)}), bf16[8,144,128]{2,1,0:T(8,128)(2,1)S(1)}, u32[]{:S(2)}, u32[]{:S(2)}) async-start(bf16[8,144,128]{2,1,0:T(8,128)(2,1)} %shard_map.94), calls=%async_computation.2 | async-start | bytes 589824 | tf_op jit(solution)/shard_map/all_to_all | solution.py:356
  71.8 1.2 copy-done.3
  73.0 6.7 %shard_map.95 = (bf16[8,2,256,128]{3,2,1,0:T(8,128)(2,1)S(1)}, bf16[8,2,256,128]{3,2,1,0:T(8,128)(2,1)S(1)}, f32[128,128]{1,0:T(8,128)S(1)}) custom-call(s32[2]{0:T(128)S(1)} %copy-done.1, bf16[8,2,256,128]{3,2,1,0:T(8,128)(2,1)S(1)} %get-tuple-element.46.kv_ref, bf16[8,2,256,128]{3,2,1,0:T(8,128)(2,1)S(1)} %copy-done.3, ...), custom_call_target="tpu_custom_call" | custom-call | flops 3000000000 | bytes 12000000 | tf_op jit(solution)/shard_map/pallas_call | solution.py:302
  79.7 1.0 copy-done.6
  80.7 1.0 copy-done.8
  81.7 1.2 copy-done.7
  82.9 1.2 copy-done.9
  84.1 3.0 %shard_map.96 = (f32[128,128]{1,0:T(8,128)S(1)}, bf16[4,256,128]{2,1,0:T(8,128)(2,1)S(1)}, bf16[4,256,128]{2,1,0:T(8,128)(2,1)S(1)}, bf16[4,256,128]{2,1,0:T(8,1...) custom-call(s32[2]{0:T(128)S(1)} %copy-done.1, ...), custom_call_target="tpu_custom_call" | custom-call | flops 1500000000 | bytes 6000000 | tf_op jit(solution)/shard_map/pallas_call | solution.py:302
  87.2 0.7 copy-done.4
  87.9 3.5 %collective-permute-start.7 = (bf16[4,256,128]{2,1,0:T(8,128)(2,1)S(1)}, bf16[4,256,128]{2,1,0:T(8,128)(2,1)S(1)}, u32[]{:S(2)}, u32[]{:S(2)}) collective-permute-start(bf16[4,256,128]{2,1,0:T(8,128)(2,1)S(1)} %get-tuple-element.54), channel_id=1, source_target_pairs={{0,4},{4,0},{8,12},{12,8},{16,20},{20,16},{24,28},{28,24},{1,5},{5... | collective-permute-start | bytes 786440 | tf_op jit(solution)/shard_map/ppermute | solution.py:316
  91.4 0.2 stack.21
  91.5 0.2 stack.22
  91.7 1.7 %collective-permute-start.9 = (bf16[4,256,128]{2,1,0:T(8,128)(2,1)}, bf16[4,256,128]{2,1,0:T(8,128)(2,1)S(1)}, u32[]{:S(2)}, u32[]{:S(2)}) collective-permute-start(bf16[4,256,128]{2,1,0:T(8,128)(2,1)} %get-tuple-element.57), channel_id=1, source_target_pairs={{0,12},{4,8},{8,4},{12,0},{16,28},{20,24},{24,20},{28,16},{1,13},{... | collective-permute-start | bytes 786440 | tf_op jit(solution)/shard_map/ppermute | solution.py:316
  93.4 2.1 %collective-permute-start.10 = (bf16[4,256,128]{2,1,0:T(8,128)(2,1)}, bf16[4,256,128]{2,1,0:T(8,128)(2,1)S(1)}, u32[]{:S(2)}, u32[]{:S(2)}) collective-permute-start(bf16[4,256,128]{2,1,0:T(8,128)(2,1)} %get-tuple-element.58), channel_id=1, source_target_pairs={{0,16},{4,20},{8,24},{12,28},{16,0},{20,4},{24,8},{28,12},{1,17},{... | collective-permute-start | bytes 786440 | tf_op jit(solution)/shard_map/ppermute | solution.py:316
  95.6 1.2 collective-permute-start.11
  96.8 2.5 %collective-permute-start.12 = (bf16[4,256,128]{2,1,0:T(8,128)(2,1)S(1)}, bf16[4,256,128]{2,1,0:T(8,128)(2,1)S(1)}, u32[]{:S(2)}, u32[]{:S(2)}) collective-permute-start(bf16[4,256,128]{2,1,0:T(8,128)(2,1)S(1)} %copy-done.5), channel_id=1, source_target_pairs={{0,24},{4,28},{8,16},{12,20},{16,8},{20,12},{24,0},{28,4},{1,25},{... | collective-permute-start | bytes 786440 | tf_op jit(solution)/shard_map/ppermute | solution.py:316
  99.3 0.2 collective-permute-done.8.refs_2_
  99.5 3.5 %collective-permute-start.13 = (bf16[4,256,128]{2,1,0:T(8,128)(2,1)S(1)}, bf16[4,256,128]{2,1,0:T(8,128)(2,1)S(1)}, u32[]{:S(2)}, u32[]{:S(2)}) collective-permute-start(bf16[4,256,128]{2,1,0:T(8,128)(2,1)S(1)} %get-tuple-element.61), channel_id=1, source_target_pairs={{0,28},{4,24},{8,20},{12,16},{16,12},{20,8},{24,4},{28,0},{1,29},{... | collective-permute-start | bytes 786440 | tf_op jit(solution)/shard_map/ppermute | solution.py:316
  103.1 0.1 maximum_bitcast_fusion
  103.2 0.4 copy.29
  103.6 1.1 reshape.52
  104.7 7.6 %all-to-all-start.3 = ((f32[256,1,128]{2,1,0:T(1,128)}), f32[256,1,128]{2,1,0:T(1,128)S(1)}, u32[]{:S(2)}, u32[]{:S(2)}) async-start(f32[256,1,128]{2,1,0:T(1,128)} %bitcast.10), calls=%async_computation.3 | async-start | bytes 262144 | tf_op jit(solution)/shard_map/all_to_all | solution.py:369
  112.3 0.7 collective-permute-done.10.refs_4_
  113.0 6.7 %collective-permute-done.11.refs_5_ = bf16[4,256,128]{2,1,0:T(8,128)(2,1)S(1)} collective-permute-done((bf16[4,256,128]{2,1,0:T(8,128)(2,1)}, bf16[4,256,128]{2,1,0:T(8,128)(2,1)S(1)}, u32[]{:S(2)}, u32[]{:S(2)}) %collective-permute-start.11) | collective-permute-done | bytes 262176 | tf_op jit(solution)/shard_map/ppermute | solution.py:316
  119.7 4.9 %collective-permute-done.13.refs_7_ = bf16[4,256,128]{2,1,0:T(8,128)(2,1)S(1)} collective-permute-done((bf16[4,256,128]{2,1,0:T(8,128)(2,1)S(1)}, bf16[4,256,128]{2,1,0:T(8,128)(2,1)S(1)}, u32[]{:S(2)}, u32[]{:S(2)}) %collective-permute-start.13) | collective-permute-done | bytes 262176 | tf_op jit(solution)/shard_map/ppermute | solution.py:316
  124.5 2.1 %shard_map.97 = (bf16[256,1024]{1,0:T(8,128)(2,1)}, bf16[256,1024]{1,0:T(8,128)(2,1)}, bf16[256,1024]{1,0:T(8,128)(2,1)}, bf16[256,1024]{1,0:T(8,128)(2,1)}) custom-call(s32[2]{0:T(128)S(1)} %copy-done.1, bf16[4,256,128]{2,1,0:T(8,128)(2,1)S(1)} %get-tuple-element.51.refs_0_, bf16[4,256,128]{2,1,0:T(8,128)(2,1)S(1)} %collective-permute-done.7.refs_1_, ...), custom_call_target="tpu_custom_call" | custom-call | flops 500000000 | bytes 2000000 | tf_op jit(solution)/shard_map/pallas_call | solution.py:302
  126.7 0.1 div.10
  126.8 0.7 copy.33
  (33 shorter events, 0.2 us)
Async XLA Ops:
  1.3 16.9 %copy-start.10 = (bf16[2,2,32,32]{3,2,1,0:T(8,128)(2,1)S(1)}, bf16[2,2,32,32]{3,2,1,0:T(8,128)(2,1)}, u32[]{:S(2)}) copy-start(bf16[2,2,32,32]{3,2,1,0:T(8,128)(2,1)} %param.9) | copy-start | bytes 24580
  4.7 8.4 %collective-permute-start = (bf16[4,256,128]{2,1,0:T(8,128)(2,1)}, bf16[4,256,128]{2,1,0:T(8,128)(2,1)S(1)}, u32[]{:S(2)}, u32[]{:S(2)}) collective-permute-start(bf16[4,256,128]{2,1,0:T(8,128)(2,1)} %get-tuple-element.36), channel_id=1, source_target_pairs={{0,4},{4,0},{8,12},{12,8},{16,20},{20,16},{24,28},{28,24},{1,5},{5... | collective-permute-start | bytes 786440 | tf_op jit(solution)/shard_map/ppermute | solution.py:316
  8.1 8.1 %collective-permute-start.1 = (bf16[4,256,128]{2,1,0:T(8,128)(2,1)}, bf16[4,256,128]{2,1,0:T(8,128)(2,1)S(1)}, u32[]{:S(2)}, u32[]{:S(2)}) collective-permute-start(bf16[4,256,128]{2,1,0:T(8,128)(2,1)} %get-tuple-element.40), channel_id=1, source_target_pairs={{0,8},{4,12},{8,0},{12,4},{16,24},{20,28},{24,16},{28,20},{1,9},{5... | collective-permute-start | bytes 786440 | tf_op jit(solution)/shard_map/ppermute | solution.py:316
  8.1 35.7 %collective-permute-start.2 = (bf16[4,256,128]{2,1,0:T(8,128)(2,1)}, bf16[4,256,128]{2,1,0:T(8,128)(2,1)S(1)}, u32[]{:S(2)}, u32[]{:S(2)}) collective-permute-start(bf16[4,256,128]{2,1,0:T(8,128)(2,1)} %get-tuple-element.41), channel_id=1, source_target_pairs={{0,12},{4,8},{8,4},{12,0},{16,28},{20,24},{24,20},{28,16},{1,13},{... | collective-permute-start | bytes 786440 | tf_op jit(solution)/shard_map/ppermute | solution.py:316
  9.8 34.0 %collective-permute-start.3 = (bf16[4,256,128]{2,1,0:T(8,128)(2,1)}, bf16[4,256,128]{2,1,0:T(8,128)(2,1)S(1)}, u32[]{:S(2)}, u32[]{:S(2)}) collective-permute-start(bf16[4,256,128]{2,1,0:T(8,128)(2,1)} %get-tuple-element.42), channel_id=1, source_target_pairs={{0,16},{4,20},{8,24},{12,28},{16,0},{20,4},{24,8},{28,12},{1,17},{... | collective-permute-start | bytes 786440 | tf_op jit(solution)/shard_map/ppermute | solution.py:316
  10.8 33.0 %collective-permute-start.4 = (bf16[4,256,128]{2,1,0:T(8,128)(2,1)}, bf16[4,256,128]{2,1,0:T(8,128)(2,1)S(1)}, u32[]{:S(2)}, u32[]{:S(2)}) collective-permute-start(bf16[4,256,128]{2,1,0:T(8,128)(2,1)} %get-tuple-element.43), channel_id=1, source_target_pairs={{0,20},{4,16},{8,28},{12,24},{16,4},{20,0},{24,12},{28,8},{1,21},{... | collective-permute-start | bytes 786440 | tf_op jit(solution)/shard_map/ppermute | solution.py:316
  13.1 30.7 %collective-permute-start.5 = (bf16[4,256,128]{2,1,0:T(8,128)(2,1)}, bf16[4,256,128]{2,1,0:T(8,128)(2,1)S(1)}, u32[]{:S(2)}, u32[]{:S(2)}) collective-permute-start(bf16[4,256,128]{2,1,0:T(8,128)(2,1)} %get-tuple-element.44), channel_id=1, source_target_pairs={{0,24},{4,28},{8,16},{12,20},{16,8},{20,12},{24,0},{28,4},{1,25},{... | collective-permute-start | bytes 786440 | tf_op jit(solution)/shard_map/ppermute | solution.py:316
  16.2 27.7 %collective-permute-start.6 = (bf16[4,256,128]{2,1,0:T(8,128)(2,1)}, bf16[4,256,128]{2,1,0:T(8,128)(2,1)S(1)}, u32[]{:S(2)}, u32[]{:S(2)}) collective-permute-start(bf16[4,256,128]{2,1,0:T(8,128)(2,1)} %get-tuple-element.45), channel_id=1, source_target_pairs={{0,28},{4,24},{8,20},{12,16},{16,12},{20,8},{24,4},{28,0},{1,29},{... | collective-permute-start | bytes 786440 | tf_op jit(solution)/shard_map/ppermute | solution.py:316
  43.6 1.0 copy-start
  43.8 0.8 copy-start.1
  67.2 1.0 copy-start.2
  68.2 13.5 %all-to-all-start.2 = ((bf16[8,144,128]{2,1,0:T(8,128)(2,1)}), bf16[8,144,128]{2,1,0:T(8,128)(2,1)S(1)}, u32[]{:S(2)}, u32[]{:S(2)}) async-start(bf16[8,144,128]{2,1,0:T(8,128)(2,1)} %shard_map.94), calls=%async_computation.2 | async-start | bytes 589824 | tf_op jit(solution)/shard_map/all_to_all | solution.py:356
  71.8 1.2 copy-start.3
  79.7 1.0 copy-start.6
  80.7 1.0 copy-start.8
  81.7 1.2 copy-start.7
  82.9 1.2 copy-start.9
  87.2 0.7 copy-start.4
  87.9 8.9 %collective-permute-start.7 = (bf16[4,256,128]{2,1,0:T(8,128)(2,1)S(1)}, bf16[4,256,128]{2,1,0:T(8,128)(2,1)S(1)}, u32[]{:S(2)}, u32[]{:S(2)}) collective-permute-start(bf16[4,256,128]{2,1,0:T(8,128)(2,1)S(1)} %get-tuple-element.54), channel_id=1, source_target_pairs={{0,4},{4,0},{8,12},{12,8},{16,20},{20,16},{24,28},{28,24},{1,5},{5... | collective-permute-start | bytes 786440 | tf_op jit(solution)/shard_map/ppermute | solution.py:316
  91.4 8.1 %collective-permute-start.8 = (bf16[4,256,128]{2,1,0:T(8,128)(2,1)}, bf16[4,256,128]{2,1,0:T(8,128)(2,1)S(1)}, u32[]{:S(2)}, u32[]{:S(2)}) collective-permute-start(bf16[4,256,128]{2,1,0:T(8,128)(2,1)} %get-tuple-element.56), channel_id=1, source_target_pairs={{0,8},{4,12},{8,0},{12,4},{16,24},{20,28},{24,16},{28,20},{1,9},{5... | collective-permute-start | bytes 786440 | tf_op jit(solution)/shard_map/ppermute | solution.py:316
  91.4 5.4 %copy-start.5 = (bf16[4,256,128]{2,1,0:T(8,128)(2,1)S(1)}, bf16[4,256,128]{2,1,0:T(8,128)(2,1)}, u32[]{:S(2)}) copy-start(bf16[4,256,128]{2,1,0:T(8,128)(2,1)} %copy-done.4) | copy-start | bytes 786436
  91.7 20.6 %collective-permute-start.9 = (bf16[4,256,128]{2,1,0:T(8,128)(2,1)}, bf16[4,256,128]{2,1,0:T(8,128)(2,1)S(1)}, u32[]{:S(2)}, u32[]{:S(2)}) collective-permute-start(bf16[4,256,128]{2,1,0:T(8,128)(2,1)} %get-tuple-element.57), channel_id=1, source_target_pairs={{0,12},{4,8},{8,4},{12,0},{16,28},{20,24},{24,20},{28,16},{1,13},{... | collective-permute-start | bytes 786440 | tf_op jit(solution)/shard_map/ppermute | solution.py:316
  93.4 19.6 %collective-permute-start.10 = (bf16[4,256,128]{2,1,0:T(8,128)(2,1)}, bf16[4,256,128]{2,1,0:T(8,128)(2,1)S(1)}, u32[]{:S(2)}, u32[]{:S(2)}) collective-permute-start(bf16[4,256,128]{2,1,0:T(8,128)(2,1)} %get-tuple-element.58), channel_id=1, source_target_pairs={{0,16},{4,20},{8,24},{12,28},{16,0},{20,4},{24,8},{28,12},{1,17},{... | collective-permute-start | bytes 786440 | tf_op jit(solution)/shard_map/ppermute | solution.py:316
  95.6 24.1 %collective-permute-start.11 = (bf16[4,256,128]{2,1,0:T(8,128)(2,1)}, bf16[4,256,128]{2,1,0:T(8,128)(2,1)S(1)}, u32[]{:S(2)}, u32[]{:S(2)}) collective-permute-start(bf16[4,256,128]{2,1,0:T(8,128)(2,1)} %get-tuple-element.59), channel_id=1, source_target_pairs={{0,20},{4,16},{8,28},{12,24},{16,4},{20,0},{24,12},{28,8},{1,21},{... | collective-permute-start | bytes 786440 | tf_op jit(solution)/shard_map/ppermute | solution.py:316
  96.8 22.9 %collective-permute-start.12 = (bf16[4,256,128]{2,1,0:T(8,128)(2,1)S(1)}, bf16[4,256,128]{2,1,0:T(8,128)(2,1)S(1)}, u32[]{:S(2)}, u32[]{:S(2)}) collective-permute-start(bf16[4,256,128]{2,1,0:T(8,128)(2,1)S(1)} %copy-done.5), channel_id=1, source_target_pairs={{0,24},{4,28},{8,16},{12,20},{16,8},{20,12},{24,0},{28,4},{1,25},{... | collective-permute-start | bytes 786440 | tf_op jit(solution)/shard_map/ppermute | solution.py:316
  99.5 25.0 %collective-permute-start.13 = (bf16[4,256,128]{2,1,0:T(8,128)(2,1)S(1)}, bf16[4,256,128]{2,1,0:T(8,128)(2,1)S(1)}, u32[]{:S(2)}, u32[]{:S(2)}) collective-permute-start(bf16[4,256,128]{2,1,0:T(8,128)(2,1)S(1)} %get-tuple-element.61), channel_id=1, source_target_pairs={{0,28},{4,24},{8,20},{12,16},{16,12},{20,8},{24,4},{28,0},{1,29},{... | collective-permute-start | bytes 786440 | tf_op jit(solution)/shard_map/ppermute | solution.py:316
  104.7 21.9 %all-to-all-start.3 = ((f32[256,1,128]{2,1,0:T(1,128)}), f32[256,1,128]{2,1,0:T(1,128)S(1)}, u32[]{:S(2)}, u32[]{:S(2)}) async-start(f32[256,1,128]{2,1,0:T(1,128)} %bitcast.10), calls=%async_computation.3 | async-start | bytes 262144 | tf_op jit(solution)/shard_map/all_to_all | solution.py:369

commit v5 on v4

--- a/solution.py
+++ b/solution.py
@@ -20,6 +20,8 @@
 PART = BF16
 STATE_ROWS = HEAD_DIM + 16
 GROUP = 4
+OUTER_LIMIT = 32
+HELD = 40
 
 
 def mm(a, b):
@@ -77,11 +79,12 @@
     low_ref[b] = low
 
 
-def pack(place_ref, *refs):
+def pack(*refs):
+    me = lax.axis_index(ROW)
     ins, outs, (held, in_sem, out_sem) = refs[:4], refs[4:-3], refs[-3:]
     loads, stores = [], []
     for s in range(len(outs)):
-        column = pl.ds(pl.multiple_of((place_ref[1] ^ s) * HEAD_DIM, HEAD_DIM), HEAD_DIM)
+        column = pl.ds(pl.multiple_of((me ^ s) * HEAD_DIM, HEAD_DIM), HEAD_DIM)
         for n, ref in enumerate(ins):
             loads.append(pltpu.make_async_copy(ref.at[:, column], held.at[s, n], in_sem.at[s, n]))
         stores.append(pltpu.make_async_copy(held.at[s], outs[s], out_sem.at[s]))
@@ -111,17 +114,18 @@
 def key_state(place_ref, map_ref, *refs):
     pieces, (kv_ref, qd_ref, out_ref) = refs[:-3], refs[-3:]
     blocks = len(pieces)
+    me = place_ref[1]
     for s, piece in enumerate(pieces):
-        kv_ref[place_ref[1] ^ s] = piece[:2]
-        qd_ref[place_ref[1] ^ s] = piece[2:]
+        kv_ref[me ^ s] = piece[:2]
+        qd_ref[me ^ s] = piece[2:]
     key_map = turned(map_ref[1])
     total = jnp.zeros((HEAD_DIM, 2 * HEAD_DIM), F32)
     mean = jnp.zeros((1, HEAD_DIM), F32)
-    feats = [feature(mm_nt(key_map, kv_ref[b, 0])).astype(BF16) for b in range(blocks)]
-    for b in range(blocks):
-        value = kv_ref[b, 1]
+    feats = [feature(mm_nt(key_map, piece[0])).astype(BF16) for piece in pieces]
+    for feat, piece in zip(feats, pieces):
+        value = piece[1]
         mean = mean + jnp.sum(value.astype(F32), axis=0, keepdims=True)
-        total = total + mm(feats[b], with_ones(value))
+        total = total + mm(feat, with_ones(value))
     centre = (mean * (1.0 / (blocks * BLOCK))).astype(BF16).astype(F32)
     column = total[:, HEAD_DIM:]
     state = (total[:, :HEAD_DIM] - column * centre).astype(BF16)
@@ -149,10 +153,9 @@
     return prior + mm_tn(jnp.concatenate(norms, axis=0).astype(BF16), centres)
 
 
-def key_stage(place, kv_ref, map_ref, sums_ref, highs, lows):
+def key_stage(prior, kv_ref, map_ref, highs, lows):
     blocks = kv_ref.shape[0]
     key_map = turned(map_ref[1])
-    prior = prior_of(place, sums_ref)
     feats = [feature(mm_nt(key_map, kv_ref[b, 0])).astype(BF16) for b in range(blocks)]
     states = [mm(feats[b], with_ones(kv_ref[b, 1])) for b in range(blocks)]
     for b in range(blocks):
@@ -178,9 +181,11 @@
     return [range(b, min(b + GROUP, blocks)) for b in range(0, blocks, GROUP)]
 
 
-def forward(place_ref, kv_ref, qd_ref, map_ref, sums_ref, out_ref, highs, lows):
+def forward(place_ref, kv_ref, qd_ref, map_ref, sums_ref, out_ref, prior_ref, highs, lows):
     blocks = kv_ref.shape[0]
-    feats = key_stage(place_ref[0], kv_ref, map_ref, sums_ref, highs, lows)
+    prior = prior_of(place_ref[0], sums_ref)
+    prior_ref[...] = prior
+    feats = key_stage(prior, kv_ref, map_ref, highs, lows)
     query_map = turned(map_ref[0])
     causal = causal_mask()
     lane = lanes(BLOCK)
@@ -206,10 +211,11 @@
         out_ref[z, HEAD_DIM:] = norms
 
 
-def inner(place_ref, kv_ref, qd_ref, map_ref, sums_ref, aq_ref, part_ref, map_grad_ref,
-          highs, lows, insides, adjoints, fks):
+def inner(kv_ref, qd_ref, map_ref, prior_ref, aq_ref, part_ref, map_grad_ref,
+          highs, lows, insides, adjoints, fks, aq, sem):
     blocks = kv_ref.shape[0]
-    feats = key_stage(place_ref[0], kv_ref, map_ref, sums_ref, highs, lows)
+    feats = key_stage(prior_ref[...], kv_ref, map_ref, highs, lows)
+    stores = [pltpu.make_async_copy(aq.at[b], aq_ref.at[0, b], sem.at[b]) for b in range(blocks)]
     query_map = turned(map_ref[0])
     causal = causal_mask()
     rows = lax.broadcasted_iota(jnp.int32, (BLOCK, BLOCK), 0)
@@ -242,8 +248,9 @@
                   for b, g, d, k in zip(group, grads, dscore, feat_k)]
         dpre = [(d * jnp.minimum(f.astype(F32), 1.0)).astype(BF16) for d, f in zip(d_feat, feat_q)]
         for n, b in enumerate(group):
-            aq_ref[b, 0] = attended[n].astype(BF16)
-            aq_ref[b, 1] = mm_nt(dpre[n], map_ref[0]).astype(BF16)
+            aq[b, 0] = attended[n].astype(BF16)
+            aq[b, 1] = mm_nt(dpre[n], map_ref[0]).astype(BF16)
+            stores[b].start()
             map_grad = map_grad + mm_tn(qd_ref[b, 0], dpre[n])
             insides[b, 0] = mm(dscore_t[n], feat_q[n])
             insides[b, 1] = mm(weight_t[n], halfs[n])
@@ -261,10 +268,17 @@
         part_ref[b, 0] = (mm_nt(wide, highs[b]) + mm_nt(wide, lows[b]) + insides[b, 0]).astype(PART)
         stacked = jnp.concatenate([highs[b, :, :HEAD_DIM], lows[b, :, :HEAD_DIM]], axis=0)
         part_ref[b, 1] = (mm(jnp.concatenate([feat_k, feat_k], axis=1), stacked) + insides[b, 1]).astype(PART)
-
-
-def outer(place_ref, kv_ref, map_ref, sums_ref, aq_ref, part_ref, out_ref, *pieces):
+    for store in stores:
+        store.wait()
+
+
+def outer(place_ref, kv_ref, map_ref, sums_ref, aq_ref, part_ref, out_ref, *refs):
+    pieces, sem = refs[:-1], refs[-1]
     place = place_ref[0]
+    copies = [pltpu.make_async_copy(aq_ref.at[0, place_ref[1] ^ s], piece.at[pl.ds(0, 2)], sem.at[s])
+              for s, piece in enumerate(pieces)]
+    for copy in copies:
+        copy.start()
     after = jnp.zeros((HEAD_DIM, HEAD_DIM), F32)
     norms = []
     for z in range(sums_ref.shape[0]):
@@ -287,11 +301,12 @@
         d_value = [mm(jnp.concatenate([f, f], axis=1), stacked) + part_ref[b, 1].astype(F32)
                    for b, f in zip(at, feat_k)]
         for n, s in enumerate(group):
-            pieces[s][:2] = aq_ref[at[n]]
             pieces[s][2] = mm_nt(dpre[n], map_ref[1]).astype(BF16)
             pieces[s][3] = d_value[n].astype(BF16)
             map_grad = map_grad + mm_tn(kv_ref[at[n], 0], dpre[n])
     out_ref[...] = map_grad
+    for copy in copies:
+        copy.wait()
 
 
 def shape(*dims, dtype=BF16):
@@ -339,7 +354,7 @@
     square = (VMEM, shape(HEAD_DIM, HEAD_DIM, dtype=F32))
 
     pieces = call(
-        pack, [(ANY, shape(*four))] * row, [(SMEM, place)] + [(ANY, v) for v in (keys, values, queries, out_grad)],
+        pack, [(ANY, shape(*four))] * row, [(ANY, v) for v in (keys, values, queries, out_grad)],
         [scratch((row, *four), BF16), DMA((row, 4)), DMA((row,))], limit=60)
     pieces = trade(pieces)
     maps = gather_maps(feature_weights)
@@ -350,17 +365,22 @@
     kv, qd, state = call(
         key_state, [paired, paired, sums], [(SMEM, place), (VMEM, maps)] + [(VMEM, v) for v in pieces])
     state = lax.all_to_all(state, "z", 0, 0, tiled=True)
-    held = [(SMEM, place), (VMEM, kv), (VMEM, qd), (VMEM, maps), (VMEM, state)]
     halved = [scratch((row, HEAD_DIM, 2 * HEAD_DIM), BF16)] * 2
-    (total,) = call(forward, [sums], held, halved, cycles=4)
+    total, prior = call(
+        forward, [sums, (VMEM, shape(HEAD_DIM, 2 * HEAD_DIM, dtype=F32))],
+        [(SMEM, place), (VMEM, kv), (VMEM, qd), (VMEM, maps), (VMEM, state)], halved, cycles=4)
     total = lax.all_to_all(total, "z", 0, 0, tiled=True)
     aq, part, map_grad_q = call(
-        inner, [paired, (VMEM, shape(row, 2, BLOCK, HEAD_DIM, dtype=PART)), square], held,
+        inner,
+        [(ANY, shape(HELD, row, 2, BLOCK, HEAD_DIM)), (VMEM, shape(row, 2, BLOCK, HEAD_DIM, dtype=PART)), square],
+        [(VMEM, kv), (VMEM, qd), (VMEM, maps), (VMEM, prior)],
         halved + [scratch((row, 2, BLOCK, HEAD_DIM), F32), scratch((row, HEAD_DIM, 2 * HEAD_DIM), F32),
-                  scratch((row, BLOCK, HEAD_DIM), BF16)], cycles=6)
+                  scratch((row, BLOCK, HEAD_DIM), BF16), scratch((row, 2, BLOCK, HEAD_DIM), BF16), DMA((row,))],
+        cycles=6)
     map_grad_k, *pieces = call(
         outer, [square] + [(VMEM, shape(*four))] * row,
-        [(SMEM, place), (VMEM, kv), (VMEM, maps), (VMEM, total), (VMEM, aq), (VMEM, part)], cycles=3)
+        [(SMEM, place), (VMEM, kv), (VMEM, maps), (VMEM, total), (ANY, aq), (VMEM, part)],
+        [DMA((row,))], cycles=3, limit=OUTER_LIMIT)
     pieces = trade(pieces)
 
     map_grad = jnp.stack((map_grad_q, map_grad_k)).reshape(2, z_size * row, own, heads // row, cut)

time: 128 us -> 125 us (0.977)
  blocking collectives: 42.1 us -> 16 us
  waiting for transfers between devices: 14.8 us -> 31.8 us
  starting transfers between devices: 36.8 us -> 46.9 us
  local copies, waits for them, and re-layouts: 11.3 us -> 8.91 us
    all_to_all x1 -> x0, blocking collectives: 24.6 us -> none  [body(): maps = lax.all_to_all(maps, FINE, 0, 0, tiled=True)]
    all_to_all x0 -> x1, waiting for transfers between devices: none -> 12.6 us  [body(): maps = lax.all_to_all(maps, FINE, 0, 0, tiled=True)]
    all_to_all x0 -> x1, starting transfers between devices: none -> 12 us  [body(): maps = lax.all_to_all(maps, FINE, 0, 0, tiled=True)]
    unnamed x22 -> x12, local copies, waits for them, and re-layouts: 8.07 us -> 4.27 us
    ppermute x14, waiting for transfers between devices: 14.8 us -> 17.2 us  [trade(): lax.ppermute(pieces[s], ROW, [(i, i ^ s) for i in range(count)])]
    all_to_all x1, starting transfers between devices: 7.57 us -> 5.16 us  [body(): map_grad = lax.all_to_all(map_grad, FINE, 0, 0, tiled=True)]
    all_to_all x1, waiting for transfers between devices: 0.01 us -> 2.03 us  [body(): total = lax.all_to_all(total, 'z', 0, 0, tiled=True)]
    all_to_all x1, blocking collectives: 17.5 us -> 16 us  [body(): state = lax.all_to_all(state, 'z', 0, 0, tiled=True)]
  transfers between devices with their start and end apart: 16 -> 17, of which waited for: 5 -> 7; matrix products, arithmetic and copies ran while one was open for 2% -> 4% of each run, Pallas kernels for 7% -> 7%
where the time goes in v5:
time: 125 us
  starting transfers between devices  46.9 us (38%)
  waiting for transfers between devices  31.8 us (25%)
  Pallas kernels  19.7 us (16%)
  blocking collectives  16 us (13%)
  local copies, waits for them, and re-layouts  8.91 us (7%)
    ppermute x14, starting transfers between devices, trade(): lax.ppermute(pieces[s], ROW, [(i, i ^ s) for i in range(count)])  26.1 us
    pallas_call x6, Pallas kernels, call(): pl.pallas_call(kernel, out_shape=[s for _, s in outs], in_specs=[spec for...  19.7 us
    ppermute x14, waiting for transfers between devices, trade(): lax.ppermute(pieces[s], ROW, [(i, i ^ s) for i in range(count)])  17.2 us
    all_to_all x1, blocking collectives, body(): state = lax.all_to_all(state, 'z', 0, 0, tiled=True)  16 us
    all_to_all x1, waiting for transfers between devices, body(): maps = lax.all_to_all(maps, FINE, 0, 0, tiled=True)  12.6 us
    all_to_all x1, starting transfers between devices, body(): maps = lax.all_to_all(maps, FINE, 0, 0, tiled=True)  12 us
    all_to_all x1, starting transfers between devices, body(): map_grad = lax.all_to_all(map_grad, FINE, 0, 0, tiled=True)  5.16 us
    unnamed x12, local copies, waits for them, and re-layouts  4.27 us
  transfers between devices with their start and end apart: 17, of which 7 were waited for; matrix products, arithmetic and copies ran while one was open for 4% of the time, Pallas kernels for 7%

profile of v5, /device:TPU:1, one launch (start us, length us, event | category | flops | bytes accessed | tf_op | source)
XLA Modules:
  0.0 124.8 jit_solution(11117736646881317753)
XLA Ops:
  0.6 2.7 %shard_map.92 = (bf16[4,256,128]{2,1,0:T(8,128)(2,1)}, bf16[4,256,128]{2,1,0:T(8,128)(2,1)}, bf16[4,256,128]{2,1,0:T(8,128)(2,1)}, bf16[4,256,128]{2,1,0:T(8,128...) custom-call(bf16[256,1024]{1,0:T(8,128)(2,1)} %refs_0_.1, ...), custom_call_target="tpu_custom_call" | custom-call | flops 500000000 | bytes 2000000 | tf_op jit(solution)/shard_map/pallas_call | solution.py:317
  3.3 3.3 %collective-permute-start = (bf16[4,256,128]{2,1,0:T(8,128)(2,1)}, bf16[4,256,128]{2,1,0:T(8,128)(2,1)S(1)}, u32[]{:S(2)}, u32[]{:S(2)}) collective-permute-start(bf16[4,256,128]{2,1,0:T(8,128)(2,1)} %get-tuple-element.38), channel_id=1, source_target_pairs={{0,4},{4,0},{8,12},{12,8},{16,20},{20,16},{24,28},{28,24},{1,5},{5... | collective-permute-start | bytes 786440 | tf_op jit(solution)/shard_map/ppermute | solution.py:331
  6.7 1.7 %collective-permute-start.2 = (bf16[4,256,128]{2,1,0:T(8,128)(2,1)}, bf16[4,256,128]{2,1,0:T(8,128)(2,1)S(1)}, u32[]{:S(2)}, u32[]{:S(2)}) collective-permute-start(bf16[4,256,128]{2,1,0:T(8,128)(2,1)} %get-tuple-element.43), channel_id=1, source_target_pairs={{0,12},{4,8},{8,4},{12,0},{16,28},{20,24},{24,20},{28,16},{1,13},{... | collective-permute-start | bytes 786440 | tf_op jit(solution)/shard_map/ppermute | solution.py:331
  8.4 1.0 collective-permute-start.3
  9.4 2.3 %collective-permute-start.4 = (bf16[4,256,128]{2,1,0:T(8,128)(2,1)}, bf16[4,256,128]{2,1,0:T(8,128)(2,1)S(1)}, u32[]{:S(2)}, u32[]{:S(2)}) collective-permute-start(bf16[4,256,128]{2,1,0:T(8,128)(2,1)} %get-tuple-element.45), channel_id=1, source_target_pairs={{0,20},{4,16},{8,28},{12,24},{16,4},{20,0},{24,12},{28,8},{1,21},{... | collective-permute-start | bytes 786440 | tf_op jit(solution)/shard_map/ppermute | solution.py:331
  11.7 0.7 collective-permute-start.5
  12.4 2.3 %collective-permute-done.1.refs_2_ = bf16[4,256,128]{2,1,0:T(8,128)(2,1)S(1)} collective-permute-done((bf16[4,256,128]{2,1,0:T(8,128)(2,1)}, bf16[4,256,128]{2,1,0:T(8,128)(2,1)S(1)}, u32[]{:S(2)}, u32[]{:S(2)}) %collective-permute-start.1) | collective-permute-done | bytes 262176 | tf_op jit(solution)/shard_map/ppermute | solution.py:331
  14.7 2.0 %collective-permute-start.6 = (bf16[4,256,128]{2,1,0:T(8,128)(2,1)}, bf16[4,256,128]{2,1,0:T(8,128)(2,1)S(1)}, u32[]{:S(2)}, u32[]{:S(2)}) collective-permute-start(bf16[4,256,128]{2,1,0:T(8,128)(2,1)} %get-tuple-element.47), channel_id=1, source_target_pairs={{0,28},{4,24},{8,20},{12,16},{16,12},{20,8},{24,4},{28,0},{1,29},{... | collective-permute-start | bytes 786440 | tf_op jit(solution)/shard_map/ppermute | solution.py:331
  16.7 0.8 copy.25
  17.5 0.1 reshape.48
  17.6 0.8 copy.27
  18.4 12.0 %all-to-all-start = ((bf16[256,1,128]{2,1,0:T(2,128)(2,1)}), bf16[256,1,128]{2,1,0:T(2,128)(2,1)S(1)}, u32[]{:S(2)}, u32[]{:S(2)}) async-start(bf16[256,1,128]{2,1,0:T(2,128)(2,1)} %copy.27), calls=%async_computation | async-start | bytes 262144 | tf_op jit(solution)/shard_map/all_to_all | solution.py:362
  30.5 12.6 %all-to-all-done = bf16[256,1,128]{2,1,0:T(2,128)(2,1)S(1)} async-done(((bf16[256,1,128]{2,1,0:T(2,128)(2,1)}), bf16[256,1,128]{2,1,0:T(2,128)(2,1)S(1)}, u32[]{:S(2)}, u32[]{:S(2)}) %all-to-all-start) | async-done | bytes 65568 | tf_op jit(solution)/shard_map/all_to_all | solution.py:362
  43.1 0.4 reduce
  43.4 0.2 reshape.50
  43.6 0.1 copy.28
  43.7 0.2 reshape.51.map_ref
  44.0 0.9 copy-done
  44.9 1.3 %shard_map.93 = (bf16[8,2,256,128]{3,2,1,0:T(8,128)(2,1)S(1)}, bf16[8,2,256,128]{3,2,1,0:T(8,128)(2,1)S(1)}, bf16[8,144,128]{2,1,0:T(8,128)(2,1)S(1)}) custom-call(s32[2]{0:T(128)S(1)} %pad_add_fusion.place_ref, bf16[2,128,128]{2,1,0:T(8,128)(2,1)S(1)} %reshape.51.map_ref, bf16[4,256,128]{2,1,0:T(8,128)(2,1)S(1)} %copy-done, ...), custom_call_target="tpu_custom_call" | custom-call | flops 500000000 | bytes 2000000 | tf_op jit(solution)/shard_map/pallas_call | solution.py:317
  46.2 16.0 %all_to_all.28.sums_ref = bf16[8,144,128]{2,1,0:T(8,128)(2,1)S(1)} all-to-all(bf16[8,144,128]{2,1,0:T(8,128)(2,1)S(1)} %get-tuple-element.50), channel_id=1, replica_groups=mesh['z'=8,'x'=4,'core'=2,'y'=4] {'z'}, dimensions={0} | all-to-all | bytes 589824 | tf_op jit(solution)/shard_map/all_to_all | solution.py:367
  62.2 3.8 %shard_map.94 = (bf16[8,144,128]{2,1,0:T(8,128)(2,1)}, f32[128,256]{1,0:T(8,128)S(1)}) custom-call(s32[2]{0:T(128)S(1)} %pad_add_fusion.place_ref, bf16[8,2,256,128]{3,2,1,0:T(8,128)(2,1)S(1)} %get-tuple-element.48.kv_ref, bf16[8,2,256,128]{3,2,1,0:T(8,128)(2,1)S(1)} %get-tuple-element.49.qd_ref, bf16[2,128,128]{2,1,0:T(8,128)(2,1)S(1)} %reshape.51.map_ref, ...), custom_call_target="tpu_custom_call" | custom-call | flops 2000000000 | bytes 8000000 | tf_op jit(solution)/shard_map/pallas_call | solution.py:317
  66.0 3.6 %all-to-all-start.2 = ((bf16[8,144,128]{2,1,0:T(8,128)(2,1)}), bf16[8,144,128]{2,1,0:T(8,128)(2,1)S(1)}, u32[]{:S(2)}, u32[]{:S(2)}) async-start(bf16[8,144,128]{2,1,0:T(8,128)(2,1)} %get-tuple-element.51), calls=%async_computation.2 | async-start | bytes 589824 | tf_op jit(solution)/shard_map/all_to_all | solution.py:372
  69.6 1.2 copy-done.2
  70.8 6.2 %shard_map.95 = (bf16[40,8,2,256,128]{4,3,2,1,0:T(8,128)(2,1)}, bf16[8,2,256,128]{3,2,1,0:T(8,128)(2,1)S(1)}, f32[128,128]{1,0:T(8,128)S(1)}) custom-call(bf16[8,2,256,128]{3,2,1,0:T(8,128)(2,1)S(1)} %get-tuple-element.48.kv_ref, bf16[8,2,256,128]{3,2,1,0:T(8,128)(2,1)S(1)} %copy-done.2, bf16[2,128,128]{2,1,0:T(8,128)(2,1)S(1)} %reshape.51.map_ref, ...), custom_call_target="tpu_custom_call" | custom-call | flops 3000000000 | bytes 12000000 | tf_op jit(solution)/shard_map/pallas_call | solution.py:317
  77.0 2.0 %all-to-all-done.2.sums_ref = bf16[8,144,128]{2,1,0:T(8,128)(2,1)S(1)} async-done(((bf16[8,144,128]{2,1,0:T(8,128)(2,1)}), bf16[8,144,128]{2,1,0:T(8,128)(2,1)S(1)}, u32[]{:S(2)}, u32[]{:S(2)}) %all-to-all-start.2) | async-done | bytes 294944 | tf_op jit(solution)/shard_map/all_to_all | solution.py:372
  79.0 3.7 %shard_map.96 = (f32[128,128]{1,0:T(8,128)S(1)}, bf16[4,256,128]{2,1,0:T(8,128)(2,1)S(1)}, bf16[4,256,128]{2,1,0:T(8,128)(2,1)}, bf16[4,256,128]{2,1,0:T(8,128)(...) custom-call(s32[2]{0:T(128)S(1)} %pad_add_fusion.place_ref, ...), custom_call_target="tpu_custom_call" | custom-call | flops 1500000000 | bytes 6000000 | tf_op jit(solution)/shard_map/pallas_call | solution.py:317
  82.7 0.7 copy-done.3
  83.4 0.7 copy-done.4
  84.1 0.7 copy-done.5
  84.8 3.9 %collective-permute-start.7 = (bf16[4,256,128]{2,1,0:T(8,128)(2,1)}, bf16[4,256,128]{2,1,0:T(8,128)(2,1)S(1)}, u32[]{:S(2)}, u32[]{:S(2)}) collective-permute-start(bf16[4,256,128]{2,1,0:T(8,128)(2,1)} %get-tuple-element.58), channel_id=1, source_target_pairs={{0,4},{4,0},{8,12},{12,8},{16,20},{20,16},{24,28},{28,24},{1,5},{5... | collective-permute-start | bytes 786440 | tf_op jit(solution)/shard_map/ppermute | solution.py:331
  88.7 0.2 stack.21
  88.9 0.2 stack.22
  89.1 1.7 %collective-permute-start.9 = (bf16[4,256,128]{2,1,0:T(8,128)(2,1)}, bf16[4,256,128]{2,1,0:T(8,128)(2,1)S(1)}, u32[]{:S(2)}, u32[]{:S(2)}) collective-permute-start(bf16[4,256,128]{2,1,0:T(8,128)(2,1)} %copy-done.5), channel_id=1, source_target_pairs={{0,12},{4,8},{8,4},{12,0},{16,28},{20,24},{24,20},{28,16},{1,13},{... | collective-permute-start | bytes 786440 | tf_op jit(solution)/shard_map/ppermute | solution.py:331
  90.8 2.1 %collective-permute-start.10 = (bf16[4,256,128]{2,1,0:T(8,128)(2,1)}, bf16[4,256,128]{2,1,0:T(8,128)(2,1)S(1)}, u32[]{:S(2)}, u32[]{:S(2)}) collective-permute-start(bf16[4,256,128]{2,1,0:T(8,128)(2,1)} %copy-done.4), channel_id=1, source_target_pairs={{0,16},{4,20},{8,24},{12,28},{16,0},{20,4},{24,8},{28,12},{1,17},{... | collective-permute-start | bytes 786440 | tf_op jit(solution)/shard_map/ppermute | solution.py:331
  92.9 1.2 collective-permute-start.11
  94.2 2.5 %collective-permute-start.12 = (bf16[4,256,128]{2,1,0:T(8,128)(2,1)S(1)}, bf16[4,256,128]{2,1,0:T(8,128)(2,1)S(1)}, u32[]{:S(2)}, u32[]{:S(2)}) collective-permute-start(bf16[4,256,128]{2,1,0:T(8,128)(2,1)S(1)} %get-tuple-element.64), channel_id=1, source_target_pairs={{0,24},{4,28},{8,16},{12,20},{16,8},{20,12},{24,0},{28,4},{1,25},{... | collective-permute-start | bytes 786440 | tf_op jit(solution)/shard_map/ppermute | solution.py:331
  96.6 0.2 collective-permute-done.8.refs_2_
  96.9 3.5 %collective-permute-start.13 = (bf16[4,256,128]{2,1,0:T(8,128)(2,1)S(1)}, bf16[4,256,128]{2,1,0:T(8,128)(2,1)S(1)}, u32[]{:S(2)}, u32[]{:S(2)}) collective-permute-start(bf16[4,256,128]{2,1,0:T(8,128)(2,1)S(1)} %get-tuple-element.65), channel_id=1, source_target_pairs={{0,28},{4,24},{8,20},{12,16},{16,12},{20,8},{24,4},{28,0},{1,29},{... | collective-permute-start | bytes 786440 | tf_op jit(solution)/shard_map/ppermute | solution.py:331
  100.4 0.1 maximum_bitcast_fusion
  100.6 0.4 copy.29
  101.0 1.1 reshape.52
  102.1 5.2 %all-to-all-start.3 = ((f32[256,1,128]{2,1,0:T(1,128)}), f32[256,1,128]{2,1,0:T(1,128)S(1)}, u32[]{:S(2)}, u32[]{:S(2)}) async-start(f32[256,1,128]{2,1,0:T(1,128)} %bitcast.10), calls=%async_computation.3 | async-start | bytes 262144 | tf_op jit(solution)/shard_map/all_to_all | solution.py:389
  107.2 3.1 %collective-permute-done.10.refs_4_ = bf16[4,256,128]{2,1,0:T(8,128)(2,1)S(1)} collective-permute-done((bf16[4,256,128]{2,1,0:T(8,128)(2,1)}, bf16[4,256,128]{2,1,0:T(8,128)(2,1)S(1)}, u32[]{:S(2)}, u32[]{:S(2)}) %collective-permute-start.10) | collective-permute-done | bytes 262176 | tf_op jit(solution)/shard_map/ppermute | solution.py:331
  110.4 7.3 %collective-permute-done.11.refs_5_ = bf16[4,256,128]{2,1,0:T(8,128)(2,1)S(1)} collective-permute-done((bf16[4,256,128]{2,1,0:T(8,128)(2,1)}, bf16[4,256,128]{2,1,0:T(8,128)(2,1)S(1)}, u32[]{:S(2)}, u32[]{:S(2)}) %collective-permute-start.11) | collective-permute-done | bytes 262176 | tf_op jit(solution)/shard_map/ppermute | solution.py:331
  117.6 4.3 %collective-permute-done.13.refs_7_ = bf16[4,256,128]{2,1,0:T(8,128)(2,1)S(1)} collective-permute-done((bf16[4,256,128]{2,1,0:T(8,128)(2,1)S(1)}, bf16[4,256,128]{2,1,0:T(8,128)(2,1)S(1)}, u32[]{:S(2)}, u32[]{:S(2)}) %collective-permute-start.13) | collective-permute-done | bytes 262176 | tf_op jit(solution)/shard_map/ppermute | solution.py:331
  121.9 2.1 %shard_map.97 = (bf16[256,1024]{1,0:T(8,128)(2,1)}, bf16[256,1024]{1,0:T(8,128)(2,1)}, bf16[256,1024]{1,0:T(8,128)(2,1)}, bf16[256,1024]{1,0:T(8,128)(2,1)}) custom-call(s32[2]{0:T(128)S(1)} %pad_add_fusion.place_ref, bf16[4,256,128]{2,1,0:T(8,128)(2,1)S(1)} %get-tuple-element.55.refs_0_, bf16[4,256,128]{2,1,0:T(8,128)(2,1)S(1)} %collective-permute-done.7.refs_1_, ...), custom_call_target="tpu_custom_call" | custom-call | flops 500000000 | bytes 2000000 | tf_op jit(solution)/shard_map/pallas_call | solution.py:317
  124.1 0.1 div.10
  124.2 0.7 copy.33
  (24 shorter events, 0.2 us)
Async XLA Ops:
  3.3 8.4 %collective-permute-start = (bf16[4,256,128]{2,1,0:T(8,128)(2,1)}, bf16[4,256,128]{2,1,0:T(8,128)(2,1)S(1)}, u32[]{:S(2)}, u32[]{:S(2)}) collective-permute-start(bf16[4,256,128]{2,1,0:T(8,128)(2,1)} %get-tuple-element.38), channel_id=1, source_target_pairs={{0,4},{4,0},{8,12},{12,8},{16,20},{20,16},{24,28},{28,24},{1,5},{5... | collective-permute-start | bytes 786440 | tf_op jit(solution)/shard_map/ppermute | solution.py:331
  6.7 8.1 %collective-permute-start.1 = (bf16[4,256,128]{2,1,0:T(8,128)(2,1)}, bf16[4,256,128]{2,1,0:T(8,128)(2,1)S(1)}, u32[]{:S(2)}, u32[]{:S(2)}) collective-permute-start(bf16[4,256,128]{2,1,0:T(8,128)(2,1)} %get-tuple-element.42), channel_id=1, source_target_pairs={{0,8},{4,12},{8,0},{12,4},{16,24},{20,28},{24,16},{28,20},{1,9},{5... | collective-permute-start | bytes 786440 | tf_op jit(solution)/shard_map/ppermute | solution.py:331
  6.7 37.2 %collective-permute-start.2 = (bf16[4,256,128]{2,1,0:T(8,128)(2,1)}, bf16[4,256,128]{2,1,0:T(8,128)(2,1)S(1)}, u32[]{:S(2)}, u32[]{:S(2)}) collective-permute-start(bf16[4,256,128]{2,1,0:T(8,128)(2,1)} %get-tuple-element.43), channel_id=1, source_target_pairs={{0,12},{4,8},{8,4},{12,0},{16,28},{20,24},{24,20},{28,16},{1,13},{... | collective-permute-start | bytes 786440 | tf_op jit(solution)/shard_map/ppermute | solution.py:331
  8.4 35.5 %collective-permute-start.3 = (bf16[4,256,128]{2,1,0:T(8,128)(2,1)}, bf16[4,256,128]{2,1,0:T(8,128)(2,1)S(1)}, u32[]{:S(2)}, u32[]{:S(2)}) collective-permute-start(bf16[4,256,128]{2,1,0:T(8,128)(2,1)} %get-tuple-element.44), channel_id=1, source_target_pairs={{0,16},{4,20},{8,24},{12,28},{16,0},{20,4},{24,8},{28,12},{1,17},{... | collective-permute-start | bytes 786440 | tf_op jit(solution)/shard_map/ppermute | solution.py:331
  9.4 34.5 %collective-permute-start.4 = (bf16[4,256,128]{2,1,0:T(8,128)(2,1)}, bf16[4,256,128]{2,1,0:T(8,128)(2,1)S(1)}, u32[]{:S(2)}, u32[]{:S(2)}) collective-permute-start(bf16[4,256,128]{2,1,0:T(8,128)(2,1)} %get-tuple-element.45), channel_id=1, source_target_pairs={{0,20},{4,16},{8,28},{12,24},{16,4},{20,0},{24,12},{28,8},{1,21},{... | collective-permute-start | bytes 786440 | tf_op jit(solution)/shard_map/ppermute | solution.py:331
  11.7 32.2 %collective-permute-start.5 = (bf16[4,256,128]{2,1,0:T(8,128)(2,1)}, bf16[4,256,128]{2,1,0:T(8,128)(2,1)S(1)}, u32[]{:S(2)}, u32[]{:S(2)}) collective-permute-start(bf16[4,256,128]{2,1,0:T(8,128)(2,1)} %get-tuple-element.46), channel_id=1, source_target_pairs={{0,24},{4,28},{8,16},{12,20},{16,8},{20,12},{24,0},{28,4},{1,25},{... | collective-permute-start | bytes 786440 | tf_op jit(solution)/shard_map/ppermute | solution.py:331
  14.7 29.2 %collective-permute-start.6 = (bf16[4,256,128]{2,1,0:T(8,128)(2,1)}, bf16[4,256,128]{2,1,0:T(8,128)(2,1)S(1)}, u32[]{:S(2)}, u32[]{:S(2)}) collective-permute-start(bf16[4,256,128]{2,1,0:T(8,128)(2,1)} %get-tuple-element.47), channel_id=1, source_target_pairs={{0,28},{4,24},{8,20},{12,16},{16,12},{20,8},{24,4},{28,0},{1,29},{... | collective-permute-start | bytes 786440 | tf_op jit(solution)/shard_map/ppermute | solution.py:331
  18.4 24.7 %all-to-all-start = ((bf16[256,1,128]{2,1,0:T(2,128)(2,1)}), bf16[256,1,128]{2,1,0:T(2,128)(2,1)S(1)}, u32[]{:S(2)}, u32[]{:S(2)}) async-start(bf16[256,1,128]{2,1,0:T(2,128)(2,1)} %copy.27), calls=%async_computation | async-start | bytes 262144 | tf_op jit(solution)/shard_map/all_to_all | solution.py:362
  43.9 1.0 copy-start
  46.2 19.8 %copy-start.1 = (bf16[8,2,256,128]{3,2,1,0:T(8,128)(2,1)}, bf16[8,2,256,128]{3,2,1,0:T(8,128)(2,1)S(1)}, u32[]{:S(2)}) copy-start(bf16[8,2,256,128]{3,2,1,0:T(8,128)(2,1)S(1)} %get-tuple-element.49.qd_ref) | copy-start | bytes 3145732
  66.0 13.1 %all-to-all-start.2 = ((bf16[8,144,128]{2,1,0:T(8,128)(2,1)}), bf16[8,144,128]{2,1,0:T(8,128)(2,1)S(1)}, u32[]{:S(2)}, u32[]{:S(2)}) async-start(bf16[8,144,128]{2,1,0:T(8,128)(2,1)} %get-tuple-element.51), calls=%async_computation.2 | async-start | bytes 589824 | tf_op jit(solution)/shard_map/all_to_all | solution.py:372
  69.6 1.2 copy-start.2
  82.7 0.7 copy-start.3
  83.4 0.7 copy-start.4
  84.1 0.7 copy-start.5
  84.8 9.3 %collective-permute-start.7 = (bf16[4,256,128]{2,1,0:T(8,128)(2,1)}, bf16[4,256,128]{2,1,0:T(8,128)(2,1)S(1)}, u32[]{:S(2)}, u32[]{:S(2)}) collective-permute-start(bf16[4,256,128]{2,1,0:T(8,128)(2,1)} %get-tuple-element.58), channel_id=1, source_target_pairs={{0,4},{4,0},{8,12},{12,8},{16,20},{20,16},{24,28},{28,24},{1,5},{5... | collective-permute-start | bytes 786440 | tf_op jit(solution)/shard_map/ppermute | solution.py:331
  88.7 8.1 %collective-permute-start.8 = (bf16[4,256,128]{2,1,0:T(8,128)(2,1)}, bf16[4,256,128]{2,1,0:T(8,128)(2,1)S(1)}, u32[]{:S(2)}, u32[]{:S(2)}) collective-permute-start(bf16[4,256,128]{2,1,0:T(8,128)(2,1)} %get-tuple-element.60), channel_id=1, source_target_pairs={{0,8},{4,12},{8,0},{12,4},{16,24},{20,28},{24,16},{28,20},{1,9},{5... | collective-permute-start | bytes 786440 | tf_op jit(solution)/shard_map/ppermute | solution.py:331
  89.1 18.2 %collective-permute-start.9 = (bf16[4,256,128]{2,1,0:T(8,128)(2,1)}, bf16[4,256,128]{2,1,0:T(8,128)(2,1)S(1)}, u32[]{:S(2)}, u32[]{:S(2)}) collective-permute-start(bf16[4,256,128]{2,1,0:T(8,128)(2,1)} %copy-done.5), channel_id=1, source_target_pairs={{0,12},{4,8},{8,4},{12,0},{16,28},{20,24},{24,20},{28,16},{1,13},{... | collective-permute-start | bytes 786440 | tf_op jit(solution)/shard_map/ppermute | solution.py:331
  90.8 19.6 %collective-permute-start.10 = (bf16[4,256,128]{2,1,0:T(8,128)(2,1)}, bf16[4,256,128]{2,1,0:T(8,128)(2,1)S(1)}, u32[]{:S(2)}, u32[]{:S(2)}) collective-permute-start(bf16[4,256,128]{2,1,0:T(8,128)(2,1)} %copy-done.4), channel_id=1, source_target_pairs={{0,16},{4,20},{8,24},{12,28},{16,0},{20,4},{24,8},{28,12},{1,17},{... | collective-permute-start | bytes 786440 | tf_op jit(solution)/shard_map/ppermute | solution.py:331
  92.9 24.7 %collective-permute-start.11 = (bf16[4,256,128]{2,1,0:T(8,128)(2,1)}, bf16[4,256,128]{2,1,0:T(8,128)(2,1)S(1)}, u32[]{:S(2)}, u32[]{:S(2)}) collective-permute-start(bf16[4,256,128]{2,1,0:T(8,128)(2,1)} %copy-done.3), channel_id=1, source_target_pairs={{0,20},{4,16},{8,28},{12,24},{16,4},{20,0},{24,12},{28,8},{1,21},{... | collective-permute-start | bytes 786440 | tf_op jit(solution)/shard_map/ppermute | solution.py:331
  94.2 23.5 %collective-permute-start.12 = (bf16[4,256,128]{2,1,0:T(8,128)(2,1)S(1)}, bf16[4,256,128]{2,1,0:T(8,128)(2,1)S(1)}, u32[]{:S(2)}, u32[]{:S(2)}) collective-permute-start(bf16[4,256,128]{2,1,0:T(8,128)(2,1)S(1)} %get-tuple-element.64), channel_id=1, source_target_pairs={{0,24},{4,28},{8,16},{12,20},{16,8},{20,12},{24,0},{28,4},{1,25},{... | collective-permute-start | bytes 786440 | tf_op jit(solution)/shard_map/ppermute | solution.py:331
  96.9 25.0 %collective-permute-start.13 = (bf16[4,256,128]{2,1,0:T(8,128)(2,1)S(1)}, bf16[4,256,128]{2,1,0:T(8,128)(2,1)S(1)}, u32[]{:S(2)}, u32[]{:S(2)}) collective-permute-start(bf16[4,256,128]{2,1,0:T(8,128)(2,1)S(1)} %get-tuple-element.65), channel_id=1, source_target_pairs={{0,28},{4,24},{8,20},{12,16},{16,12},{20,8},{24,4},{28,0},{1,29},{... | collective-permute-start | bytes 786440 | tf_op jit(solution)/shard_map/ppermute | solution.py:331
  102.1 22.0 %all-to-all-start.3 = ((f32[256,1,128]{2,1,0:T(1,128)}), f32[256,1,128]{2,1,0:T(1,128)S(1)}, u32[]{:S(2)}, u32[]{:S(2)}) async-start(f32[256,1,128]{2,1,0:T(1,128)} %bitcast.10), calls=%async_computation.3 | async-start | bytes 262144 | tf_op jit(solution)/shard_map/all_to_all | solution.py:389

commit v6 on v5

--- a/solution.py
+++ b/solution.py
@@ -19,7 +19,7 @@
 DMA = pltpu.SemaphoreType.DMA
 PART = BF16
 STATE_ROWS = HEAD_DIM + 16
-GROUP = 4
+GROUP = 8
 OUTER_LIMIT = 32
 HELD = 40
 
@@ -98,13 +98,16 @@
         store.wait()
 
 
+def own_columns(me, outs, piece, sem):
+    column = pl.ds(pl.multiple_of(me * HEAD_DIM, HEAD_DIM), HEAD_DIM)
+    return [pltpu.make_async_copy(piece.at[n], ref.at[:, column], sem.at[n]) for n, ref in enumerate(outs)]
+
+
 def unpack(place_ref, *refs):
-    pieces, outs, sem = refs[:-5], refs[-5:-1], refs[-1]
+    pieces, outs, sem = refs[4:-5], refs[-5:-1], refs[-1]
     copies = []
-    for s, piece in enumerate(pieces):
-        column = pl.ds(pl.multiple_of((place_ref[1] ^ s) * HEAD_DIM, HEAD_DIM), HEAD_DIM)
-        for n, ref in enumerate(outs):
-            copies.append(pltpu.make_async_copy(piece.at[n], ref.at[:, column], sem.at[s, n]))
+    for s, piece in enumerate(pieces, start=1):
+        copies += own_columns(place_ref[1] ^ s, outs, piece, sem.at[s])
     for copy in copies:
         copy.start()
     for copy in copies:
@@ -273,7 +276,8 @@
 
 
 def outer(place_ref, kv_ref, map_ref, sums_ref, aq_ref, part_ref, out_ref, *refs):
-    pieces, sem = refs[:-1], refs[-1]
+    outs, sent, (held, sem, own_sem) = refs[:4], refs[4:-3], refs[-3:]
+    pieces = [held, *sent]
     place = place_ref[0]
     copies = [pltpu.make_async_copy(aq_ref.at[0, place_ref[1] ^ s], piece.at[pl.ds(0, 2)], sem.at[s])
               for s, piece in enumerate(pieces)]
@@ -305,7 +309,11 @@
             pieces[s][3] = d_value[n].astype(BF16)
             map_grad = map_grad + mm_tn(kv_ref[at[n], 0], dpre[n])
     out_ref[...] = map_grad
-    for copy in copies:
+    copies[0].wait()
+    own = own_columns(place_ref[1], outs, held, own_sem)
+    for copy in own:
+        copy.start()
+    for copy in copies[1:] + own:
         copy.wait()
 
 
@@ -313,23 +321,22 @@
     return jax.ShapeDtypeStruct(dims, dtype)
 
 
-def call(kernel, outs, operands, scratch=(), cycles=1, limit=32):
+def call(kernel, outs, operands, scratch=(), cycles=1, limit=32, aliases={}):
     return pl.pallas_call(
         kernel,
         out_shape=[s for _, s in outs],
         in_specs=[spec for spec, _ in operands],
         out_specs=[spec for spec, _ in outs],
         scratch_shapes=list(scratch),
+        input_output_aliases=aliases,
         compiler_params=pltpu.CompilerParams(vmem_limit_bytes=limit * 1024 * 1024),
         cost_estimate=pl.CostEstimate(flops=cycles * 500_000_000, bytes_accessed=cycles * 2_000_000, transcendentals=0),
     )(*[v for _, v in operands])
 
 
 def trade(pieces):
-    count = len(pieces)
-    return [pieces[0]] + [
-        lax.ppermute(pieces[s], ROW, [(i, i ^ s) for i in range(count)]) for s in range(1, count)
-    ]
+    count = len(pieces) + 1
+    return [lax.ppermute(pieces[s - 1], ROW, [(i, i ^ s) for i in range(count)]) for s in range(1, count)]
 
 
 def gather_maps(maps):
@@ -356,7 +363,7 @@
     pieces = call(
         pack, [(ANY, shape(*four))] * row, [(ANY, v) for v in (keys, values, queries, out_grad)],
         [scratch((row, *four), BF16), DMA((row, 4)), DMA((row,))], limit=60)
-    pieces = trade(pieces)
+    pieces = [pieces[0], *trade(pieces[1:])]
     maps = gather_maps(feature_weights)
     maps, pieces[1] = lax.optimization_barrier((maps, pieces[1]))
     maps = lax.all_to_all(maps, FINE, 0, 0, tiled=True)
@@ -377,21 +384,23 @@
         halved + [scratch((row, 2, BLOCK, HEAD_DIM), F32), scratch((row, HEAD_DIM, 2 * HEAD_DIM), F32),
                   scratch((row, BLOCK, HEAD_DIM), BF16), scratch((row, 2, BLOCK, HEAD_DIM), BF16), DMA((row,))],
         cycles=6)
+    outs = [(ANY, shape(*queries.shape))] * 4
     map_grad_k, *pieces = call(
-        outer, [square] + [(VMEM, shape(*four))] * row,
+        outer, [square] + outs + [(VMEM, shape(*four))] * (row - 1),
         [(SMEM, place), (VMEM, kv), (VMEM, maps), (VMEM, total), (ANY, aq), (VMEM, part)],
-        [DMA((row,))], cycles=3, limit=OUTER_LIMIT)
-    pieces = trade(pieces)
+        [scratch(four, BF16), DMA((row,)), DMA((4,))], cycles=3, limit=OUTER_LIMIT)
+    owned, pieces = pieces[:4], trade(pieces[4:])
 
     map_grad = jnp.stack((map_grad_q, map_grad_k)).reshape(2, z_size * row, own, heads // row, cut)
     map_grad = map_grad.transpose(1, 3, 2, 0, 4).reshape(z_size * heads, own * 2 * cut)
-    map_grad, pieces[1] = lax.optimization_barrier((map_grad, pieces[1]))
+    map_grad, pieces[0] = lax.optimization_barrier((map_grad, pieces[0]))
     map_grad = lax.all_to_all(map_grad, FINE, 0, 0, tiled=True)
     map_grad = jnp.sum(map_grad.reshape(z_size, heads, own * 2 * cut), axis=0) / tokens
     map_grad = map_grad.reshape(row, heads // row, own, 2, cut).transpose(2, 3, 1, 0, 4)
     map_grad = map_grad.reshape(own, 2, heads, cut)
     attended, query_grad, key_grad, value_grad = call(
-        unpack, [(ANY, shape(*queries.shape))] * 4, [(SMEM, place)] + [(VMEM, v) for v in pieces], [DMA((row, 4))])
+        unpack, outs, [(SMEM, place)] + [(ANY, v) for v in owned] + [(VMEM, v) for v in pieces], [DMA((row, 4))],
+        aliases={n + 1: n for n in range(4)})
     return attended, query_grad, key_grad, value_grad, map_grad
 
 

time: 125 us -> 125 us (level)
    unnamed x12 -> x10, local copies, waits for them, and re-layouts: 4.27 us -> 3.57 us
where the time goes in v6:
time: 125 us; the launch traced here: 124 us
  starting transfers between devices  46.9 us (38%)
  waiting for transfers between devices  31.9 us (26%)
  Pallas kernels  19.6 us (16%)
  blocking collectives  16 us (13%)
  local copies, waits for them, and re-layouts  8.22 us (7%)
    ppermute x14, starting transfers between devices, trade(): lax.ppermute(pieces[s - 1], ROW, [(i, i ^ s) for i in range(count)])  26.1 us
    pallas_call x6, Pallas kernels, call(): pl.pallas_call(kernel, out_shape=[s for _, s in outs], in_specs=[spec for...  19.6 us
    ppermute x14, waiting for transfers between devices, trade(): lax.ppermute(pieces[s - 1], ROW, [(i, i ^ s) for i in range(count)])  17.2 us
    all_to_all x1, blocking collectives, body(): state = lax.all_to_all(state, 'z', 0, 0, tiled=True)  16 us
    all_to_all x1, waiting for transfers between devices, body(): maps = lax.all_to_all(maps, FINE, 0, 0, tiled=True)  12.6 us
    all_to_all x1, starting transfers between devices, body(): maps = lax.all_to_all(maps, FINE, 0, 0, tiled=True)  12 us
    all_to_all x1, starting transfers between devices, body(): map_grad = lax.all_to_all(map_grad, FINE, 0, 0, tiled=True)  5.13 us
    all_to_all x1, starting transfers between devices, body(): total = lax.all_to_all(total, 'z', 0, 0, tiled=True)  3.6 us
  transfers between devices with their start and end apart: 17, of which 7 were waited for; matrix products, arithmetic and copies ran while one was open for 4% of the time, Pallas kernels for 7%

profile of v6, /device:TPU:1, one launch (start us, length us, event | category | flops | bytes accessed | tf_op | source)
XLA Modules:
  0.0 124.0 jit_solution(1950457683308858081)
XLA Ops:
  0.6 2.7 %shard_map.92 = (bf16[4,256,128]{2,1,0:T(8,128)(2,1)}, bf16[4,256,128]{2,1,0:T(8,128)(2,1)}, bf16[4,256,128]{2,1,0:T(8,128)(2,1)}, bf16[4,256,128]{2,1,0:T(8,128...) custom-call(bf16[256,1024]{1,0:T(8,128)(2,1)} %refs_0_.1, ...), custom_call_target="tpu_custom_call" | custom-call | flops 500000000 | bytes 2000000 | tf_op jit(solution)/shard_map/pallas_call | solution.py:325
  3.3 3.3 %collective-permute-start = (bf16[4,256,128]{2,1,0:T(8,128)(2,1)}, bf16[4,256,128]{2,1,0:T(8,128)(2,1)S(1)}, u32[]{:S(2)}, u32[]{:S(2)}) collective-permute-start(bf16[4,256,128]{2,1,0:T(8,128)(2,1)} %get-tuple-element.41), channel_id=1, source_target_pairs={{0,4},{4,0},{8,12},{12,8},{16,20},{20,16},{24,28},{28,24},{1,5},{5... | collective-permute-start | bytes 786440 | tf_op jit(solution)/shard_map/ppermute | solution.py:339
  6.7 1.7 %collective-permute-start.2 = (bf16[4,256,128]{2,1,0:T(8,128)(2,1)}, bf16[4,256,128]{2,1,0:T(8,128)(2,1)S(1)}, u32[]{:S(2)}, u32[]{:S(2)}) collective-permute-start(bf16[4,256,128]{2,1,0:T(8,128)(2,1)} %get-tuple-element.46), channel_id=1, source_target_pairs={{0,12},{4,8},{8,4},{12,0},{16,28},{20,24},{24,20},{28,16},{1,13},{... | collective-permute-start | bytes 786440 | tf_op jit(solution)/shard_map/ppermute | solution.py:339
  8.4 1.0 collective-permute-start.3
  9.4 2.3 %collective-permute-start.4 = (bf16[4,256,128]{2,1,0:T(8,128)(2,1)}, bf16[4,256,128]{2,1,0:T(8,128)(2,1)S(1)}, u32[]{:S(2)}, u32[]{:S(2)}) collective-permute-start(bf16[4,256,128]{2,1,0:T(8,128)(2,1)} %get-tuple-element.48), channel_id=1, source_target_pairs={{0,20},{4,16},{8,28},{12,24},{16,4},{20,0},{24,12},{28,8},{1,21},{... | collective-permute-start | bytes 786440 | tf_op jit(solution)/shard_map/ppermute | solution.py:339
  11.7 0.7 collective-permute-start.5
  12.4 2.3 %collective-permute-done.1.refs_2_ = bf16[4,256,128]{2,1,0:T(8,128)(2,1)S(1)} collective-permute-done((bf16[4,256,128]{2,1,0:T(8,128)(2,1)}, bf16[4,256,128]{2,1,0:T(8,128)(2,1)S(1)}, u32[]{:S(2)}, u32[]{:S(2)}) %collective-permute-start.1) | collective-permute-done | bytes 262176 | tf_op jit(solution)/shard_map/ppermute | solution.py:339
  14.7 2.0 %collective-permute-start.6 = (bf16[4,256,128]{2,1,0:T(8,128)(2,1)}, bf16[4,256,128]{2,1,0:T(8,128)(2,1)S(1)}, u32[]{:S(2)}, u32[]{:S(2)}) collective-permute-start(bf16[4,256,128]{2,1,0:T(8,128)(2,1)} %get-tuple-element.50), channel_id=1, source_target_pairs={{0,28},{4,24},{8,20},{12,16},{16,12},{20,8},{24,4},{28,0},{1,29},{... | collective-permute-start | bytes 786440 | tf_op jit(solution)/shard_map/ppermute | solution.py:339
  16.7 0.8 copy.29
  17.5 0.1 reshape.48
  17.6 0.8 copy.31
  18.4 12.0 %all-to-all-start = ((bf16[256,1,128]{2,1,0:T(2,128)(2,1)}), bf16[256,1,128]{2,1,0:T(2,128)(2,1)S(1)}, u32[]{:S(2)}, u32[]{:S(2)}) async-start(bf16[256,1,128]{2,1,0:T(2,128)(2,1)} %copy.31), calls=%async_computation | async-start | bytes 262144 | tf_op jit(solution)/shard_map/all_to_all | solution.py:369
  30.4 0.1 pad_add_fusion.place_ref
  30.5 12.6 %all-to-all-done = bf16[256,1,128]{2,1,0:T(2,128)(2,1)S(1)} async-done(((bf16[256,1,128]{2,1,0:T(2,128)(2,1)}), bf16[256,1,128]{2,1,0:T(2,128)(2,1)S(1)}, u32[]{:S(2)}, u32[]{:S(2)}) %all-to-all-start) | async-done | bytes 65568 | tf_op jit(solution)/shard_map/all_to_all | solution.py:369
  43.1 0.4 reduce
  43.5 0.2 reshape.50
  43.6 0.1 copy.32
  43.7 0.2 reshape.51.map_ref
  44.0 0.9 copy-done
  44.9 1.3 %shard_map.93 = (bf16[8,2,256,128]{3,2,1,0:T(8,128)(2,1)S(1)}, bf16[8,2,256,128]{3,2,1,0:T(8,128)(2,1)S(1)}, bf16[8,144,128]{2,1,0:T(8,128)(2,1)S(1)}) custom-call(s32[2]{0:T(128)S(1)} %pad_add_fusion.place_ref, bf16[2,128,128]{2,1,0:T(8,128)(2,1)S(1)} %reshape.51.map_ref, bf16[4,256,128]{2,1,0:T(8,128)(2,1)S(1)} %copy-done, ...), custom_call_target="tpu_custom_call" | custom-call | flops 500000000 | bytes 2000000 | tf_op jit(solution)/shard_map/pallas_call | solution.py:325
  46.2 16.0 %all_to_all.28.sums_ref = bf16[8,144,128]{2,1,0:T(8,128)(2,1)S(1)} all-to-all(bf16[8,144,128]{2,1,0:T(8,128)(2,1)S(1)} %get-tuple-element.53), channel_id=1, replica_groups=mesh['z'=8,'x'=4,'core'=2,'y'=4] {'z'}, dimensions={0} | all-to-all | bytes 589824 | tf_op jit(solution)/shard_map/all_to_all | solution.py:374
  62.2 3.6 %shard_map.94 = (bf16[8,144,128]{2,1,0:T(8,128)(2,1)}, f32[128,256]{1,0:T(8,128)S(1)}) custom-call(s32[2]{0:T(128)S(1)} %pad_add_fusion.place_ref, bf16[8,2,256,128]{3,2,1,0:T(8,128)(2,1)S(1)} %get-tuple-element.51.kv_ref, bf16[8,2,256,128]{3,2,1,0:T(8,128)(2,1)S(1)} %get-tuple-element.52.qd_ref, bf16[2,128,128]{2,1,0:T(8,128)(2,1)S(1)} %reshape.51.map_ref, ...), custom_call_target="tpu_custom_call" | custom-call | flops 2000000000 | bytes 8000000 | tf_op jit(solution)/shard_map/pallas_call | solution.py:325
  65.8 3.6 %all-to-all-start.2 = ((bf16[8,144,128]{2,1,0:T(8,128)(2,1)}), bf16[8,144,128]{2,1,0:T(8,128)(2,1)S(1)}, u32[]{:S(2)}, u32[]{:S(2)}) async-start(bf16[8,144,128]{2,1,0:T(8,128)(2,1)} %get-tuple-element.54), calls=%async_computation.2 | async-start | bytes 589824 | tf_op jit(solution)/shard_map/all_to_all | solution.py:379
  69.4 1.2 copy-done.2
  70.6 6.2 %shard_map.95 = (bf16[40,8,2,256,128]{4,3,2,1,0:T(8,128)(2,1)}, bf16[8,2,256,128]{3,2,1,0:T(8,128)(2,1)S(1)}, f32[128,128]{1,0:T(8,128)S(1)}) custom-call(bf16[8,2,256,128]{3,2,1,0:T(8,128)(2,1)S(1)} %get-tuple-element.51.kv_ref, bf16[8,2,256,128]{3,2,1,0:T(8,128)(2,1)S(1)} %copy-done.2, bf16[2,128,128]{2,1,0:T(8,128)(2,1)S(1)} %reshape.51.map_ref, ...), custom_call_target="tpu_custom_call" | custom-call | flops 3000000000 | bytes 12000000 | tf_op jit(solution)/shard_map/pallas_call | solution.py:325
  76.8 2.0 %all-to-all-done.2.sums_ref = bf16[8,144,128]{2,1,0:T(8,128)(2,1)S(1)} async-done(((bf16[8,144,128]{2,1,0:T(8,128)(2,1)}), bf16[8,144,128]{2,1,0:T(8,128)(2,1)S(1)}, u32[]{:S(2)}, u32[]{:S(2)}) %all-to-all-start.2) | async-done | bytes 294944 | tf_op jit(solution)/shard_map/all_to_all | solution.py:379
  78.9 3.8 %shard_map.96 = (f32[128,128]{1,0:T(8,128)S(1)}, bf16[256,1024]{1,0:T(8,128)(2,1)}, bf16[256,1024]{1,0:T(8,128)(2,1)}, bf16[256,1024]{1,0:T(8,128)(2,1)}, bf16[2...) custom-call(s32[2]{0:T(128)S(1)} %pad_add_fusion.place_ref, ...), custom_call_target="tpu_custom_call" | custom-call | flops 1500000000 | bytes 6000000 | tf_op jit(solution)/shard_map/pallas_call | solution.py:325
  82.7 0.7 copy-done.3
  83.4 0.7 copy-done.4
  84.1 3.9 %collective-permute-start.7 = (bf16[4,256,128]{2,1,0:T(8,128)(2,1)}, bf16[4,256,128]{2,1,0:T(8,128)(2,1)S(1)}, u32[]{:S(2)}, u32[]{:S(2)}) collective-permute-start(bf16[4,256,128]{2,1,0:T(8,128)(2,1)} %get-tuple-element.64), channel_id=1, source_target_pairs={{0,4},{4,0},{8,12},{12,8},{16,20},{20,16},{24,28},{28,24},{1,5},{5... | collective-permute-start | bytes 786440 | tf_op jit(solution)/shard_map/ppermute | solution.py:339
  88.0 0.2 stack.21
  88.2 0.2 stack.22
  88.4 1.7 %collective-permute-start.9 = (bf16[4,256,128]{2,1,0:T(8,128)(2,1)}, bf16[4,256,128]{2,1,0:T(8,128)(2,1)S(1)}, u32[]{:S(2)}, u32[]{:S(2)}) collective-permute-start(bf16[4,256,128]{2,1,0:T(8,128)(2,1)} %copy-done.4), channel_id=1, source_target_pairs={{0,12},{4,8},{8,4},{12,0},{16,28},{20,24},{24,20},{28,16},{1,13},{... | collective-permute-start | bytes 786440 | tf_op jit(solution)/shard_map/ppermute | solution.py:339
  90.1 2.1 %collective-permute-start.10 = (bf16[4,256,128]{2,1,0:T(8,128)(2,1)}, bf16[4,256,128]{2,1,0:T(8,128)(2,1)S(1)}, u32[]{:S(2)}, u32[]{:S(2)}) collective-permute-start(bf16[4,256,128]{2,1,0:T(8,128)(2,1)} %copy-done.3), channel_id=1, source_target_pairs={{0,16},{4,20},{8,24},{12,28},{16,0},{20,4},{24,8},{28,12},{1,17},{... | collective-permute-start | bytes 786440 | tf_op jit(solution)/shard_map/ppermute | solution.py:339
  92.2 1.2 collective-permute-start.11
  93.4 2.5 %collective-permute-start.12 = (bf16[4,256,128]{2,1,0:T(8,128)(2,1)S(1)}, bf16[4,256,128]{2,1,0:T(8,128)(2,1)S(1)}, u32[]{:S(2)}, u32[]{:S(2)}) collective-permute-start(bf16[4,256,128]{2,1,0:T(8,128)(2,1)S(1)} %get-tuple-element.70), channel_id=1, source_target_pairs={{0,24},{4,28},{8,16},{12,20},{16,8},{20,12},{24,0},{28,4},{1,25},{... | collective-permute-start | bytes 786440 | tf_op jit(solution)/shard_map/ppermute | solution.py:339
  95.9 0.2 collective-permute-done.8.refs_5_
  96.2 3.5 %collective-permute-start.13 = (bf16[4,256,128]{2,1,0:T(8,128)(2,1)S(1)}, bf16[4,256,128]{2,1,0:T(8,128)(2,1)S(1)}, u32[]{:S(2)}, u32[]{:S(2)}) collective-permute-start(bf16[4,256,128]{2,1,0:T(8,128)(2,1)S(1)} %get-tuple-element.71), channel_id=1, source_target_pairs={{0,28},{4,24},{8,20},{12,16},{16,12},{20,8},{24,4},{28,0},{1,29},{... | collective-permute-start | bytes 786440 | tf_op jit(solution)/shard_map/ppermute | solution.py:339
  99.7 0.1 maximum_bitcast_fusion
  99.8 0.4 copy.33
  100.3 1.1 reshape.52
  101.3 5.1 %all-to-all-start.3 = ((f32[256,1,128]{2,1,0:T(1,128)}), f32[256,1,128]{2,1,0:T(1,128)S(1)}, u32[]{:S(2)}, u32[]{:S(2)}) async-start(f32[256,1,128]{2,1,0:T(1,128)} %bitcast.10), calls=%async_computation.3 | async-start | bytes 262144 | tf_op jit(solution)/shard_map/all_to_all | solution.py:397
  106.5 3.1 %collective-permute-done.10.refs_7_ = bf16[4,256,128]{2,1,0:T(8,128)(2,1)S(1)} collective-permute-done((bf16[4,256,128]{2,1,0:T(8,128)(2,1)}, bf16[4,256,128]{2,1,0:T(8,128)(2,1)S(1)}, u32[]{:S(2)}, u32[]{:S(2)}) %collective-permute-start.10) | collective-permute-done | bytes 262176 | tf_op jit(solution)/shard_map/ppermute | solution.py:339
  109.6 7.3 %collective-permute-done.11.refs_8_ = bf16[4,256,128]{2,1,0:T(8,128)(2,1)S(1)} collective-permute-done((bf16[4,256,128]{2,1,0:T(8,128)(2,1)S(1)}, bf16[4,256,128]{2,1,0:T(8,128)(2,1)S(1)}, u32[]{:S(2)}, u32[]{:S(2)}) %collective-permute-start.11) | collective-permute-done | bytes 262176 | tf_op jit(solution)/shard_map/ppermute | solution.py:339
  116.9 4.3 %collective-permute-done.13.refs_10_ = bf16[4,256,128]{2,1,0:T(8,128)(2,1)S(1)} collective-permute-done((bf16[4,256,128]{2,1,0:T(8,128)(2,1)S(1)}, bf16[4,256,128]{2,1,0:T(8,128)(2,1)S(1)}, u32[]{:S(2)}, u32[]{:S(2)}) %collective-permute-start.13) | collective-permute-done | bytes 262176 | tf_op jit(solution)/shard_map/ppermute | solution.py:339
  121.2 2.0 %shard_map.97 = (bf16[256,1024]{1,0:T(8,128)(2,1)}, bf16[256,1024]{1,0:T(8,128)(2,1)}, bf16[256,1024]{1,0:T(8,128)(2,1)}, bf16[256,1024]{1,0:T(8,128)(2,1)}) custom-call(s32[2]{0:T(128)S(1)} %pad_add_fusion.place_ref, bf16[256,1024]{1,0:T(8,128)(2,1)} %get-tuple-element.58.refs_0_, ...), custom_call_target="tpu_custom_call", output_to_operand_aliasing={{0}: (1, {}), {1}: (2, {}), {2}: (3, {}), {3}: (4, {})} | custom-call | flops 500000000 | bytes 2000000 | tf_op jit(solution)/shard_map/pallas_call | solution.py:325
  123.3 0.1 div.10
  123.4 0.7 copy.37
  (22 shorter events, 0.1 us)
Async XLA Ops:
  3.3 8.4 %collective-permute-start = (bf16[4,256,128]{2,1,0:T(8,128)(2,1)}, bf16[4,256,128]{2,1,0:T(8,128)(2,1)S(1)}, u32[]{:S(2)}, u32[]{:S(2)}) collective-permute-start(bf16[4,256,128]{2,1,0:T(8,128)(2,1)} %get-tuple-element.41), channel_id=1, source_target_pairs={{0,4},{4,0},{8,12},{12,8},{16,20},{20,16},{24,28},{28,24},{1,5},{5... | collective-permute-start | bytes 786440 | tf_op jit(solution)/shard_map/ppermute | solution.py:339
  6.7 8.1 %collective-permute-start.1 = (bf16[4,256,128]{2,1,0:T(8,128)(2,1)}, bf16[4,256,128]{2,1,0:T(8,128)(2,1)S(1)}, u32[]{:S(2)}, u32[]{:S(2)}) collective-permute-start(bf16[4,256,128]{2,1,0:T(8,128)(2,1)} %get-tuple-element.45), channel_id=1, source_target_pairs={{0,8},{4,12},{8,0},{12,4},{16,24},{20,28},{24,16},{28,20},{1,9},{5... | collective-permute-start | bytes 786440 | tf_op jit(solution)/shard_map/ppermute | solution.py:339
  6.7 37.2 %collective-permute-start.2 = (bf16[4,256,128]{2,1,0:T(8,128)(2,1)}, bf16[4,256,128]{2,1,0:T(8,128)(2,1)S(1)}, u32[]{:S(2)}, u32[]{:S(2)}) collective-permute-start(bf16[4,256,128]{2,1,0:T(8,128)(2,1)} %get-tuple-element.46), channel_id=1, source_target_pairs={{0,12},{4,8},{8,4},{12,0},{16,28},{20,24},{24,20},{28,16},{1,13},{... | collective-permute-start | bytes 786440 | tf_op jit(solution)/shard_map/ppermute | solution.py:339
  8.4 35.5 %collective-permute-start.3 = (bf16[4,256,128]{2,1,0:T(8,128)(2,1)}, bf16[4,256,128]{2,1,0:T(8,128)(2,1)S(1)}, u32[]{:S(2)}, u32[]{:S(2)}) collective-permute-start(bf16[4,256,128]{2,1,0:T(8,128)(2,1)} %get-tuple-element.47), channel_id=1, source_target_pairs={{0,16},{4,20},{8,24},{12,28},{16,0},{20,4},{24,8},{28,12},{1,17},{... | collective-permute-start | bytes 786440 | tf_op jit(solution)/shard_map/ppermute | solution.py:339
  9.4 34.5 %collective-permute-start.4 = (bf16[4,256,128]{2,1,0:T(8,128)(2,1)}, bf16[4,256,128]{2,1,0:T(8,128)(2,1)S(1)}, u32[]{:S(2)}, u32[]{:S(2)}) collective-permute-start(bf16[4,256,128]{2,1,0:T(8,128)(2,1)} %get-tuple-element.48), channel_id=1, source_target_pairs={{0,20},{4,16},{8,28},{12,24},{16,4},{20,0},{24,12},{28,8},{1,21},{... | collective-permute-start | bytes 786440 | tf_op jit(solution)/shard_map/ppermute | solution.py:339
  11.7 32.2 %collective-permute-start.5 = (bf16[4,256,128]{2,1,0:T(8,128)(2,1)}, bf16[4,256,128]{2,1,0:T(8,128)(2,1)S(1)}, u32[]{:S(2)}, u32[]{:S(2)}) collective-permute-start(bf16[4,256,128]{2,1,0:T(8,128)(2,1)} %get-tuple-element.49), channel_id=1, source_target_pairs={{0,24},{4,28},{8,16},{12,20},{16,8},{20,12},{24,0},{28,4},{1,25},{... | collective-permute-start | bytes 786440 | tf_op jit(solution)/shard_map/ppermute | solution.py:339
  14.7 29.2 %collective-permute-start.6 = (bf16[4,256,128]{2,1,0:T(8,128)(2,1)}, bf16[4,256,128]{2,1,0:T(8,128)(2,1)S(1)}, u32[]{:S(2)}, u32[]{:S(2)}) collective-permute-start(bf16[4,256,128]{2,1,0:T(8,128)(2,1)} %get-tuple-element.50), channel_id=1, source_target_pairs={{0,28},{4,24},{8,20},{12,16},{16,12},{20,8},{24,4},{28,0},{1,29},{... | collective-permute-start | bytes 786440 | tf_op jit(solution)/shard_map/ppermute | solution.py:339
  18.4 24.7 %all-to-all-start = ((bf16[256,1,128]{2,1,0:T(2,128)(2,1)}), bf16[256,1,128]{2,1,0:T(2,128)(2,1)S(1)}, u32[]{:S(2)}, u32[]{:S(2)}) async-start(bf16[256,1,128]{2,1,0:T(2,128)(2,1)} %copy.31), calls=%async_computation | async-start | bytes 262144 | tf_op jit(solution)/shard_map/all_to_all | solution.py:369
  43.9 1.0 copy-start
  46.2 19.6 %copy-start.1 = (bf16[8,2,256,128]{3,2,1,0:T(8,128)(2,1)}, bf16[8,2,256,128]{3,2,1,0:T(8,128)(2,1)S(1)}, u32[]{:S(2)}) copy-start(bf16[8,2,256,128]{3,2,1,0:T(8,128)(2,1)S(1)} %get-tuple-element.52.qd_ref) | copy-start | bytes 3145732
  65.8 13.1 %all-to-all-start.2 = ((bf16[8,144,128]{2,1,0:T(8,128)(2,1)}), bf16[8,144,128]{2,1,0:T(8,128)(2,1)S(1)}, u32[]{:S(2)}, u32[]{:S(2)}) async-start(bf16[8,144,128]{2,1,0:T(8,128)(2,1)} %get-tuple-element.54), calls=%async_computation.2 | async-start | bytes 589824 | tf_op jit(solution)/shard_map/all_to_all | solution.py:379
  69.4 1.2 copy-start.2
  82.7 0.7 copy-start.3
  83.4 0.7 copy-start.4
  84.1 9.3 %collective-permute-start.7 = (bf16[4,256,128]{2,1,0:T(8,128)(2,1)}, bf16[4,256,128]{2,1,0:T(8,128)(2,1)S(1)}, u32[]{:S(2)}, u32[]{:S(2)}) collective-permute-start(bf16[4,256,128]{2,1,0:T(8,128)(2,1)} %get-tuple-element.64), channel_id=1, source_target_pairs={{0,4},{4,0},{8,12},{12,8},{16,20},{20,16},{24,28},{28,24},{1,5},{5... | collective-permute-start | bytes 786440 | tf_op jit(solution)/shard_map/ppermute | solution.py:339
  88.0 8.1 %collective-permute-start.8 = (bf16[4,256,128]{2,1,0:T(8,128)(2,1)}, bf16[4,256,128]{2,1,0:T(8,128)(2,1)S(1)}, u32[]{:S(2)}, u32[]{:S(2)}) collective-permute-start(bf16[4,256,128]{2,1,0:T(8,128)(2,1)} %get-tuple-element.66), channel_id=1, source_target_pairs={{0,8},{4,12},{8,0},{12,4},{16,24},{20,28},{24,16},{28,20},{1,9},{5... | collective-permute-start | bytes 786440 | tf_op jit(solution)/shard_map/ppermute | solution.py:339
  88.4 18.1 %collective-permute-start.9 = (bf16[4,256,128]{2,1,0:T(8,128)(2,1)}, bf16[4,256,128]{2,1,0:T(8,128)(2,1)S(1)}, u32[]{:S(2)}, u32[]{:S(2)}) collective-permute-start(bf16[4,256,128]{2,1,0:T(8,128)(2,1)} %copy-done.4), channel_id=1, source_target_pairs={{0,12},{4,8},{8,4},{12,0},{16,28},{20,24},{24,20},{28,16},{1,13},{... | collective-permute-start | bytes 786440 | tf_op jit(solution)/shard_map/ppermute | solution.py:339
  90.1 19.6 %collective-permute-start.10 = (bf16[4,256,128]{2,1,0:T(8,128)(2,1)}, bf16[4,256,128]{2,1,0:T(8,128)(2,1)S(1)}, u32[]{:S(2)}, u32[]{:S(2)}) collective-permute-start(bf16[4,256,128]{2,1,0:T(8,128)(2,1)} %copy-done.3), channel_id=1, source_target_pairs={{0,16},{4,20},{8,24},{12,28},{16,0},{20,4},{24,8},{28,12},{1,17},{... | collective-permute-start | bytes 786440 | tf_op jit(solution)/shard_map/ppermute | solution.py:339
  92.2 24.7 %collective-permute-start.11 = (bf16[4,256,128]{2,1,0:T(8,128)(2,1)S(1)}, bf16[4,256,128]{2,1,0:T(8,128)(2,1)S(1)}, u32[]{:S(2)}, u32[]{:S(2)}) collective-permute-start(bf16[4,256,128]{2,1,0:T(8,128)(2,1)S(1)} %get-tuple-element.69), channel_id=1, source_target_pairs={{0,20},{4,16},{8,28},{12,24},{16,4},{20,0},{24,12},{28,8},{1,21},{... | collective-permute-start | bytes 786440 | tf_op jit(solution)/shard_map/ppermute | solution.py:339
  93.4 23.5 %collective-permute-start.12 = (bf16[4,256,128]{2,1,0:T(8,128)(2,1)S(1)}, bf16[4,256,128]{2,1,0:T(8,128)(2,1)S(1)}, u32[]{:S(2)}, u32[]{:S(2)}) collective-permute-start(bf16[4,256,128]{2,1,0:T(8,128)(2,1)S(1)} %get-tuple-element.70), channel_id=1, source_target_pairs={{0,24},{4,28},{8,16},{12,20},{16,8},{20,12},{24,0},{28,4},{1,25},{... | collective-permute-start | bytes 786440 | tf_op jit(solution)/shard_map/ppermute | solution.py:339
  96.2 25.0 %collective-permute-start.13 = (bf16[4,256,128]{2,1,0:T(8,128)(2,1)S(1)}, bf16[4,256,128]{2,1,0:T(8,128)(2,1)S(1)}, u32[]{:S(2)}, u32[]{:S(2)}) collective-permute-start(bf16[4,256,128]{2,1,0:T(8,128)(2,1)S(1)} %get-tuple-element.71), channel_id=1, source_target_pairs={{0,28},{4,24},{8,20},{12,16},{16,12},{20,8},{24,4},{28,0},{1,29},{... | collective-permute-start | bytes 786440 | tf_op jit(solution)/shard_map/ppermute | solution.py:339
  101.3 21.9 %all-to-all-start.3 = ((f32[256,1,128]{2,1,0:T(1,128)}), f32[256,1,128]{2,1,0:T(1,128)S(1)}, u32[]{:S(2)}, u32[]{:S(2)}) async-start(f32[256,1,128]{2,1,0:T(1,128)} %bitcast.10), calls=%async_computation.3 | async-start | bytes 262144 | tf_op jit(solution)/shard_map/all_to_all | solution.py:397
